TPU v7x, 32 devices: a whole 2x2x4 slice. The times are simulated.
32 devices in a mesh: dp: 8 (over y, x, core), fsdp: 4 (over z).
Axes of the slice: x: 2, y: 2, z: 4, core: 2. Of those that a mesh axis runs over, the one named last changes fastest.
Arguments:
- tokens: bfloat16 [4, 2048, 960], P('fsdp', 'dp'), may hold values from -6 to 6
- cotangent: bfloat16 [4, 2048, 960], P('fsdp', 'dp'), may hold values from -6 to 6
- route_depth: int32 [4, 2048], P('fsdp', 'dp'), may hold values from 1 to 3
- lengths: int32 [4, 3], P('fsdp'), may hold values from 1 to 1920, 2048 in all within a row
- qkv_weight: bfloat16 [960, 1600], P('fsdp'), may hold values from -0.1875 to 0.1875
- out_weight: bfloat16 [960, 960], P('fsdp'), may hold values from -2.5 to 2.5
- gate_up_weight: bfloat16 [960, 5120], P('fsdp'), may hold values from -0.1875 to 0.1875
- down_weight: bfloat16 [2560, 960], P('fsdp'), may hold values from -0.125 to 0.125
- attn_gain: bfloat16 [960], P('fsdp'), may hold values from 0.5 to 1.5
- ffn_gain: bfloat16 [960], P('fsdp'), may hold values from 0.5 to 1.5
- router_weight: bfloat16 [960, 3], P('fsdp'), may hold values from -0.1875 to 0.1875
Outputs:
- hidden_out: float32 [4, 2048, 960], P('fsdp', 'dp')
- input_grad: float32 [4, 2048, 960], P('fsdp', 'dp')
- qkv_grad: float32 [960, 1600], P('fsdp')
- out_grad: float32 [960, 960], P('fsdp')
- gate_up_grad: float32 [960, 5120], P('fsdp')
- down_grad: float32 [2560, 960], P('fsdp')
- attn_gain_grad: float32 [960], P('fsdp')
- ffn_gain_grad: float32 [960], P('fsdp')
- router_grad: float32 [960, 3], P('fsdp')
Inputs may be any that keep to these rules, and one draw needn't show every extreme that they name: The 3 lengths of a group sum to 2048 and the longest is exactly 1920.
All inputs are finite; a program needn't handle non-finite values.
Results may differ from a plain program's by a relative error of at most 0.023.
Values may be sent and summed in bfloat16 or wider, within the bound.
No kernel may reach another device: no remote copies, remote signals or barrier semaphores. Data moves between devices by JAX's collectives and lax.ppermute only.
A program may use at most 256 MiB of HBM per device.

v0:
```python
import math

import jax
import jax.numpy as jnp
from jax import lax
from jax.sharding import PartitionSpec as P

D = 960
HEADS = 15
KV_HEADS = 5
HEAD = 64
FF = 2560
STEPS = 3


EPSILON = 1e-05


def rms_scale(vectors):
    return lax.rsqrt(jnp.mean(vectors * vectors, axis=-1, keepdims=True) + EPSILON)


def rotate(vectors, cosine_table, sine_table):
    half_head = vectors.shape[-1] // 2
    first_half = vectors[..., :half_head]
    second = vectors[..., half_head:]
    return jnp.concatenate(
        [
            first_half * cosine_table - second * sine_table,
            second * cosine_table + first_half * sine_table,
        ],
        axis=-1,
    )


def rotate_back(vectors, cosine_table, sine_table):
    half_head = vectors.shape[-1] // 2
    first_half = vectors[..., :half_head]
    second = vectors[..., half_head:]
    return jnp.concatenate(
        [
            first_half * cosine_table + second * sine_table,
            second * cosine_table - first_half * sine_table,
        ],
        axis=-1,
    )


def norm_back(source, scale_rows, gain_row, grad_out):
    scaled = gain_row * grad_out
    grad_in = scale_rows * scaled - source * scale_rows**3 * jnp.mean(
        scaled * source, axis=-1, keepdims=True
    )
    grad_gain = jnp.sum(grad_out * source * scale_rows, axis=0)
    return (grad_in, grad_gain)


def per_device(
    tokens,
    cotangent,
    route_depth,
    lengths,
    qkv_weight,
    out_weight,
    gate_up_weight,
    down_weight,
    attn_gain,
    ffn_gain,
    router_weight,
):
    rows_dev = tokens.shape[1]
    data_ranks = lax.axis_size("dp")
    rank_here = lax.axis_index("dp")
    group_rows = rows_dev * data_ranks
    kv_width = KV_HEADS * HEAD
    per_kv = HEADS // KV_HEADS
    half_head = HEAD // 2
    block_rows = min(512, group_rows)
    block_count = group_rows // block_rows
    scale_const = HEAD ** (-0.5)
    depth_here = route_depth[0]
    depth_all = lax.all_gather(depth_here, "dp", axis=0, tiled=True)
    lengths_here = lengths[0]
    token_index = jnp.arange(group_rows, dtype=jnp.int32)
    seq_ends = jnp.cumsum(lengths_here)
    passed = (token_index[:, None] >= seq_ends[None, :]).astype(jnp.int32)
    seq_all = jnp.sum(passed, axis=1)
    seq_start = jnp.sum(passed * lengths_here[None, :], axis=1)
    first_row = rank_here * rows_dev
    query_index = first_row + jnp.arange(rows_dev, dtype=jnp.int32)
    query_seq = lax.dynamic_slice_in_dim(seq_all, first_row, rows_dev)
    position = query_index - lax.dynamic_slice_in_dim(seq_start, first_row, rows_dev)
    frequency = jnp.exp(
        jnp.arange(half_head, dtype=jnp.float32) * (-2.0 * math.log(10000.0) / HEAD)
    )
    angles = position.astype(jnp.float32)[:, None] * frequency[None, :]
    cosine_table = jnp.cos(angles)[:, None, :]
    sine_table = jnp.sin(angles)[:, None, :]
    first_keys = block_rows * jnp.arange(block_count, dtype=jnp.int32)

    def allowed_for(first_key, recursion):
        key_index = first_key + jnp.arange(block_rows, dtype=jnp.int32)
        key_seq = lax.dynamic_slice_in_dim(seq_all, first_key, block_rows)
        key_live = lax.dynamic_slice_in_dim(depth_all, first_key, block_rows) > recursion
        same_seq = query_seq[:, None] == key_seq[None, :]
        causal = key_index[None, :] <= query_index[:, None]
        itself = key_index[None, :] == query_index[:, None]
        return same_seq & causal & (key_live[None, :] | itself)

    def project(hidden, weights):
        scale_one = rms_scale(hidden)
        normed = (hidden * scale_one * weights[4].astype(jnp.float32)).astype(jnp.bfloat16)
        projected = jnp.dot(normed, weights[0], preferred_element_type=jnp.float32)
        queries = rotate(
            projected[:, :D].reshape(rows_dev, HEADS, HEAD), cosine_table, sine_table
        ).astype(jnp.bfloat16)
        keys_rot = rotate(
            projected[:, D : D + kv_width].reshape(rows_dev, KV_HEADS, HEAD),
            cosine_table,
            sine_table,
        ).astype(jnp.bfloat16)
        values = projected[:, D + kv_width :].astype(jnp.bfloat16)
        kv_local = jnp.concatenate([keys_rot.reshape(rows_dev, kv_width), values], axis=1)
        return (scale_one, normed, queries.reshape(rows_dev, KV_HEADS, per_kv, HEAD), kv_local)

    def block_scores(grouped, key_block):
        keys_part = key_block[:, :kv_width].reshape(block_rows, KV_HEADS, HEAD)
        return (
            jnp.einsum("qkgh,nkh->kgqn", grouped, keys_part, preferred_element_type=jnp.float32)
            * scale_const
        )

    def finish(hidden, mixed_f, weights, recursion):
        attn_rounded = mixed_f.astype(jnp.bfloat16)
        attended = jnp.dot(attn_rounded, weights[1], preferred_element_type=jnp.float32)
        middle = hidden + attended
        scale_two = rms_scale(middle)
        normed_ffn = (middle * scale_two * weights[5].astype(jnp.float32)).astype(jnp.bfloat16)
        gate_up = jnp.dot(normed_ffn, weights[2], preferred_element_type=jnp.float32)
        inner = (jax.nn.silu(gate_up[:, :FF]) * gate_up[:, FF:]).astype(jnp.bfloat16)
        ffn_out = jnp.dot(inner, weights[3], preferred_element_type=jnp.float32)
        update = attended + ffn_out
        router_col = weights[6][:, recursion].astype(jnp.float32)
        router_gate = jax.nn.sigmoid(jnp.dot(hidden, router_col, precision=lax.Precision.HIGHEST))
        live_rows = (depth_here > recursion).astype(jnp.float32)
        new_hidden = hidden + (live_rows * router_gate)[:, None] * update
        return (
            new_hidden,
            attn_rounded,
            middle,
            scale_two,
            normed_ffn,
            gate_up,
            inner,
            update,
            router_gate,
            live_rows,
            router_col,
        )

    weights = (
        lax.all_gather(qkv_weight, "fsdp", axis=0, tiled=True),
        lax.all_gather(out_weight, "fsdp", axis=0, tiled=True),
        lax.all_gather(gate_up_weight, "fsdp", axis=0, tiled=True),
        lax.all_gather(down_weight, "fsdp", axis=0, tiled=True),
        lax.all_gather(attn_gain, "fsdp", axis=0, tiled=True),
        lax.all_gather(ffn_gain, "fsdp", axis=0, tiled=True),
        lax.all_gather(router_weight, "fsdp", axis=0, tiled=True),
    )
    hidden = tokens[0].astype(jnp.float32)
    kept_steps = []
    for recursion in range(STEPS):
        scale_one, normed, grouped, kv_local = project(hidden, weights)
        keys_all = lax.all_gather(kv_local, "dp", axis=0, tiled=True)
        attend_key_blocks = keys_all.reshape(block_count, block_rows, 2 * kv_width)

        def max_sum(carry, member):
            highest, totals = carry
            key_block, first_key = member
            allowed = allowed_for(first_key, recursion)
            scores = jnp.where(allowed, block_scores(grouped, key_block), -1e30)
            new_high = jnp.maximum(highest, jnp.max(scores, axis=-1))
            exponent = jnp.where(allowed, jnp.exp(scores - new_high[..., None]), 0.0)
            totals = totals * jnp.exp(highest - new_high) + jnp.sum(exponent, axis=-1)
            return ((new_high, totals), None)

        start_state = (
            jnp.full((KV_HEADS, per_kv, rows_dev), -1e30, jnp.float32),
            jnp.zeros((KV_HEADS, per_kv, rows_dev), jnp.float32),
        )
        (highest, totals), unused = lax.scan(max_sum, start_state, (attend_key_blocks, first_keys))
        attend_log_total = highest + jnp.log(totals)

        def weighted(carry, member):
            key_block, first_key = member
            allowed = allowed_for(first_key, recursion)
            scores = block_scores(grouped, key_block)
            chances = jnp.where(allowed, jnp.exp(scores - attend_log_total[..., None]), 0.0).astype(
                jnp.bfloat16
            )
            values_part = key_block[:, kv_width:].reshape(block_rows, KV_HEADS, HEAD)
            return (
                carry
                + jnp.einsum(
                    "kgqn,nkh->qkgh", chances, values_part, preferred_element_type=jnp.float32
                ),
                None,
            )

        mixed, unused = lax.scan(
            weighted,
            jnp.zeros((rows_dev, KV_HEADS, per_kv, HEAD), jnp.float32),
            (attend_key_blocks, first_keys),
        )
        mixed_f = mixed.reshape(rows_dev, D)
        log_total = attend_log_total
        outputs_now = finish(hidden, mixed_f, weights, recursion)
        kept_steps.append((hidden, mixed_f, log_total, keys_all))
        hidden = outputs_now[0]
    hidden_out = hidden
    back_weights = (
        lax.all_gather(qkv_weight, "fsdp", axis=0, tiled=True),
        lax.all_gather(out_weight, "fsdp", axis=0, tiled=True),
        lax.all_gather(gate_up_weight, "fsdp", axis=0, tiled=True),
        lax.all_gather(down_weight, "fsdp", axis=0, tiled=True),
        lax.all_gather(attn_gain, "fsdp", axis=0, tiled=True),
        lax.all_gather(ffn_gain, "fsdp", axis=0, tiled=True),
        lax.all_gather(router_weight, "fsdp", axis=0, tiled=True),
    )
    gain_first_f = back_weights[4].astype(jnp.float32)
    gain_second_f = back_weights[5].astype(jnp.float32)
    qkv_total = jnp.zeros(back_weights[0].shape, jnp.float32)
    out_total = jnp.zeros(back_weights[1].shape, jnp.float32)
    gate_total = jnp.zeros(back_weights[2].shape, jnp.float32)
    down_total = jnp.zeros(back_weights[3].shape, jnp.float32)
    first_gain = jnp.zeros((D,), jnp.float32)
    second_gain = jnp.zeros((D,), jnp.float32)
    router_cols = [None] * STEPS
    grad_hidden = cotangent[0].astype(jnp.float32)
    for recursion in reversed(range(STEPS)):
        hidden, mixed_f, log_total, kept_keys = kept_steps[recursion]
        scale_one, normed, grouped, kv_local = project(hidden, back_weights)
        keys_all = lax.all_gather(kv_local, "dp", axis=0, tiled=True)
        (
            unused_hidden,
            attn_rounded,
            middle,
            scale_two,
            normed_ffn,
            gate_up,
            inner,
            update,
            router_gate,
            live_rows,
            router_col,
        ) = finish(hidden, mixed_f, back_weights, recursion)
        grad_update = (live_rows * router_gate)[:, None] * grad_hidden
        grad_logit = (
            live_rows * router_gate * (1.0 - router_gate) * jnp.sum(grad_hidden * update, axis=-1)
        )
        router_cols[recursion] = jnp.dot(grad_logit, hidden, precision=lax.Precision.HIGHEST)
        grad_ffn = grad_update.astype(jnp.bfloat16)
        down_total = down_total + jnp.einsum(
            "tf,td->fd", inner, grad_ffn, preferred_element_type=jnp.float32
        )
        grad_inner = jnp.einsum(
            "td,fd->tf", grad_ffn, back_weights[3], preferred_element_type=jnp.float32
        )
        gate_part = gate_up[:, :FF]
        up_part = gate_up[:, FF:]
        sigmoid_gate = jax.nn.sigmoid(gate_part)
        grad_gate = jnp.concatenate(
            [
                grad_inner * up_part * sigmoid_gate * (1.0 + gate_part * (1.0 - sigmoid_gate)),
                grad_inner * jax.nn.silu(gate_part),
            ],
            axis=1,
        ).astype(jnp.bfloat16)
        gate_total = gate_total + jnp.einsum(
            "td,tf->df", normed_ffn, grad_gate, preferred_element_type=jnp.float32
        )
        grad_normed_ffn = jnp.einsum(
            "tf,df->td", grad_gate, back_weights[2], preferred_element_type=jnp.float32
        )
        grad_middle, gain_part = norm_back(middle, scale_two, gain_second_f, grad_normed_ffn)
        second_gain = second_gain + gain_part
        grad_attended = (grad_update + grad_middle).astype(jnp.bfloat16)
        out_total = out_total + jnp.einsum(
            "ti,td->id", attn_rounded, grad_attended, preferred_element_type=jnp.float32
        )
        grad_mixed = jnp.einsum(
            "td,id->ti", grad_attended, back_weights[1], preferred_element_type=jnp.float32
        ).astype(jnp.bfloat16)
        grad_mixed = grad_mixed.reshape(rows_dev, KV_HEADS, per_kv, HEAD)
        key_blocks = keys_all.reshape(block_count, block_rows, 2 * kv_width)
        row_delta = jnp.sum(
            grad_mixed.astype(jnp.float32) * mixed_f.reshape(rows_dev, KV_HEADS, per_kv, HEAD),
            axis=-1,
        )
        row_delta = jnp.transpose(row_delta, (1, 2, 0))

        def key_step(carry, member):
            key_block, first_key = member
            allowed = allowed_for(first_key, recursion)
            keys_part = key_block[:, :kv_width].reshape(block_rows, KV_HEADS, HEAD)
            values_part = key_block[:, kv_width:].reshape(block_rows, KV_HEADS, HEAD)
            scores = (
                jnp.einsum("qkgh,nkh->kgqn", grouped, keys_part, preferred_element_type=jnp.float32)
                * scale_const
            )
            chances = jnp.where(allowed, jnp.exp(scores - log_total[..., None]), 0.0)
            grad_chances = jnp.einsum(
                "qkgh,nkh->kgqn", grad_mixed, values_part, preferred_element_type=jnp.float32
            )
            grad_scores = (chances * (grad_chances - row_delta[..., None])).astype(jnp.bfloat16)
            carry = (
                carry
                + jnp.einsum(
                    "kgqn,nkh->qkgh", grad_scores, keys_part, preferred_element_type=jnp.float32
                )
                * scale_const
            )
            grad_keys = (
                jnp.einsum(
                    "kgqn,qkgh->nkh", grad_scores, grouped, preferred_element_type=jnp.float32
                )
                * scale_const
            )
            grad_values = jnp.einsum(
                "kgqn,qkgh->nkh",
                chances.astype(jnp.bfloat16),
                grad_mixed,
                preferred_element_type=jnp.float32,
            )
            return (
                carry,
                jnp.concatenate(
                    [
                        grad_keys.reshape(block_rows, kv_width),
                        grad_values.reshape(block_rows, kv_width),
                    ],
                    axis=1,
                ),
            )

        grad_query, grad_blocks = lax.scan(
            key_step,
            jnp.zeros((rows_dev, KV_HEADS, per_kv, HEAD), jnp.float32),
            (key_blocks, first_keys),
        )
        grad_query, grad_kv_all = (grad_query, grad_blocks.reshape(group_rows, 2 * kv_width))
        grad_kv = lax.psum_scatter(
            grad_kv_all.astype(jnp.bfloat16), "dp", scatter_dimension=0, tiled=True
        ).astype(jnp.float32)
        query_back = rotate_back(
            grad_query.reshape(rows_dev, HEADS, HEAD), cosine_table, sine_table
        ).reshape(rows_dev, D)
        key_back = rotate_back(
            grad_kv[:, :kv_width].reshape(rows_dev, KV_HEADS, HEAD), cosine_table, sine_table
        ).reshape(rows_dev, kv_width)
        grad_projected = jnp.concatenate(
            [query_back, key_back, grad_kv[:, kv_width:]], axis=1
        ).astype(jnp.bfloat16)
        qkv_total = qkv_total + jnp.einsum(
            "td,tp->dp", normed, grad_projected, preferred_element_type=jnp.float32
        )
        grad_normed = jnp.einsum(
            "tp,dp->td", grad_projected, back_weights[0], preferred_element_type=jnp.float32
        )
        grad_first, gain_first = norm_back(hidden, scale_one, gain_first_f, grad_normed)
        first_gain = first_gain + gain_first
        grad_hidden = (
            grad_hidden + grad_middle + grad_first + grad_logit[:, None] * router_col[None, :]
        )
    router_total = jnp.stack(router_cols, axis=1)
    shards = (
        lax.psum_scatter(
            qkv_total.astype(jnp.bfloat16), "fsdp", scatter_dimension=0, tiled=True
        ).astype(jnp.float32),
        lax.psum_scatter(
            out_total.astype(jnp.bfloat16), "fsdp", scatter_dimension=0, tiled=True
        ).astype(jnp.float32),
        lax.psum_scatter(
            gate_total.astype(jnp.bfloat16), "fsdp", scatter_dimension=0, tiled=True
        ).astype(jnp.float32),
        lax.psum_scatter(
            down_total.astype(jnp.bfloat16), "fsdp", scatter_dimension=0, tiled=True
        ).astype(jnp.float32),
        lax.psum_scatter(
            first_gain.astype(jnp.bfloat16), "fsdp", scatter_dimension=0, tiled=True
        ).astype(jnp.float32),
        lax.psum_scatter(
            second_gain.astype(jnp.bfloat16), "fsdp", scatter_dimension=0, tiled=True
        ).astype(jnp.float32),
        lax.psum_scatter(
            router_total.astype(jnp.bfloat16), "fsdp", scatter_dimension=0, tiled=True
        ).astype(jnp.float32),
    )
    summed = (
        lax.psum(shards[0].astype(jnp.bfloat16), "dp").astype(jnp.float32),
        lax.psum(shards[1].astype(jnp.bfloat16), "dp").astype(jnp.float32),
        lax.psum(shards[2].astype(jnp.bfloat16), "dp").astype(jnp.float32),
        lax.psum(shards[3].astype(jnp.bfloat16), "dp").astype(jnp.float32),
        lax.psum(shards[4].astype(jnp.bfloat16), "dp").astype(jnp.float32),
        lax.psum(shards[5].astype(jnp.bfloat16), "dp").astype(jnp.float32),
        lax.psum(shards[6].astype(jnp.bfloat16), "dp").astype(jnp.float32),
    )
    return (
        hidden_out[None],
        grad_hidden[None],
        summed[0],
        summed[1],
        summed[2],
        summed[3],
        summed[4],
        summed[5],
        summed[6],
    )


def solution(mesh):
    placed = (
        P("fsdp", "dp", None),
        P("fsdp", "dp", None),
        P("fsdp", "dp"),
        P("fsdp", None),
        P("fsdp", None),
        P("fsdp", None),
        P("fsdp", None),
        P("fsdp", None),
        P("fsdp"),
        P("fsdp"),
        P("fsdp", None),
    )
    return jax.shard_map(
        per_device,
        mesh=mesh,
        in_specs=placed,
        out_specs=(
            P("fsdp", "dp", None),
            P("fsdp", "dp", None),
            P("fsdp", None),
            P("fsdp", None),
            P("fsdp", None),
            P("fsdp", None),
            P("fsdp"),
            P("fsdp"),
            P("fsdp", None),
        ),
        check_vma=False,
    )
```

profile of v0, /device:TPU:0, one launch (start us, length us, event | category | flops | bytes accessed | tf_op | source)
XLA Modules:
  0.0 1655.0 jit_solution(13140073022576174713)
XLA Ops:
  12.5 13.6 all-reduce.7
  29.0 47.7 %all-gather.10.cloned.1.call-done = bf16[960,1600]{1,0:T(8,128)(2,1)} async-done(((bf16[240,1600]{1,0:T(8,128)(2,1)}), bf16[960,1600]{1,0:T(8,128)(2,1)}) %all-gather.10.cloned.1.call-update) | async-done | bytes 3072016 | tf_op jit(solution)/shard_map/all_gather | solution.py:162
  84.4 8.9 all-gather
  93.9 11.9 all-gather.1
  115.2 58.8 %while.111 = (s32[]{:T(128)}, f32[5,3,256]{2,1,0:T(4,128)S(1)}, f32[5,3,256]{2,1,0:T(4,128)S(1)}, s32[256]{0:T(256)S(1)}, s32[4]{0:T(128)S(1)}, /*index=5*/s32[2...) while((s32[]{:T(128)}, f32[5,3,256]{2,1,0:T(4,128)S(1)}, ...), condition=%wide.region_7.8_spmd.clone, body=%wide.region_4.7_spmd.clone.sunk | while | flops 268193792 | bytes 19123400 | solution.py:191
  174.1 28.9 %while.112 = (s32[]{:T(128)}, f32[256,5,3,64]{0,3,2,1:T(8,128)S(1)}, bf16[4,512,640]{1,2,0:T(8,128)(2,1)}, s32[256]{0:T(256)S(1)}, s32[4]{0:T(128)S(1)}, /*index...) while((s32[]{:T(128)}, f32[256,5,3,64]{0,3,2,1:T(8,128)S(1)}, ...), condition=%wide.region_9.10_spmd.clone, body=%wide.region_8.9_spmd.clone.sunk | while | flops 512460032 | bytes 6028489 | solution.py:210
  207.7 122.7 %all-gather.16.cloned.1.call-done = bf16[960,5120]{1,0:T(8,128)(2,1)} async-done(((bf16[240,5120]{1,0:T(8,128)(2,1)}), bf16[960,5120]{1,0:T(8,128)(2,1)}) %all-gather.16.cloned.1.call-update) | async-done | bytes 9830416 | tf_op jit(solution)/shard_map/all_gather | solution.py:164
  339.3 83.4 %all-gather.18.cloned.1.call-done = bf16[2560,960]{0,1:T(8,128)(2,1)} async-done(((bf16[640,960]{0,1:T(8,128)(2,1)}), bf16[2560,960]{0,1:T(8,128)(2,1)}) %all-gather.18.cloned.1.call-update) | async-done | bytes 4915216 | tf_op jit(solution)/shard_map/all_gather | solution.py:165
  432.9 27.9 %all-gather.20.cloned.1.call-done = bf16[2048,640]{0,1:T(8,128)(2,1)} async-done(((bf16[256,640]{0,1:T(8,128)(2,1)}), bf16[2048,640]{0,1:T(8,128)(2,1)}) %all-gather.20.cloned.1.call-update) | async-done | bytes 2621456 | tf_op jit(solution)/shard_map/all_gather | solution.py:174
  464.2 57.3 %while.113 = (s32[]{:T(128)}, f32[5,3,256]{2,1,0:T(4,128)S(1)}, f32[5,3,256]{2,1,0:T(4,128)S(1)}, s32[256]{0:T(256)S(1)}, s32[4]{0:T(128)S(1)}, /*index=5*/s32[2...) while((s32[]{:T(128)}, f32[5,3,256]{2,1,0:T(4,128)S(1)}, ...), condition=%wide.region_15.16_spmd.clone, body=%wide.region_12.15_spmd.clone.sunk | while | flops 268193792 | bytes 19123400 | solution.py:191
  522.2 43.4 %while.114 = (s32[]{:T(128)}, f32[256,5,3,64]{0,3,2,1:T(8,128)}, bf16[4,512,640]{1,2,0:T(8,128)(2,1)}, s32[256]{0:T(256)S(1)}, s32[4]{0:T(128)S(1)}, /*index=5*/...) while((s32[]{:T(128)}, f32[256,5,3,64]{0,3,2,1:T(8,128)}, ...), condition=%wide.region_17.18_spmd.clone, body=%wide.region_16.17_spmd.clone.sunk | while | flops 512460032 | bytes 6028489 | solution.py:210
  584.2 29.7 %all-gather.22.cloned.1.call-done = bf16[2048,640]{0,1:T(8,128)(2,1)} async-done(((bf16[256,640]{0,1:T(8,128)(2,1)}), bf16[2048,640]{0,1:T(8,128)(2,1)}) %all-gather.22.cloned.1.call-update) | async-done | bytes 2621456 | tf_op jit(solution)/shard_map/all_gather | solution.py:174
  617.4 57.2 %while.115 = (s32[]{:T(128)}, f32[5,3,256]{2,1,0:T(4,128)S(1)}, f32[5,3,256]{2,1,0:T(4,128)S(1)}, s32[256]{0:T(256)S(1)}, s32[4]{0:T(128)S(1)}, /*index=5*/s32[2...) while((s32[]{:T(128)}, f32[5,3,256]{2,1,0:T(4,128)S(1)}, ...), condition=%wide.region_23.24_spmd.clone, body=%wide.region_20.23_spmd.clone.sunk | while | flops 268193792 | bytes 19123400 | solution.py:191
  674.6 35.7 %while.116 = (s32[]{:T(128)}, f32[256,5,3,64]{0,3,2,1:T(8,128)}, bf16[4,512,640]{1,2,0:T(8,128)(2,1)}, s32[256]{0:T(256)S(1)}, s32[4]{0:T(128)S(1)}, /*index=5*/...) while((s32[]{:T(128)}, f32[256,5,3,64]{0,3,2,1:T(8,128)}, ...), condition=%wide.region_25.26_spmd.clone, body=%wide.region_24.25_spmd.clone.sunk | while | flops 512460032 | bytes 6028489 | solution.py:210
  732.9 80.4 %while.117 = (s32[]{:T(128)}, f32[256,5,3,64]{0,3,2,1:T(8,128)}, bf16[4,512,640]{2,1,0:T(8,128)(2,1)}, bf16[4,512,640]{1,2,0:T(8,128)(2,1)}, s32[256]{0:T(256)S(...) while((s32[]{:T(128)}, f32[256,5,3,64]{0,3,2,1:T(8,128)}, ...), condition=%wide.region_30.31_spmd.clone, body=%wide.region_29.30_spmd.clone.sunk | while | flops 1281115392 | bytes 67630896 | solution.py:346
  819.5 42.1 %reduce-scatter.13.cloned.1.call-done = bf16[256,640]{0,1:T(8,128)(2,1)} async-done(((bf16[2048,640]{0,1:T(8,128)(2,1)}), bf16[256,640]{0,1:T(8,128)(2,1)}) %reduce-scatter.13.cloned.1.call-update) | async-done | bytes 327696 | tf_op jit(solution)/shard_map/reduce_scatter | solution.py:352
  883.1 71.4 %while.118 = (s32[]{:T(128)}, f32[256,5,3,64]{0,3,2,1:T(8,128)S(1)}, bf16[4,512,640]{2,1,0:T(8,128)(2,1)}, bf16[4,512,640]{1,2,0:T(8,128)(2,1)}, s32[256]{0:T(25...) while((s32[]{:T(128)}, f32[256,5,3,64]{0,3,2,1:T(8,128)S(1)}, ...), condition=%wide.region_37.38_spmd.clone, body=%wide.region_36.37_spmd.clone.sunk | while | flops 1281115392 | bytes 65664792 | solution.py:346
  961.5 41.7 %reduce-scatter.15.cloned.1.call-done = bf16[256,640]{0,1:T(8,128)(2,1)} async-done(((bf16[2048,640]{0,1:T(8,128)(2,1)}), bf16[256,640]{0,1:T(8,128)(2,1)}) %reduce-scatter.15.cloned.1.call-update) | async-done | bytes 327696 | tf_op jit(solution)/shard_map/reduce_scatter | solution.py:352
  1024.7 76.1 %while.119 = (s32[]{:T(128)}, f32[256,5,3,64]{0,3,2,1:T(8,128)}, bf16[4,512,640]{2,1,0:T(8,128)(2,1)}, bf16[4,512,640]{1,2,0:T(8,128)(2,1)}, s32[256]{0:T(256)S(...) while((s32[]{:T(128)}, f32[256,5,3,64]{0,3,2,1:T(8,128)}, ...), condition=%wide.region_44.45_spmd.clone, body=%wide.region_43.44_spmd.clone.sunk | while | flops 1281115392 | bytes 65664792 | solution.py:346
  1113.7 8.4 add_convert_fusion.1
  1122.1 7.8 copy.229
  1159.3 11.3 fusion.117
  1170.6 8.3 fusion.115
  1178.9 17.8 %add_convert_fusion = bf16[960,5120]{1,0:T(8,128)(2,1)} fusion(f32[960,5120]{1,0:T(8,128)} %fusion.117, f32[960,5120]{1,0:T(8,128)} %fusion.115, bf16[256,2560]{1,0:T(8,128)(2,1)S(1)} %copy-done.91, bf16[256,2560]{1,0:T(8,128)(2,1)S(1)} %copy-done.89, f32[256,960]{0,1:T(8,128)S(1)} %copy-done.18, f32[960]{0:T(1024)S(1)} %convert_element_type.305, ...), kind=kOutput, calls=%fused_computation.159 | convolution fusion | flops 2537308160 | bytes 52761344 | tf_op jit(solution)/shard_map/td,tf->df/dot_general | solution.py:279
  1201.9 43.3 %reduce-scatter.25.cloned.1.call-done = bf16[640,960]{1,0:T(8,128)(2,1)} async-done(((bf16[2560,960]{1,0:T(8,128)(2,1)}), bf16[640,960]{1,0:T(8,128)(2,1)}) %reduce-scatter.25.cloned.1.call-update) | async-done | bytes 1228816
  1247.6 42.3 %reduce-scatter.21.cloned.1.call-done = bf16[240,960]{1,0:T(8,128)(2,1)} async-done(((bf16[960,960]{1,0:T(8,128)(2,1)}), bf16[240,960]{1,0:T(8,128)(2,1)}) %reduce-scatter.21.cloned.1.call-update) | async-done | bytes 460816 | tf_op jit(solution)/shard_map/reduce_scatter | solution.py:380
  1289.9 63.3 %reduce-scatter.19.cloned.1.call-done = bf16[240,1600]{1,0:T(8,128)(2,1)} async-done(((bf16[960,1600]{1,0:T(8,128)(2,1)}), bf16[240,1600]{1,0:T(8,128)(2,1)}) %reduce-scatter.19.cloned.1.call-update) | async-done | bytes 768016 | tf_op jit(solution)/shard_map/reduce_scatter | solution.py:377
  1353.2 170.0 %reduce-scatter.23.cloned.1.call-done = bf16[240,5120]{1,0:T(8,128)(2,1)} async-done(((bf16[960,5120]{1,0:T(8,128)(2,1)}), bf16[240,5120]{1,0:T(8,128)(2,1)}) %reduce-scatter.23.cloned.1.call-update) | async-done | bytes 2457616 | tf_op jit(solution)/shard_map/reduce_scatter | solution.py:383
  1523.9 22.0 %reduce-scatter.27.cloned.1.call-done = bf16[240,3]{1,0:T(8,128)(2,1)} async-done(((bf16[960,3]{1,0:T(8,128)(2,1)}), bf16[240,3]{1,0:T(8,128)(2,1)}) %reduce-scatter.27.cloned.1.call-update) | async-done | bytes 1456
  1550.9 8.8 all-reduce.6
  1559.9 12.8 all-reduce.4
  1577.5 61.9 %all-reduce.10.cloned.1.call-done = (bf16[240,1600]{1,0:T(8,128)(2,1)}, bf16[240,960]{1,0:T(8,128)(2,1)}, bf16[240,5120]{1,0:T(8,128)(2,1)}, bf16[640,960]{0,1:T(8,128)(2,1)}) async-done(((bf16[240,1600]{1,0:T(8,128)(2,1)}, bf16[240,960]{1,0:T(8,128)(2,1)}, bf16[240,5120]{1,0:T(8,128)(2,1)}, bf16[640,960]{0,1:T(8,128)(2,1)}), (bf16[240,1600]{1,0:T(8,128)(2,1)}, bf16[240,960]{1,0:T(8,128)(2,1)}, ...) | async-done | bytes 4915216 | tf_op jit(solution)/shard_map/psum | solution.py:400
  (1090 shorter events, 656.4 us)
Async XLA Ops:
  7.2 69.5 %all-gather.10.cloned.1.call-start = ((), (), s32[]{:S(2)}) async-start(), calls=%async_computation.8 | async-start | bytes 3993600 | tf_op jit(solution)/shard_map/all_gather | solution.py:162
  7.9 103.8 %all-gather.12.cloned.1.call-start = ((), (), s32[]{:S(2)}) async-start(), calls=%async_computation.9 | async-start | bytes 2949120 | tf_op jit(solution)/shard_map/all_gather | solution.py:174
  26.1 554.0 %copy-start.93 = (f32[960]{0:T(1024)}, f32[960]{0:T(1024)S(1)}, u32[]{:S(2)}) copy-start(f32[960]{0:T(1024)S(1)} %convert_element_type.298) | copy-start | bytes 11524
  28.9 554.6 %copy-start.45 = (f32[256,32]{0,1:T(8,128)}, f32[256,32]{0,1:T(8,128)S(1)}, u32[]{:S(2)}) copy-start(f32[256,32]{0,1:T(8,128)S(1)} %get-tuple-element.1789) | copy-start | bytes 98308
  29.0 554.6 %copy-start.47 = (f32[256,32]{0,1:T(8,128)}, f32[256,32]{0,1:T(8,128)S(1)}, u32[]{:S(2)}) copy-start(f32[256,32]{0,1:T(8,128)S(1)} %get-tuple-element.1790) | copy-start | bytes 98308
  82.4 120.7 %all-gather.14.cloned.1.call-start = ((), (), s32[]{:S(2)}) async-start(), calls=%async_computation.10 | async-start | bytes 2457600 | tf_op jit(solution)/shard_map/all_gather | solution.py:163
  83.2 247.2 %all-gather.16.cloned.1.call-start = ((), (), s32[]{:S(2)}) async-start(), calls=%async_computation.11 | async-start | bytes 12288000 | tf_op jit(solution)/shard_map/all_gather | solution.py:164
  83.7 339.0 %all-gather.18.cloned.1.call-start = ((), (), s32[]{:S(2)}) async-start(), calls=%async_computation.12 | async-start | bytes 6144000 | tf_op jit(solution)/shard_map/all_gather | solution.py:165
  84.3 376.5 %all-gather.20.cloned.1.call-start = ((), (), s32[]{:S(2)}) async-start(), calls=%async_computation.13 | async-start | bytes 2949120 | tf_op jit(solution)/shard_map/all_gather | solution.py:174
  93.8 339.1 %copy-start.155 = (pred[256]{0:T(512)(128)(4,1)}, pred[256]{0:T(512)(128)(4,1)S(1)}, u32[]{:S(2)}) copy-start(pred[256]{0:T(512)(128)(4,1)S(1)} %get-tuple-element.1504) | copy-start | bytes 772
  105.9 477.9 %copy-start.114 = (bf16[960,3]{0,1:T(4,128)(2,1)}, bf16[960,3]{0,1:T(4,128)(2,1)S(1)}, u32[]{:S(2)}) copy-start(bf16[960,3]{0,1:T(4,128)(2,1)S(1)} %reshape.560) | copy-start | bytes 17284
  106.1 316.6 %copy-start.150 = (f32[256]{0:T(256)}, f32[256]{0:T(256)S(1)}, u32[]{:S(2)}) copy-start(f32[256]{0:T(256)S(1)} %broadcast_select_fusion.2) | copy-start | bytes 3076
  431.7 182.2 %all-gather.22.cloned.1.call-start = ((), (), s32[]{:S(2)}) async-start(), calls=%async_computation.14 | async-start | bytes 2949120 | tf_op jit(solution)/shard_map/all_gather | solution.py:174
  579.5 287.3 %copy-start.9 = (f32[256,960]{0,1:T(8,128)}, f32[256,960]{0,1:T(8,128)S(1)}, u32[]{:S(2)}) copy-start(f32[256,960]{0,1:T(8,128)S(1)} %get-tuple-element.1724) | copy-start | bytes 2949124
  583.2 278.4 %reduce-scatter.13.cloned.1.call-start = ((), (), s32[]{:S(2)}) async-start(), calls=%async_computation.15 | async-start | bytes 2949120 | tf_op jit(solution)/shard_map/reduce_scatter | solution.py:352
  714.4 152.4 %copy-start.118 = (f32[256]{0:T(256)}, f32[256]{0:T(256)S(1)}, u32[]{:S(2)}) copy-start(f32[256]{0:T(256)S(1)} %get-tuple-element.1802) | copy-start | bytes 3076
  714.4 152.4 %copy-start.127 = (f32[256]{0:T(256)}, f32[256]{0:T(256)S(1)}, u32[]{:S(2)}) copy-start(f32[256]{0:T(256)S(1)} %get-tuple-element.1817) | copy-start | bytes 3076
  817.8 185.3 %reduce-scatter.15.cloned.1.call-start = ((), (), s32[]{:S(2)}) async-start(), calls=%async_computation.16 | async-start | bytes 2949120 | tf_op jit(solution)/shard_map/reduce_scatter | solution.py:352
  959.3 189.8 %reduce-scatter.17.cloned.1.call-start = ((), (), s32[]{:S(2)}) async-start(), calls=%async_computation.17 | async-start | bytes 2949120 | tf_op jit(solution)/shard_map/reduce_scatter | solution.py:352
  1105.3 139.9 %reduce-scatter.25.cloned.1.call-start = ((), (), s32[]{:S(2)}) async-start(), calls=%async_computation.21 | async-start | bytes 6553600
  1130.0 159.9 %reduce-scatter.21.cloned.1.call-start = ((), (), s32[]{:S(2)}) async-start(), calls=%async_computation.19 | async-start | bytes 2457600 | tf_op jit(solution)/shard_map/reduce_scatter | solution.py:380
  1135.2 218.1 %reduce-scatter.19.cloned.1.call-start = ((), (), s32[]{:S(2)}) async-start(), calls=%async_computation.18 | async-start | bytes 3993600 | tf_op jit(solution)/shard_map/reduce_scatter | solution.py:377
  1157.9 365.3 %reduce-scatter.23.cloned.1.call-start = ((), (), s32[]{:S(2)}) async-start(), calls=%async_computation.20 | async-start | bytes 12288000 | tf_op jit(solution)/shard_map/reduce_scatter | solution.py:383
  1196.7 349.2 %reduce-scatter.27.cloned.1.call-start = ((), (), s32[]{:S(2)}) async-start(), calls=%async_computation.22 | async-start | bytes 307200
  1201.8 321.5 %copy-start.152 = (bf16[960]{0:T(1024)(128)(2,1)S(1)}, bf16[960]{0:T(1024)(128)(2,1)}, u32[]{:S(2)}) copy-start(bf16[960]{0:T(1024)(128)(2,1)} %get-tuple-element.1500) | copy-start | bytes 5764
  1201.8 322.1 %copy-start.161 = (f32[960]{0:T(1024)S(1)}, f32[960]{0:T(1024)}, u32[]{:S(2)}) copy-start(f32[960]{0:T(1024)} %get-tuple-element.1490) | copy-start | bytes 11524
  1201.8 322.1 %copy-start.163 = (f32[960]{0:T(1024)S(1)}, f32[960]{0:T(1024)}, u32[]{:S(2)}) copy-start(f32[960]{0:T(1024)} %get-tuple-element.1488) | copy-start | bytes 11524
  1201.8 322.1 %copy-start.165 = (f32[960]{0:T(1024)S(1)}, f32[960]{0:T(1024)}, u32[]{:S(2)}) copy-start(f32[960]{0:T(1024)} %get-tuple-element.1492) | copy-start | bytes 11524
  1201.8 345.0 %copy-start.34 = (bf16[1,256,960]{1,2,0:T(8,128)(2,1)S(1)}, bf16[1,256,960]{1,2,0:T(8,128)(2,1)}, u32[]{:S(2)}) copy-start(bf16[1,256,960]{1,2,0:T(8,128)(2,1)} %param.29) | copy-start | bytes 1474564
  1201.8 345.0 %copy-start.79 = (bf16[256,15,64]{0,2,1:T(8,128)(2,1)S(1)}, bf16[256,15,64]{0,2,1:T(8,128)(2,1)}, u32[]{:S(2)}) copy-start(bf16[256,15,64]{0,2,1:T(8,128)(2,1)} %copy-done.78) | copy-start | bytes 1474564
  1201.8 345.0 %copy-start.98 = (bf16[256,5,64]{0,2,1:T(8,128)(2,1)S(1)}, bf16[256,5,64]{0,2,1:T(8,128)(2,1)}, u32[]{:S(2)}) copy-start(bf16[256,5,64]{0,2,1:T(8,128)(2,1)} %copy-done.97) | copy-start | bytes 491524
  1201.8 437.6 %all-reduce.10.cloned.1.call-start = ((), (), s32[]{:S(2)}) async-start(), calls=%async_computation.23 | async-start | bytes 9953280 | tf_op jit(solution)/shard_map/psum | solution.py:400
  (192 other events, 2123.3 us)
Sparse Core Ops, SparseCore 0:
  9.6 67.0 all-gather.9
  82.5 29.1 all-gather.11
  113.3 43.5 all-gather.13
  158.3 172.0 all-gather.15
  331.8 90.8 all-gather.17
  431.8 28.9 all-gather.19
  583.4 30.4 all-gather.21
  817.9 43.6 reduce-scatter.12
  959.5 43.6 reduce-scatter.14
  1105.4 43.6 reduce-scatter.16
  1151.4 93.7 reduce-scatter.24
  1247.9 41.9 reduce-scatter.20
  1292.8 60.3 reduce-scatter.18
  1355.6 167.5 reduce-scatter.22
  1525.3 20.5 reduce-scatter.26
  1550.6 88.7 all-reduce.9
where the time goes:
time: 1660 us; the launch traced here: 1650 us
  waiting for transfers between devices  811 us (49%)
  matrix products  385 us (23%)
  local copies, waits for them, and re-layouts  174 us (10%)
  other arithmetic  136 us (8%)
  loops' own time  72.8 us (4%)
  blocking collectives  55.9 us (3%)
  between operations  18.3 us (1%)
    reduce_scatter x1, waiting for transfers between devices, per_device(): lax.psum_scatter(gate_total.astype(jnp.bfloat16), 'fsdp', scatter_dimensi...  170 us
    all_gather x1, waiting for transfers between devices, per_device(): lax.all_gather(gate_up_weight, 'fsdp', axis=0, tiled=True)  123 us
    reduce_scatter x3, waiting for transfers between devices, per_device(): lax.psum_scatter(grad_kv_all.astype(jnp.bfloat16), 'dp', scatter_dimensio...  88.5 us
    all_gather x1, waiting for transfers between devices, per_device(): lax.all_gather(down_weight, 'fsdp', axis=0, tiled=True)  83.4 us
    unnamed x18, waiting for transfers between devices  67.9 us
    reduce_scatter x1, waiting for transfers between devices, per_device(): lax.psum_scatter(qkv_total.astype(jnp.bfloat16), 'fsdp', scatter_dimensio...  63.3 us
    all_gather x3, waiting for transfers between devices, per_device(): keys_all = lax.all_gather(kv_local, 'dp', axis=0, tiled=True)  63 us
    psum x1, waiting for transfers between devices, per_device(): lax.psum(shards[0].astype(jnp.bfloat16), 'dp').astype(jnp.float32)  61.9 us
  transfers between devices with their start and end apart: 16, of which 15 were waited for; matrix products, arithmetic and copies ran while one was open for 12% of the time, Pallas kernels for 0%

commit v1 on v0

--- a/solution.py
+++ b/solution.py
@@ -82,7 +82,9 @@
     depth_all = lax.all_gather(depth_here, "dp", axis=0, tiled=True)
     lengths_here = lengths[0]
     token_index = jnp.arange(group_rows, dtype=jnp.int32)
-    seq_ends = jnp.cumsum(lengths_here)
+    count_seq = lengths_here.shape[0]
+    not_after = jnp.arange(count_seq)[:, None] <= jnp.arange(count_seq)[None, :]
+    seq_ends = jnp.sum(jnp.where(not_after, lengths_here[:, None], 0), axis=0)
     passed = (token_index[:, None] >= seq_ends[None, :]).astype(jnp.int32)
     seq_all = jnp.sum(passed, axis=1)
     seq_start = jnp.sum(passed * lengths_here[None, :], axis=1)

time: 1660 us -> 1660 us (level)
  no operation moved by 1% of the time
where the time goes in v1:
time: 1660 us; the launch traced here: 1650 us
  waiting for transfers between devices  811 us (49%)
  matrix products  385 us (23%)
  local copies, waits for them, and re-layouts  174 us (10%)
  other arithmetic  136 us (8%)
  loops' own time  72.8 us (4%)
  blocking collectives  55.9 us (3%)
  between operations  18.3 us (1%)
    reduce_scatter x1, waiting for transfers between devices, per_device(): lax.psum_scatter(gate_total.astype(jnp.bfloat16), 'fsdp', scatter_dimensi...  170 us
    all_gather x1, waiting for transfers between devices, per_device(): lax.all_gather(gate_up_weight, 'fsdp', axis=0, tiled=True)  123 us
    reduce_scatter x3, waiting for transfers between devices, per_device(): lax.psum_scatter(grad_kv_all.astype(jnp.bfloat16), 'dp', scatter_dimensio...  88.5 us
    all_gather x1, waiting for transfers between devices, per_device(): lax.all_gather(down_weight, 'fsdp', axis=0, tiled=True)  83.4 us
    unnamed x18, waiting for transfers between devices  67.9 us
    reduce_scatter x1, waiting for transfers between devices, per_device(): lax.psum_scatter(qkv_total.astype(jnp.bfloat16), 'fsdp', scatter_dimensio...  63.3 us
    all_gather x3, waiting for transfers between devices, per_device(): keys_all = lax.all_gather(kv_local, 'dp', axis=0, tiled=True)  63 us
    psum x1, waiting for transfers between devices, per_device(): lax.psum(shards[0].astype(jnp.bfloat16), 'dp').astype(jnp.float32)  61.8 us
  transfers between devices with their start and end apart: 16, of which 15 were waited for; matrix products, arithmetic and copies ran while one was open for 12% of the time, Pallas kernels for 0%

profile of v1, /device:TPU:0, one launch (start us, length us, event | category | flops | bytes accessed | tf_op | source)
XLA Modules:
  0.0 1654.9 jit_solution(7339996573909270204)
XLA Ops:
  11.7 13.5 all-reduce.7
  28.8 47.8 %all-gather.10.cloned.1.call-done = bf16[960,1600]{1,0:T(8,128)(2,1)} async-done(((bf16[240,1600]{1,0:T(8,128)(2,1)}), bf16[960,1600]{1,0:T(8,128)(2,1)}) %all-gather.10.cloned.1.call-update) | async-done | bytes 3072016 | tf_op jit(solution)/shard_map/all_gather | solution.py:164
  84.4 8.9 all-gather
  93.9 11.9 all-gather.1
  115.2 58.8 %while.111 = (s32[]{:T(128)}, f32[5,3,256]{2,1,0:T(4,128)S(1)}, f32[5,3,256]{2,1,0:T(4,128)S(1)}, s32[256]{0:T(256)S(1)}, s32[4]{0:T(128)S(1)}, /*index=5*/s32[2...) while((s32[]{:T(128)}, f32[5,3,256]{2,1,0:T(4,128)S(1)}, ...), condition=%wide.region_7.8_spmd.clone, body=%wide.region_4.7_spmd.clone.sunk | while | flops 268193792 | bytes 19123400 | solution.py:193
  174.1 28.9 %while.112 = (s32[]{:T(128)}, f32[256,5,3,64]{0,3,2,1:T(8,128)S(1)}, bf16[4,512,640]{1,2,0:T(8,128)(2,1)}, s32[256]{0:T(256)S(1)}, s32[4]{0:T(128)S(1)}, /*index...) while((s32[]{:T(128)}, f32[256,5,3,64]{0,3,2,1:T(8,128)S(1)}, ...), condition=%wide.region_9.10_spmd.clone, body=%wide.region_8.9_spmd.clone.sunk | while | flops 512460032 | bytes 6028489 | solution.py:212
  207.7 122.7 %all-gather.16.cloned.1.call-done = bf16[960,5120]{1,0:T(8,128)(2,1)} async-done(((bf16[240,5120]{1,0:T(8,128)(2,1)}), bf16[960,5120]{1,0:T(8,128)(2,1)}) %all-gather.16.cloned.1.call-update) | async-done | bytes 9830416 | tf_op jit(solution)/shard_map/all_gather | solution.py:166
  339.3 83.4 %all-gather.18.cloned.1.call-done = bf16[2560,960]{0,1:T(8,128)(2,1)} async-done(((bf16[640,960]{0,1:T(8,128)(2,1)}), bf16[2560,960]{0,1:T(8,128)(2,1)}) %all-gather.18.cloned.1.call-update) | async-done | bytes 4915216 | tf_op jit(solution)/shard_map/all_gather | solution.py:167
  432.9 27.9 %all-gather.20.cloned.1.call-done = bf16[2048,640]{0,1:T(8,128)(2,1)} async-done(((bf16[256,640]{0,1:T(8,128)(2,1)}), bf16[2048,640]{0,1:T(8,128)(2,1)}) %all-gather.20.cloned.1.call-update) | async-done | bytes 2621456 | tf_op jit(solution)/shard_map/all_gather | solution.py:176
  464.2 57.3 %while.113 = (s32[]{:T(128)}, f32[5,3,256]{2,1,0:T(4,128)S(1)}, f32[5,3,256]{2,1,0:T(4,128)S(1)}, s32[256]{0:T(256)S(1)}, s32[4]{0:T(128)S(1)}, /*index=5*/s32[2...) while((s32[]{:T(128)}, f32[5,3,256]{2,1,0:T(4,128)S(1)}, ...), condition=%wide.region_15.16_spmd.clone, body=%wide.region_12.15_spmd.clone.sunk | while | flops 268193792 | bytes 19123400 | solution.py:193
  522.2 43.4 %while.114 = (s32[]{:T(128)}, f32[256,5,3,64]{0,3,2,1:T(8,128)}, bf16[4,512,640]{1,2,0:T(8,128)(2,1)}, s32[256]{0:T(256)S(1)}, s32[4]{0:T(128)S(1)}, /*index=5*/...) while((s32[]{:T(128)}, f32[256,5,3,64]{0,3,2,1:T(8,128)}, ...), condition=%wide.region_17.18_spmd.clone, body=%wide.region_16.17_spmd.clone.sunk | while | flops 512460032 | bytes 6028489 | solution.py:212
  584.2 29.7 %all-gather.22.cloned.1.call-done = bf16[2048,640]{0,1:T(8,128)(2,1)} async-done(((bf16[256,640]{0,1:T(8,128)(2,1)}), bf16[2048,640]{0,1:T(8,128)(2,1)}) %all-gather.22.cloned.1.call-update) | async-done | bytes 2621456 | tf_op jit(solution)/shard_map/all_gather | solution.py:176
  617.4 57.2 %while.115 = (s32[]{:T(128)}, f32[5,3,256]{2,1,0:T(4,128)S(1)}, f32[5,3,256]{2,1,0:T(4,128)S(1)}, s32[256]{0:T(256)S(1)}, s32[4]{0:T(128)S(1)}, /*index=5*/s32[2...) while((s32[]{:T(128)}, f32[5,3,256]{2,1,0:T(4,128)S(1)}, ...), condition=%wide.region_23.24_spmd.clone, body=%wide.region_20.23_spmd.clone.sunk | while | flops 268193792 | bytes 19123400 | solution.py:193
  674.6 35.7 %while.116 = (s32[]{:T(128)}, f32[256,5,3,64]{0,3,2,1:T(8,128)}, bf16[4,512,640]{1,2,0:T(8,128)(2,1)}, s32[256]{0:T(256)S(1)}, s32[4]{0:T(128)S(1)}, /*index=5*/...) while((s32[]{:T(128)}, f32[256,5,3,64]{0,3,2,1:T(8,128)}, ...), condition=%wide.region_25.26_spmd.clone, body=%wide.region_24.25_spmd.clone.sunk | while | flops 512460032 | bytes 6028489 | solution.py:212
  732.9 80.4 %while.117 = (s32[]{:T(128)}, f32[256,5,3,64]{0,3,2,1:T(8,128)}, bf16[4,512,640]{2,1,0:T(8,128)(2,1)}, bf16[4,512,640]{1,2,0:T(8,128)(2,1)}, s32[256]{0:T(256)S(...) while((s32[]{:T(128)}, f32[256,5,3,64]{0,3,2,1:T(8,128)}, ...), condition=%wide.region_30.31_spmd.clone, body=%wide.region_29.30_spmd.clone.sunk | while | flops 1281115392 | bytes 67630896 | solution.py:348
  819.5 42.1 %reduce-scatter.13.cloned.1.call-done = bf16[256,640]{0,1:T(8,128)(2,1)} async-done(((bf16[2048,640]{0,1:T(8,128)(2,1)}), bf16[256,640]{0,1:T(8,128)(2,1)}) %reduce-scatter.13.cloned.1.call-update) | async-done | bytes 327696 | tf_op jit(solution)/shard_map/reduce_scatter | solution.py:354
  883.1 71.4 %while.118 = (s32[]{:T(128)}, f32[256,5,3,64]{0,3,2,1:T(8,128)S(1)}, bf16[4,512,640]{2,1,0:T(8,128)(2,1)}, bf16[4,512,640]{1,2,0:T(8,128)(2,1)}, s32[256]{0:T(25...) while((s32[]{:T(128)}, f32[256,5,3,64]{0,3,2,1:T(8,128)S(1)}, ...), condition=%wide.region_37.38_spmd.clone, body=%wide.region_36.37_spmd.clone.sunk | while | flops 1281115392 | bytes 65664792 | solution.py:348
  961.5 41.6 %reduce-scatter.15.cloned.1.call-done = bf16[256,640]{0,1:T(8,128)(2,1)} async-done(((bf16[2048,640]{0,1:T(8,128)(2,1)}), bf16[256,640]{0,1:T(8,128)(2,1)}) %reduce-scatter.15.cloned.1.call-update) | async-done | bytes 327696 | tf_op jit(solution)/shard_map/reduce_scatter | solution.py:354
  1024.6 76.1 %while.119 = (s32[]{:T(128)}, f32[256,5,3,64]{0,3,2,1:T(8,128)}, bf16[4,512,640]{2,1,0:T(8,128)(2,1)}, bf16[4,512,640]{1,2,0:T(8,128)(2,1)}, s32[256]{0:T(256)S(...) while((s32[]{:T(128)}, f32[256,5,3,64]{0,3,2,1:T(8,128)}, ...), condition=%wide.region_44.45_spmd.clone, body=%wide.region_43.44_spmd.clone.sunk | while | flops 1281115392 | bytes 65664792 | solution.py:348
  1113.7 8.4 add_convert_fusion.1
  1122.1 7.9 copy.229
  1159.3 11.3 fusion.117
  1170.6 8.3 fusion.115
  1178.9 17.8 %add_convert_fusion = bf16[960,5120]{1,0:T(8,128)(2,1)} fusion(f32[960,5120]{1,0:T(8,128)} %fusion.117, f32[960,5120]{1,0:T(8,128)} %fusion.115, bf16[256,2560]{1,0:T(8,128)(2,1)S(1)} %copy-done.91, bf16[256,2560]{1,0:T(8,128)(2,1)S(1)} %copy-done.89, f32[256,960]{0,1:T(8,128)S(1)} %copy-done.18, f32[960]{0:T(1024)S(1)} %convert_element_type.305, ...), kind=kOutput, calls=%fused_computation.159 | convolution fusion | flops 2537308160 | bytes 52761344 | tf_op jit(solution)/shard_map/td,tf->df/dot_general | solution.py:281
  1201.9 43.3 %reduce-scatter.25.cloned.1.call-done = bf16[640,960]{1,0:T(8,128)(2,1)} async-done(((bf16[2560,960]{1,0:T(8,128)(2,1)}), bf16[640,960]{1,0:T(8,128)(2,1)}) %reduce-scatter.25.cloned.1.call-update) | async-done | bytes 1228816
  1247.6 42.3 %reduce-scatter.21.cloned.1.call-done = bf16[240,960]{1,0:T(8,128)(2,1)} async-done(((bf16[960,960]{1,0:T(8,128)(2,1)}), bf16[240,960]{1,0:T(8,128)(2,1)}) %reduce-scatter.21.cloned.1.call-update) | async-done | bytes 460816 | tf_op jit(solution)/shard_map/reduce_scatter | solution.py:382
  1289.9 63.3 %reduce-scatter.19.cloned.1.call-done = bf16[240,1600]{1,0:T(8,128)(2,1)} async-done(((bf16[960,1600]{1,0:T(8,128)(2,1)}), bf16[240,1600]{1,0:T(8,128)(2,1)}) %reduce-scatter.19.cloned.1.call-update) | async-done | bytes 768016 | tf_op jit(solution)/shard_map/reduce_scatter | solution.py:379
  1353.2 170.0 %reduce-scatter.23.cloned.1.call-done = bf16[240,5120]{1,0:T(8,128)(2,1)} async-done(((bf16[960,5120]{1,0:T(8,128)(2,1)}), bf16[240,5120]{1,0:T(8,128)(2,1)}) %reduce-scatter.23.cloned.1.call-update) | async-done | bytes 2457616 | tf_op jit(solution)/shard_map/reduce_scatter | solution.py:385
  1523.9 22.0 %reduce-scatter.27.cloned.1.call-done = bf16[240,3]{1,0:T(8,128)(2,1)} async-done(((bf16[960,3]{1,0:T(8,128)(2,1)}), bf16[240,3]{1,0:T(8,128)(2,1)}) %reduce-scatter.27.cloned.1.call-update) | async-done | bytes 1456
  1550.9 8.8 all-reduce.6
  1559.9 12.8 all-reduce.4
  1577.5 61.8 %all-reduce.10.cloned.1.call-done = (bf16[240,1600]{1,0:T(8,128)(2,1)}, bf16[240,960]{1,0:T(8,128)(2,1)}, bf16[240,5120]{1,0:T(8,128)(2,1)}, bf16[640,960]{0,1:T(8,128)(2,1)}) async-done(((bf16[240,1600]{1,0:T(8,128)(2,1)}, bf16[240,960]{1,0:T(8,128)(2,1)}, bf16[240,5120]{1,0:T(8,128)(2,1)}, bf16[640,960]{0,1:T(8,128)(2,1)}), (bf16[240,1600]{1,0:T(8,128)(2,1)}, bf16[240,960]{1,0:T(8,128)(2,1)}, ...) | async-done | bytes 4915216 | tf_op jit(solution)/shard_map/psum | solution.py:402
  (1090 shorter events, 656.3 us)
Async XLA Ops:
  7.2 69.5 %all-gather.10.cloned.1.call-start = ((), (), s32[]{:S(2)}) async-start(), calls=%async_computation.8 | async-start | bytes 3993600 | tf_op jit(solution)/shard_map/all_gather | solution.py:164
  7.9 103.8 %all-gather.12.cloned.1.call-start = ((), (), s32[]{:S(2)}) async-start(), calls=%async_computation.9 | async-start | bytes 2949120 | tf_op jit(solution)/shard_map/all_gather | solution.py:176
  25.2 554.9 %copy-start.93 = (f32[960]{0:T(1024)}, f32[960]{0:T(1024)S(1)}, u32[]{:S(2)}) copy-start(f32[960]{0:T(1024)S(1)} %convert_element_type.298) | copy-start | bytes 11524
  28.8 554.8 %copy-start.45 = (f32[256,32]{0,1:T(8,128)}, f32[256,32]{0,1:T(8,128)S(1)}, u32[]{:S(2)}) copy-start(f32[256,32]{0,1:T(8,128)S(1)} %get-tuple-element.1789) | copy-start | bytes 98308
  28.8 554.8 %copy-start.47 = (f32[256,32]{0,1:T(8,128)}, f32[256,32]{0,1:T(8,128)S(1)}, u32[]{:S(2)}) copy-start(f32[256,32]{0,1:T(8,128)S(1)} %get-tuple-element.1790) | copy-start | bytes 98308
  82.4 120.7 %all-gather.14.cloned.1.call-start = ((), (), s32[]{:S(2)}) async-start(), calls=%async_computation.10 | async-start | bytes 2457600 | tf_op jit(solution)/shard_map/all_gather | solution.py:165
  83.2 247.2 %all-gather.16.cloned.1.call-start = ((), (), s32[]{:S(2)}) async-start(), calls=%async_computation.11 | async-start | bytes 12288000 | tf_op jit(solution)/shard_map/all_gather | solution.py:166
  83.7 339.0 %all-gather.18.cloned.1.call-start = ((), (), s32[]{:S(2)}) async-start(), calls=%async_computation.12 | async-start | bytes 6144000 | tf_op jit(solution)/shard_map/all_gather | solution.py:167
  84.3 376.4 %all-gather.20.cloned.1.call-start = ((), (), s32[]{:S(2)}) async-start(), calls=%async_computation.13 | async-start | bytes 2949120 | tf_op jit(solution)/shard_map/all_gather | solution.py:176
  93.8 339.1 %copy-start.155 = (pred[256]{0:T(512)(128)(4,1)}, pred[256]{0:T(512)(128)(4,1)S(1)}, u32[]{:S(2)}) copy-start(pred[256]{0:T(512)(128)(4,1)S(1)} %get-tuple-element.1504) | copy-start | bytes 772
  105.9 477.9 %copy-start.114 = (bf16[960,3]{0,1:T(4,128)(2,1)}, bf16[960,3]{0,1:T(4,128)(2,1)S(1)}, u32[]{:S(2)}) copy-start(bf16[960,3]{0,1:T(4,128)(2,1)S(1)} %reshape.536) | copy-start | bytes 17284
  106.1 316.6 %copy-start.150 = (f32[256]{0:T(256)}, f32[256]{0:T(256)S(1)}, u32[]{:S(2)}) copy-start(f32[256]{0:T(256)S(1)} %broadcast_select_fusion.2) | copy-start | bytes 3076
  431.7 182.2 %all-gather.22.cloned.1.call-start = ((), (), s32[]{:S(2)}) async-start(), calls=%async_computation.14 | async-start | bytes 2949120 | tf_op jit(solution)/shard_map/all_gather | solution.py:176
  579.5 287.3 %copy-start.9 = (f32[256,960]{0,1:T(8,128)}, f32[256,960]{0,1:T(8,128)S(1)}, u32[]{:S(2)}) copy-start(f32[256,960]{0,1:T(8,128)S(1)} %get-tuple-element.1724) | copy-start | bytes 2949124
  583.2 278.4 %reduce-scatter.13.cloned.1.call-start = ((), (), s32[]{:S(2)}) async-start(), calls=%async_computation.15 | async-start | bytes 2949120 | tf_op jit(solution)/shard_map/reduce_scatter | solution.py:354
  714.4 152.4 %copy-start.118 = (f32[256]{0:T(256)}, f32[256]{0:T(256)S(1)}, u32[]{:S(2)}) copy-start(f32[256]{0:T(256)S(1)} %get-tuple-element.1802) | copy-start | bytes 3076
  714.4 152.4 %copy-start.127 = (f32[256]{0:T(256)}, f32[256]{0:T(256)S(1)}, u32[]{:S(2)}) copy-start(f32[256]{0:T(256)S(1)} %get-tuple-element.1817) | copy-start | bytes 3076
  817.8 185.3 %reduce-scatter.15.cloned.1.call-start = ((), (), s32[]{:S(2)}) async-start(), calls=%async_computation.16 | async-start | bytes 2949120 | tf_op jit(solution)/shard_map/reduce_scatter | solution.py:354
  959.4 189.7 %reduce-scatter.17.cloned.1.call-start = ((), (), s32[]{:S(2)}) async-start(), calls=%async_computation.17 | async-start | bytes 2949120 | tf_op jit(solution)/shard_map/reduce_scatter | solution.py:354
  1105.3 139.9 %reduce-scatter.25.cloned.1.call-start = ((), (), s32[]{:S(2)}) async-start(), calls=%async_computation.21 | async-start | bytes 6553600
  1130.0 159.9 %reduce-scatter.21.cloned.1.call-start = ((), (), s32[]{:S(2)}) async-start(), calls=%async_computation.19 | async-start | bytes 2457600 | tf_op jit(solution)/shard_map/reduce_scatter | solution.py:382
  1135.2 218.0 %reduce-scatter.19.cloned.1.call-start = ((), (), s32[]{:S(2)}) async-start(), calls=%async_computation.18 | async-start | bytes 3993600 | tf_op jit(solution)/shard_map/reduce_scatter | solution.py:379
  1157.9 365.3 %reduce-scatter.23.cloned.1.call-start = ((), (), s32[]{:S(2)}) async-start(), calls=%async_computation.20 | async-start | bytes 12288000 | tf_op jit(solution)/shard_map/reduce_scatter | solution.py:385
  1196.7 349.2 %reduce-scatter.27.cloned.1.call-start = ((), (), s32[]{:S(2)}) async-start(), calls=%async_computation.22 | async-start | bytes 307200
  1201.7 321.5 %copy-start.152 = (bf16[960]{0:T(1024)(128)(2,1)S(1)}, bf16[960]{0:T(1024)(128)(2,1)}, u32[]{:S(2)}) copy-start(bf16[960]{0:T(1024)(128)(2,1)} %get-tuple-element.1500) | copy-start | bytes 5764
  1201.7 322.1 %copy-start.161 = (f32[960]{0:T(1024)S(1)}, f32[960]{0:T(1024)}, u32[]{:S(2)}) copy-start(f32[960]{0:T(1024)} %get-tuple-element.1490) | copy-start | bytes 11524
  1201.8 322.1 %copy-start.163 = (f32[960]{0:T(1024)S(1)}, f32[960]{0:T(1024)}, u32[]{:S(2)}) copy-start(f32[960]{0:T(1024)} %get-tuple-element.1488) | copy-start | bytes 11524
  1201.8 322.1 %copy-start.165 = (f32[960]{0:T(1024)S(1)}, f32[960]{0:T(1024)}, u32[]{:S(2)}) copy-start(f32[960]{0:T(1024)} %get-tuple-element.1492) | copy-start | bytes 11524
  1201.8 345.0 %copy-start.34 = (bf16[1,256,960]{1,2,0:T(8,128)(2,1)S(1)}, bf16[1,256,960]{1,2,0:T(8,128)(2,1)}, u32[]{:S(2)}) copy-start(bf16[1,256,960]{1,2,0:T(8,128)(2,1)} %param.29) | copy-start | bytes 1474564
  1201.8 345.0 %copy-start.79 = (bf16[256,15,64]{0,2,1:T(8,128)(2,1)S(1)}, bf16[256,15,64]{0,2,1:T(8,128)(2,1)}, u32[]{:S(2)}) copy-start(bf16[256,15,64]{0,2,1:T(8,128)(2,1)} %copy-done.78) | copy-start | bytes 1474564
  1201.8 345.0 %copy-start.98 = (bf16[256,5,64]{0,2,1:T(8,128)(2,1)S(1)}, bf16[256,5,64]{0,2,1:T(8,128)(2,1)}, u32[]{:S(2)}) copy-start(bf16[256,5,64]{0,2,1:T(8,128)(2,1)} %copy-done.97) | copy-start | bytes 491524
  1201.8 437.5 %all-reduce.10.cloned.1.call-start = ((), (), s32[]{:S(2)}) async-start(), calls=%async_computation.23 | async-start | bytes 9953280 | tf_op jit(solution)/shard_map/psum | solution.py:402
  (192 other events, 2123.1 us)
Sparse Core Ops, SparseCore 0:
  9.6 67.0 all-gather.9
  82.5 29.1 all-gather.11
  113.3 43.5 all-gather.13
  158.3 172.0 all-gather.15
  331.8 90.8 all-gather.17
  431.8 28.9 all-gather.19
  583.4 30.4 all-gather.21
  817.9 43.6 reduce-scatter.12
  959.5 43.6 reduce-scatter.14
  1105.4 43.6 reduce-scatter.16
  1151.4 93.7 reduce-scatter.24
  1247.9 41.9 reduce-scatter.20
  1292.8 60.4 reduce-scatter.18
  1355.6 167.5 reduce-scatter.22
  1525.3 20.5 reduce-scatter.26
  1550.5 88.7 all-reduce.9

commit v2 on v0

v2 whole, which is shorter than its diff:
```python
import functools
import math

import jax
import jax.numpy as jnp
from jax import lax
from jax.experimental import pallas as pl
from jax.experimental.pallas import tpu as pltpu
from jax.sharding import PartitionSpec as P

D = 960
HEADS = 15
KV_HEADS = 5
GROUPED = 3
HEAD = 64
FF = 2560
STEPS = 3
EPSILON = 1e-05
LANES = 128
Q_COLS = 1024
KV_COLS = 640
ALL_COLS = Q_COLS + KV_COLS
PAD_Q = HEADS * LANES
KEYS = 512
FF_BLOCK = 512
FAR = 1 << 30
LOW = -1e30
START_MAX = -1e20
SCALE = HEAD**-0.5
BF = jnp.bfloat16
F32 = jnp.float32
ANY = pl.BlockSpec(memory_space=pl.ANY)
VMEM = pl.BlockSpec(memory_space=pltpu.VMEM)
MIB = 1 << 20


def dot(a, b):
    return jnp.dot(a, b, preferred_element_type=F32)


def dot_nt(a, b):
    return lax.dot_general(a, b, (((1,), (1,)), ((), ())), preferred_element_type=F32)


def dot_tn(a, b):
    return lax.dot_general(a, b, (((0,), (0,)), ((), ())), preferred_element_type=F32)


def call(kernel, outs, args, specs, scratch, flops, limit, out_specs=None):
    moved = sum(math.prod(x.shape) * x.dtype.itemsize for x in args)
    moved += sum(math.prod(x.shape) * x.dtype.itemsize for x in outs)
    return pl.pallas_call(
        kernel,
        out_shape=outs,
        in_specs=specs,
        out_specs=out_specs or [VMEM] * len(outs),
        scratch_shapes=scratch,
        compiler_params=pltpu.CompilerParams(vmem_limit_bytes=limit * MIB),
        cost_estimate=pl.CostEstimate(flops=flops, bytes_accessed=moved, transcendentals=0),
    )(*args)


def shaped(*shape, dtype=F32):
    return jax.ShapeDtypeStruct(shape, dtype)


def pairs(size, bit):
    return [(i, i ^ bit) for i in range(size)]


def outer_bits(size):
    return [b for b in (2, 4, 8, 16, 32) if b < size]


def tie(values, *others):
    values = tuple(values)
    return lax.optimization_barrier((*values, *others))[: len(values)]


def spread_first(piece, axis, size):
    return {b: lax.ppermute(piece, "dp", pairs(size, b)) for b in outer_bits(size)}


def part(x, axis, start, stop):
    return lax.slice_in_dim(x, start, stop, axis=axis)


def spread(piece, axis, split, size):
    rows = piece.shape[axis]
    got = {(0, 0): (rows, piece)}
    bits = outer_bits(size)
    for b in bits:
        got[b, 0] = (rows, lax.ppermute(piece, "dp", pairs(size, b)))
    if len(bits) == 2:
        got[6, 0] = (split, lax.ppermute(part(got[2, 0][1], axis, 0, split), "dp", pairs(size, 4)))
        got[6, split] = (rows - split, lax.ppermute(part(got[4, 0][1], axis, split, rows), "dp", pairs(size, 2)))
    else:
        for m in range(0, size, 2):
            if (m, 0) not in got:
                low_bit = m & -m
                got[m, 0] = (rows, lax.ppermute(got[m ^ low_bit, 0][1], "dp", pairs(size, low_bit)))
    if size > 1:
        for m, first in list(got):
            n, x = got[m, first]
            got[m | 1, first] = (n, lax.ppermute(x, "dp", pairs(size, 1)))
    return [(m, first, n, x) for (m, first), (n, x) in got.items()]


def add_up(*terms):
    return functools.reduce(jnp.add, [t.astype(F32) for t in terms])


def gather_halves(even, odd, size):
    if size > 1:
        got = lax.ppermute(odd, "dp", pairs(size, 1))
    else:
        got = jnp.zeros_like(even)
    cut = even.shape[1] // 2
    bits = outer_bits(size)
    if len(bits) == 2:
        both = lambda m, h: add_up(even[m, h], got[m, h])
        lo, hi = slice(0, cut), slice(cut, None)
        send_x = jnp.stack([both(1, lo), both(3, lo)]).astype(BF)
        send_y = jnp.stack([both(2, hi), both(3, hi)]).astype(BF)
        got_x = lax.ppermute(send_x, "dp", pairs(size, 2))
        got_y = lax.ppermute(send_y, "dp", pairs(size, 4))
        next_y = add_up(even[2, lo], got[2, lo], got_x[1]).astype(BF)
        next_x = add_up(even[1, hi], got[1, hi], got_y[1]).astype(BF)
        last_y = lax.ppermute(next_y, "dp", pairs(size, 4))
        last_x = lax.ppermute(next_x, "dp", pairs(size, 2))
        return (
            (add_up(even[0, lo], got[0, lo], got_x[0]).astype(BF), last_y),
            (add_up(even[0, hi], got[0, hi], got_y[0]).astype(BF), last_x),
        )
    held = [add_up(even[m], got[m]) for m in range(even.shape[0])]
    while len(held) > 1:
        n = len(held) // 2
        send = jnp.stack(held[n:]).astype(BF)
        came = lax.ppermute(send, "dp", pairs(size, 2 * n))
        held = [add_up(held[m], came[m]) for m in range(n)]
    whole = held[0].astype(BF)
    zero = jnp.zeros_like(whole)
    return ((whole[:cut], zero[:cut]), (whole[cut:], zero[cut:]))


def zig_pairs(size):
    def owner(c):
        return c if c < size else 2 * size - 1 - c

    return ([(s, owner(2 * s)) for s in range(size)], [(s, owner(2 * s + 1)) for s in range(size)])


def zig(x, size, rank):
    half = x.shape[0] // 2
    to_lo, to_hi = zig_pairs(size)
    lo = lax.ppermute(x[:half], "dp", to_lo)
    hi = lax.ppermute(x[half:], "dp", to_hi)
    swap = rank % 2 == 1
    return jnp.concatenate([jnp.where(swap, hi, lo), jnp.where(swap, lo, hi)], axis=0)


def unzig(x, size, rank):
    half = x.shape[0] // 2
    to_lo, to_hi = zig_pairs(size)
    swap = rank % 2 == 1
    first, second = x[:half], x[half:]
    lo = lax.ppermute(jnp.where(swap, second, first), "dp", [(b, a) for a, b in to_lo])
    hi = lax.ppermute(jnp.where(swap, first, second), "dp", [(b, a) for a, b in to_hi])
    return jnp.concatenate([lo, hi], axis=0)


def slice_rows(rows, size):
    unit = 8 if rows % 16 else 16
    return -(-rows // (unit * size)) * unit


def split_at(step):
    return step // 2 if step % 32 == 0 or step % 16 else (step // 32 + 1) * 16


def assemble_kernel(count, rows, step, spots, n_own, *refs):
    owns, refs = refs[:n_own], refs[n_own:]
    segments, out, sems = refs[:-2], refs[-2], refs[-1]
    rank, z = lax.axis_index("dp"), lax.axis_index("fsdp")
    copies = []

    def copy(src, dst):
        copies.append(pltpu.make_async_copy(src, dst, sems.at[len(copies)]))
        copies[-1].start()

    at = 0
    for own, n in zip(owns, rows):
        copy(own, out.at[z, pl.ds(at, n)])
        at += n
    for (m, first, n), segment in zip(spots, segments):
        unit = math.gcd(math.gcd(step, first) if first else step, 128)
        where = pl.multiple_of((rank ^ m) * step + first, unit)
        for k in range(count - 1):
            copy(segment.at[k], out.at[lax.rem(z + count - 1 - k, count), pl.ds(where, n)])
    for c in copies:
        c.wait()


def assemble(owns, segments, count, step, size):
    cols = owns[0].shape[1]
    rows = [x.shape[0] for x in owns]
    spots = [s[:3] for s in segments]
    arrays = [s[3] for s in segments]
    n = len(owns) + len(segments) * (count - 1)
    out = shaped(count, size * step, cols, dtype=BF)
    return call(
        functools.partial(assemble_kernel, count, rows, step, spots, len(owns)),
        [out],
        [*owns, *arrays],
        [ANY] * (len(owns) + len(arrays)),
        [pltpu.SemaphoreType.DMA((n,))],
        0,
        14,
    )[0]


def gather_weights(jobs, size, count, rank):
    shifts = [[(i, (i + k) % count) for i in range(count)] for k in range(1, count)]
    total = len(jobs)
    steps = [full.shape[0] // size for full, _ in jobs]
    bits = outer_bits(size)
    state = [{} for _ in jobs]
    results = [None] * total
    hold = None
    def stage(w, s):
        st, step = state[w], steps[w]
        cut = split_at(step)
        if s == 0:
            piece = lax.dynamic_slice_in_dim(jobs[w][0], rank * step, step)
            return [(("z", k), piece, "fsdp", shift) for k, shift in enumerate(shifts)]
        if s == 1:
            st[0, 0, step] = jnp.stack([st["z", k] for k in range(count - 1)])
            return [((b, 0, step), st[0, 0, step], "dp", pairs(size, b)) for b in bits]
        if s == 2 and len(bits) == 2:
            return [
                ((6, 0, cut), part(st[2, 0, step], 1, 0, cut), "dp", pairs(size, 4)),
                ((6, cut, step - cut), part(st[4, 0, step], 1, cut, step), "dp", pairs(size, 2)),
            ] + [((m | 1, 0, step), st[m, 0, step], "dp", pairs(size, 1)) for m in (0, 2, 4)]
        if s == 2:
            for m in range(0, size, 2):
                if (m, 0, step) not in st:
                    low = m & -m
                    st[m, 0, step] = lax.ppermute(st[m ^ low, 0, step], "dp", pairs(size, low))
            return [((m | 1, 0, step), st[m, 0, step], "dp", pairs(size, 1)) for m in range(0, size, 2)]
        if s == 3 and len(bits) == 2:
            return [((7, f, n), st[6, f, n], "dp", pairs(size, 1)) for f, n in ((0, cut), (cut, step - cut))]
        return []

    for phase in range(total + 4):
        sends, keys = [], []
        for w in range(total):
            s = phase - w
            if 0 <= s < 4:
                for key, *send in stage(w, s):
                    keys.append((w, key))
                    sends.append(send)
        if sends:
            arrays = [s[0] for s in sends]
            if hold is not None:
                arrays = tie(arrays, *hold)
            got = [lax.ppermute(a, axis, perm) for a, (_, axis, perm) in zip(arrays, sends)]
            got = lax.optimization_barrier(tuple(got))
            hold = got[:1]
            for (w, key), g in zip(keys, got):
                state[w][key] = g
        w = phase - 3
        if 0 <= w < total:
            segments = [(*k, v) for k, v in state[w].items() if k[0] != "z"]
            results[w] = assemble(jobs[w][1], segments, count, steps[w], size)
    return results


def lane_of(shape):
    return lax.broadcasted_iota(jnp.int32, shape, len(shape) - 1)


def swap_halves(x, lanes):
    return jnp.where(lanes % HEAD < HEAD // 2, pltpu.roll(x, LANES - HEAD // 2, 1), pltpu.roll(x, HEAD // 2, 1))


def load_rows(src, rows, dst, sems, base):
    return [
        pltpu.make_async_copy(src.at[k, pl.ds(rows[0], rows[1])], dst.at[pl.ds(k * rows[1], rows[1])], sems.at[base + k])
        for k in range(src.shape[0])
    ]


def norm_qkv_kernel(hid_ref, gain_ref, cos_ref, sin_ref, w_any, n1_ref, q_ref, kv_ref, w_ref, sems):
    rows = D // w_any.shape[0]
    copies = load_rows(w_any, (0, rows), w_ref, sems, 0)
    for c in copies:
        c.start()
    h = hid_ref[...]
    rho = lax.rsqrt(jnp.mean(h * h, axis=-1, keepdims=True) + EPSILON)
    n1 = (h * rho * gain_ref[...]).astype(BF)
    n1_ref[...] = n1
    for c in copies:
        c.wait()
    lanes = lane_of((h.shape[0], LANES))
    low = lanes < HEAD
    cos, sin = cos_ref[...], sin_ref[...]
    for b in range(Q_COLS // 256):
        wide = dot(n1, w_ref[:, 256 * b : 256 * (b + 1)]) * SCALE
        for i in range(2):
            x = wide[:, LANES * i : LANES * (i + 1)]
            x = x * cos + swap_halves(x, lanes) * sin
            head = 4 * b + 2 * i
            q_ref[:, LANES * head : LANES * (head + 1)] = jnp.where(low, x, 0.0).astype(BF)
            if head + 1 < HEADS:
                q_ref[:, LANES * (head + 1) : LANES * (head + 2)] = jnp.where(low, pltpu.roll(x, HEAD, 1), 0.0).astype(BF)
    cos, sin = jnp.where(low, cos, 1.0), jnp.where(low, sin, 0.0)
    wide = dot(n1, w_ref[:, Q_COLS:])
    for b in range(KV_HEADS):
        x = wide[:, LANES * b : LANES * (b + 1)]
        kv_ref[:, LANES * b : LANES * (b + 1)] = (x * cos + swap_halves(x, lanes) * sin).astype(BF)


def norm_qkv(h, gain, cos, sin, w):
    rows = h.shape[0]
    return call(
        norm_qkv_kernel,
        [shaped(rows, D, dtype=BF), shaped(rows, PAD_Q, dtype=BF), shaped(rows, KV_COLS, dtype=BF)],
        [h, gain, cos, sin, w],
        [VMEM] * 4 + [ANY],
        [pltpu.VMEM((D, ALL_COLS), BF), pltpu.SemaphoreType.DMA((w.shape[0],))],
        2 * rows * D * ALL_COLS,
        24,
    )


def kv_copies(spots, segments, kv_ref, sems, size, rank, half):
    copies = []
    for (m, first, n), segment in zip(spots, segments):
        for start in range(first, first + n, half):
            owner = rank ^ m
            chunk = owner if start == 0 else 2 * size - 1 - owner
            at = pl.multiple_of(chunk * half, half)
            copies.append(
                pltpu.make_async_copy(segment.at[pl.ds(start - first, half)], kv_ref.at[pl.ds(at, half)], sems.at[len(copies)])
            )
    return copies


def chunk_of(a, rank, size):
    return jnp.where(a == 0, rank, 2 * size - 1 - rank)


def stack3(ref, at, half, h):
    return jnp.concatenate(
        [ref[pl.ds(at, half), LANES * (GROUPED * h + g) : LANES * (GROUPED * h + g + 1)] for g in range(GROUPED)], axis=0
    )


def attend_kernel(spots, size, q_ref, tj_ref, meta_ref, *refs):
    segments, (o_ref, l_ref, kv_ref, kv1_ref, sems) = refs[: len(spots)], refs[len(spots) :]
    rank = lax.axis_index("dp")
    half = q_ref.shape[0] // 2
    copies = kv_copies(spots, segments, kv_ref, sems, size, rank, half)
    for c in copies:
        c.start()
    for c in copies:
        c.wait()
    blocks = tj_ref.shape[0]

    def ones(i, _):
        at = pl.ds(pl.multiple_of(i * KEYS, KEYS), KEYS)
        for h in range(KV_HEADS):
            cols = slice(LANES * h, LANES * (h + 1))
            x = kv_ref[at, cols]
            kv1_ref[at, cols] = jnp.where(lane_of(x.shape) < HEAD, jnp.ones_like(x), x)
        return 0

    lax.fori_loop(0, blocks, ones, 0)

    def one(a, _):
        at = pl.multiple_of(a * half, half)
        used = lax.div(chunk_of(a, rank, size) * half + half + KEYS - 1, KEYS)
        ti = jnp.concatenate([meta_ref[pl.ds(at, half), 0:1]] * GROUPED, axis=0)
        si = jnp.concatenate([meta_ref[pl.ds(at, half), 1:2]] * GROUPED, axis=0)
        lanes = lane_of((GROUPED * half, LANES))
        logs = jnp.zeros((GROUPED * half, LANES), F32)
        for h in range(KV_HEADS):
            cols = slice(LANES * h, LANES * (h + 1))
            q3 = stack3(q_ref, at, half, h)

            def block(kb, carry):
                top, acc = carry
                keys = pl.ds(pl.multiple_of(kb * KEYS, KEYS), KEYS)
                tj = tj_ref[pl.ds(kb, 1), :]
                s = dot_nt(q3, kv_ref[keys, cols])
                s = jnp.where((tj <= ti) & (tj >= si), s, LOW)
                new = jnp.maximum(top, jnp.max(s, axis=-1, keepdims=True))
                p = jnp.exp(s - new).astype(BF)
                acc = acc * jnp.exp(top - new) + dot(p, kv1_ref[keys, cols])
                return new, acc

            top, acc = lax.fori_loop(
                0,
                used,
                block,
                (jnp.full((GROUPED * half, 1), START_MAX, F32), jnp.zeros((GROUPED * half, LANES), F32)),
            )
            total = acc[:, 0:1]
            some = total > 0.0
            safe = jnp.where(some, total, 1.0)
            o = jnp.where((lanes >= HEAD) & some, acc / safe, 0.0).astype(BF)
            logs = jnp.where(lanes == h, top + jnp.log(safe), logs)
            for g in range(GROUPED):
                o_ref[pl.ds(at, half), LANES * (GROUPED * h + g) : LANES * (GROUPED * h + g + 1)] = o[g * half : (g + 1) * half]
        l_ref[a] = logs
        return 0

    lax.fori_loop(0, 2, one, 0)


def attend(q, segments, tj, meta, size):
    rows = q.shape[0]
    half = rows // 2
    total = tj.size
    spots = [s[:3] for s in segments]
    n = sum(s[1] // half for s in [(0, x[2]) for x in spots])
    return call(
        functools.partial(attend_kernel, spots, size),
        [shaped(rows, PAD_Q, dtype=BF), shaped(2, GROUPED * half, LANES)],
        [q, tj, meta, *[s[3] for s in segments]],
        [VMEM] * 3 + [ANY] * len(segments),
        [pltpu.VMEM((total, KV_COLS), BF), pltpu.VMEM((total, KV_COLS), BF), pltpu.SemaphoreType.DMA((n,))],
        4 * rows * total * HEADS * LANES // 2,
        32,
    )


def post_kernel(o_ref, hid_ref, gain_ref, router_ref, meta_ref, od_any, gu_any, *refs):
    ob_ref, m_ref, n2_ref, gu_ref, g_ref, new_ref, wo_ref, wd_ref, wgu_ref, sems, inner_ref = refs
    count = od_any.shape[0]
    r_out, r_down = D // count, FF // count
    wo_copies = load_rows(od_any, (0, r_out), wo_ref, sems, 0)
    wd_copies = load_rows(od_any, (r_out, r_down), wd_ref, sems, count)
    gu_copies = []
    for c in range(FF // FF_BLOCK):
        for side in range(2):
            at = side * FF + c * FF_BLOCK
            for k in range(count):
                gu_copies.append(
                    pltpu.make_async_copy(
                        gu_any.at[k, pl.ds(0, r_out), pl.ds(at, FF_BLOCK)],
                        wgu_ref.at[pl.ds(k * r_out, r_out), pl.ds(at, FF_BLOCK)],
                        sems.at[2 * count + len(gu_copies)],
                    )
                )
    for c in wo_copies + gu_copies + wd_copies:
        c.start()
    wo_ref[D:, :] = jnp.zeros((Q_COLS - D, D), BF)
    rows = hid_ref.shape[0]
    low = lane_of((rows, LANES)) < HEAD
    for b in range(Q_COLS // LANES):
        x = pltpu.roll(o_ref[:, LANES * 2 * b : LANES * (2 * b + 1)].astype(F32), HEAD, 1)
        if 2 * b + 1 < HEADS:
            x = jnp.where(low, x, o_ref[:, LANES * (2 * b + 1) : LANES * (2 * b + 2)].astype(F32))
        ob_ref[:, LANES * b : LANES * (b + 1)] = x.astype(BF)
    for c in wo_copies:
        c.wait()
    h = hid_ref[...]
    att = dot(ob_ref[...], wo_ref[...])
    m = h + att
    m_ref[...] = m
    rho = lax.rsqrt(jnp.mean(m * m, axis=-1, keepdims=True) + EPSILON)
    n2 = (m * rho * gain_ref[...]).astype(BF)
    n2_ref[...] = n2
    per = 2 * count
    for c in range(FF // FF_BLOCK):
        for k in range(per):
            gu_copies[c * per + k].wait()
        at = c * FF_BLOCK
        gate = dot(n2, wgu_ref[:, at : at + FF_BLOCK])
        up = dot(n2, wgu_ref[:, FF + at : FF + at + FF_BLOCK])
        gu_ref[:, at : at + FF_BLOCK] = gate.astype(BF)
        gu_ref[:, FF + at : FF + at + FF_BLOCK] = up.astype(BF)
        inner_ref[:, at : at + FF_BLOCK] = (gate * jax.nn.sigmoid(gate) * up).astype(BF)
    for c in wd_copies:
        c.wait()
    total = att + dot(inner_ref[...], wd_ref[...])
    gate = jax.nn.sigmoid(jnp.sum(h * router_ref[...], axis=-1, keepdims=True))
    g_ref[...] = jnp.broadcast_to(gate, g_ref.shape)
    live = meta_ref[:, 2:3] > 0
    new_ref[...] = h + jnp.where(live, gate * total, 0.0)


def weight_scratch(count):
    return [
        pltpu.VMEM((Q_COLS, D), BF),
        pltpu.VMEM((FF, D), BF),
        pltpu.VMEM((D, 2 * FF), BF),
        pltpu.SemaphoreType.DMA((2 * count + 2 * count * (FF // FF_BLOCK),)),
    ]


def post(o, h, gain, router, meta, od, gu):
    rows = h.shape[0]
    return call(
        post_kernel,
        [
            shaped(rows, Q_COLS, dtype=BF),
            shaped(rows, D),
            shaped(rows, D, dtype=BF),
            shaped(rows, 2 * FF, dtype=BF),
            shaped(rows, LANES),
            shaped(rows, D),
        ],
        [o, h, gain, router, meta, od, gu],
        [VMEM] * 5 + [ANY] * 2,
        [*weight_scratch(od.shape[0]), pltpu.VMEM((rows, FF), BF)],
        2 * rows * (D * Q_COLS + 3 * D * FF),
        48,
    )


def ffn_back_kernel(dh_ref, hid_ref, new_ref, g_ref, meta_ref, gu_ref, m_ref, gain_ref, od_any, gu_any, *refs):
    dfb_ref, dgu_ref, inner_ref, dm_ref, datt_ref, dob_ref, dz_ref, sums_ref, wo_ref, wd_ref, wgu_ref, sems = refs
    count = od_any.shape[0]
    r_out, r_down = D // count, FF // count
    wo_copies = load_rows(od_any, (0, r_out), wo_ref, sems, 0)
    wd_copies = load_rows(od_any, (r_out, r_down), wd_ref, sems, count)
    gu_copies = []
    for c in range(FF // FF_BLOCK):
        for side in range(2):
            at = side * FF + c * FF_BLOCK
            for k in range(count):
                gu_copies.append(
                    pltpu.make_async_copy(
                        gu_any.at[k, pl.ds(0, r_out), pl.ds(at, FF_BLOCK)],
                        wgu_ref.at[pl.ds(k * r_out, r_out), pl.ds(at, FF_BLOCK)],
                        sems.at[2 * count + len(gu_copies)],
                    )
                )
    for c in wd_copies + gu_copies + wo_copies:
        c.start()
    wo_ref[D:, :] = jnp.zeros((Q_COLS - D, D), BF)
    rows = hid_ref.shape[0]
    dh, h = dh_ref[...], hid_ref[...]
    live = meta_ref[:, 2:3] > 0
    gate = g_ref[:, 0:1]
    du = jnp.where(live, gate * dh, 0.0)
    dz = (1.0 - gate) * jnp.sum(dh * (new_ref[...] - h), axis=-1, keepdims=True)
    dz_ref[...] = jnp.broadcast_to(dz, dz_ref.shape)
    sums_ref[0:1, :] = jnp.sum(dz * h, axis=0, keepdims=True)
    dfb = du.astype(BF)
    dfb_ref[...] = dfb
    for c in range(FF // FF_BLOCK):
        at = c * FF_BLOCK
        for k in range(count):
            if at <= k * r_down < at + FF_BLOCK:
                wd_copies[k].wait()
        d_inner = dot_nt(dfb, wd_ref[at : at + FF_BLOCK, :])
        x = gu_ref[:, at : at + FF_BLOCK].astype(F32)
        up = gu_ref[:, FF + at : FF + at + FF_BLOCK].astype(F32)
        sig = jax.nn.sigmoid(x)
        silu = x * sig
        inner_ref[:, at : at + FF_BLOCK] = (silu * up).astype(BF)
        d_gate = (d_inner * up * (sig * (1.0 + x - silu))).astype(BF)
        d_up = (d_inner * silu).astype(BF)
        dgu_ref[:, at : at + FF_BLOCK] = d_gate
        dgu_ref[:, FF + at : FF + at + FF_BLOCK] = d_up
    for c in gu_copies:
        c.wait()
    dn2 = dot_nt(dgu_ref[...], wgu_ref[...])
    m = m_ref[...]
    rho = lax.rsqrt(jnp.mean(m * m, axis=-1, keepdims=True) + EPSILON)
    y = gain_ref[...] * dn2
    dm = rho * y - m * (rho * rho * rho) * jnp.mean(y * m, axis=-1, keepdims=True)
    dm_ref[...] = dm
    sums_ref[1:2, :] = jnp.sum(dn2 * m * rho, axis=0, keepdims=True)
    datt = (du + dm).astype(BF)
    datt_ref[...] = datt
    for c in wo_copies:
        c.wait()
    low = lane_of((rows, LANES)) < HEAD
    for b in range(Q_COLS // LANES):
        x = dot_nt(datt, wo_ref[LANES * b : LANES * (b + 1), :])
        dob_ref[:, LANES * 2 * b : LANES * (2 * b + 1)] = jnp.where(low, 0.0, pltpu.roll(x, HEAD, 1)).astype(BF)
        if 2 * b + 1 < HEADS:
            dob_ref[:, LANES * (2 * b + 1) : LANES * (2 * b + 2)] = jnp.where(low, 0.0, x).astype(BF)


def ffn_back(dh, h, new, g, meta, gu_saved, m, gain, od, gu):
    rows = h.shape[0]
    return call(
        ffn_back_kernel,
        [
            shaped(rows, D, dtype=BF),
            shaped(rows, 2 * FF, dtype=BF),
            shaped(rows, FF, dtype=BF),
            shaped(rows, D),
            shaped(rows, D, dtype=BF),
            shaped(rows, PAD_Q, dtype=BF),
            shaped(rows, LANES),
            shaped(2, D),
        ],
        [dh, h, new, g, meta, gu_saved, m, gain, od, gu],
        [VMEM] * 8 + [ANY] * 2,
        weight_scratch(od.shape[0]),
        2 * rows * (D * Q_COLS + 3 * D * FF),
        52,
    )


def attend_back_kernel(spots, size, q_ref, o_ref, dob_ref, l_ref, tj_ref, meta_ref, cos_ref, sin_ref, *refs):
    segments, refs = refs[: len(spots)], refs[len(spots) :]
    dq_ref, even_ref, odd_ref, kv_ref, dkv_ref, wide_ref, sems = refs
    rank = lax.axis_index("dp")
    half = q_ref.shape[0] // 2
    copies = kv_copies(spots, segments, kv_ref, sems, size, rank, half)
    for c in copies:
        c.start()
    blocks = tj_ref.shape[0]

    def clear(kb, _):
        for h in range(KV_HEADS):
            dkv_ref[kb, LANES * h : LANES * (h + 1), :] = jnp.zeros((LANES, KEYS), F32)
        return 0

    lax.fori_loop(0, blocks, clear, 0)
    for c in copies:
        c.wait()

    def one(a, _):
        at = pl.multiple_of(a * half, half)
        used = lax.div(chunk_of(a, rank, size) * half + half + KEYS - 1, KEYS)
        ti = jnp.concatenate([meta_ref[pl.ds(at, half), 0:1]] * GROUPED, axis=0)
        si = jnp.concatenate([meta_ref[pl.ds(at, half), 1:2]] * GROUPED, axis=0)
        logs = l_ref[a]
        for h in range(KV_HEADS):
            cols = slice(LANES * h, LANES * (h + 1))
            q3 = stack3(q_ref, at, half, h)
            do3 = stack3(dob_ref, at, half, h)
            o3 = stack3(o_ref, at, half, h)
            delta = jnp.sum(do3.astype(F32) * o3.astype(F32), axis=-1, keepdims=True)
            log3 = logs[:, h : h + 1]
            both_t = jnp.concatenate([q3.astype(F32).T, do3.astype(F32).T], axis=1).astype(BF)

            def block(kb, acc):
                keys = pl.ds(pl.multiple_of(kb * KEYS, KEYS), KEYS)
                tj = tj_ref[pl.ds(kb, 1), :]
                kv = kv_ref[keys, cols]
                s = dot_nt(q3, kv)
                p = jnp.exp(jnp.where((tj <= ti) & (tj >= si), s - log3, LOW))
                dp = dot_nt(do3, kv)
                ds = (p * (dp - delta)).astype(BF)
                both = jnp.concatenate([ds, p.astype(BF)], axis=0)
                dkv_ref[kb, cols, :] += dot(both_t, both)
                return acc + dot(ds, kv)

            acc = lax.fori_loop(0, used, block, jnp.zeros((GROUPED * half, LANES), F32))
            for g in range(GROUPED):
                wide_ref[pl.ds(at, half), LANES * (GROUPED * h + g) : LANES * (GROUPED * h + g + 1)] = acc[g * half : (g + 1) * half]
        return 0

    lax.fori_loop(0, 2, one, 0)
    lanes = lane_of((2 * half, LANES))
    low = lanes < HEAD
    cos, sin = cos_ref[...], sin_ref[...]
    for b in range(Q_COLS // LANES):
        x = wide_ref[:, LANES * 2 * b : LANES * (2 * b + 1)]
        other = pltpu.roll(wide_ref[:, LANES * (2 * b + 1) : LANES * (2 * b + 2)], HEAD, 1) if 2 * b + 1 < HEADS else 0.0
        x = jnp.where(low, x, other) * SCALE
        dq_ref[:, LANES * b : LANES * (b + 1)] = (x * cos - swap_halves(x, lanes) * sin).astype(BF)
    per = KEYS // half
    for chunk in range(2 * size):
        owner = min(chunk, 2 * size - 1 - chunk)
        side = 0 if chunk < size else 1
        m = rank ^ owner
        at = (chunk % per) * half
        for par, ref in ((0, even_ref), (1, odd_ref)):
            @pl.when(lax.rem(m, 2) == par)
            def _(ref=ref):
                ref[lax.div(m, 2), side] = dkv_ref[chunk // per, :, at : at + half].astype(BF)


def attend_back(q, o, dob, logs, tj, meta, cos, sin, segments, size):
    rows = q.shape[0]
    half = rows // 2
    total = tj.size
    spots = [s[:3] for s in segments]
    n = sum(x[2] // half for x in spots)
    pairs_n = max(size // 2, 1)
    return call(
        functools.partial(attend_back_kernel, spots, size),
        [
            shaped(rows, Q_COLS, dtype=BF),
            shaped(pairs_n, 2, KV_COLS, half, dtype=BF),
            shaped(pairs_n, 2, KV_COLS, half, dtype=BF),
        ],
        [q, o, dob, logs, tj, meta, cos, sin, *[s[3] for s in segments]],
        [VMEM] * 8 + [ANY] * len(segments),
        [
            pltpu.VMEM((total, KV_COLS), BF),
            pltpu.VMEM((total // KEYS, KV_COLS, KEYS), F32),
            pltpu.VMEM((rows, PAD_Q), F32),
            pltpu.SemaphoreType.DMA((n,)),
        ],
        10 * rows * total * HEADS * LANES // 2,
        48,
    )


def qkv_back_kernel(dq_ref, a0, b0, a1, b1, cos_ref, sin_ref, hid_ref, dh_ref, dm_ref, dz_ref, router_ref, gain_ref, w_any, *refs):
    dp_ref, new_ref, sums_ref, w_ref, sems = refs
    rows_z = D // w_any.shape[0]
    copies = load_rows(w_any, (0, rows_z), w_ref, sems, 0)
    for c in copies:
        c.start()
    rows = hid_ref.shape[0]
    half = rows // 2
    dp_ref[:, :Q_COLS] = dq_ref[...]
    lanes = lane_of((half, LANES))
    low = lanes < HEAD
    for i, (a, b) in enumerate(((a0, b0), (a1, b1))):
        at = slice(i * half, (i + 1) * half)
        cos = jnp.where(low, cos_ref[at, :], 1.0)
        sin = jnp.where(low, sin_ref[at, :], 0.0)
        for h in range(KV_HEADS):
            cols = slice(LANES * h, LANES * (h + 1))
            x = (a[cols, :].astype(F32) + b[cols, :].astype(F32)).T
            dp_ref[at, Q_COLS + LANES * h : Q_COLS + LANES * (h + 1)] = (x * cos - swap_halves(x, lanes) * sin).astype(BF)
    for c in copies:
        c.wait()
    h = hid_ref[...]
    rho = lax.rsqrt(jnp.mean(h * h, axis=-1, keepdims=True) + EPSILON)
    dn1 = dot_nt(dp_ref[...], w_ref[...])
    y = gain_ref[...] * dn1
    d_first = rho * y - h * (rho * rho * rho) * jnp.mean(y * h, axis=-1, keepdims=True)
    sums_ref[...] = jnp.sum(dn1 * h * rho, axis=0, keepdims=True)
    new_ref[...] = dh_ref[...] + dm_ref[...] + d_first + dz_ref[:, 0:1] * router_ref[...]


def qkv_back(dq, parts, cos, sin, h, dh, dm, dz, router, gain, w):
    rows = h.shape[0]
    (a0, b0), (a1, b1) = parts
    return call(
        qkv_back_kernel,
        [shaped(rows, ALL_COLS, dtype=BF), shaped(rows, D), shaped(1, D)],
        [dq, a0, b0, a1, b1, cos, sin, h, dh, dm, dz, router, gain, w],
        [VMEM] * 13 + [ANY],
        [pltpu.VMEM((D, ALL_COLS), BF), pltpu.SemaphoreType.DMA((w.shape[0],))],
        2 * rows * D * ALL_COLS,
        24,
    )


def grads_kernel(size, count, step, spare, block, lefts_n, plan, *refs):
    lefts, rights = refs[: lefts_n * STEPS], refs[lefts_n * STEPS : 2 * lefts_n * STEPS]
    refs = refs[2 * lefts_n * STEPS :]
    extra_ref, refs = (refs[0], refs[1:]) if spare else (None, refs)
    even_ref, odd_ref = refs[:2]
    left_t, right_s, pack = refs[2 : 2 + lefts_n], refs[2 + lefts_n : 2 + 2 * lefts_n], refs[2 + 2 * lefts_n]
    sems = refs[-1]
    rank = lax.axis_index("dp")
    copies = []
    for i in range(lefts_n):
        for r in range(STEPS):
            n = rights[i * STEPS + r].shape[0]
            c = pltpu.make_async_copy(rights[i * STEPS + r], right_s[i].at[pl.ds(r * n, n)], sems.at[len(copies)])
            c.start()
            copies.append(c)
    for i in range(lefts_n):
        for r in range(STEPS):
            src = lefts[i * STEPS + r]
            n = src.shape[0]
            for b in range(left_t[i].shape[0] // LANES + (1 if left_t[i].shape[0] % LANES else 0)):
                lo, hi = b * LANES, min((b + 1) * LANES, left_t[i].shape[0])
                left_t[i][lo:hi, r * n : (r + 1) * n] = src[:, lo:hi].astype(F32).T.astype(BF)
    for c in copies:
        c.wait()
    cols_total = right_s[0].shape[1]
    filled = sum(rows for _, _, rows in plan)

    def column(cb, _):
        cols = pl.ds(pl.multiple_of(cb * block, LANES), block)
        for z in range(count):
            at = 0
            for i, _, rows in plan:
                pack[at : at + rows, :] = dot(left_t[i][z * rows : (z + 1) * rows, :], right_s[i][:, cols]).astype(BF)
                at += rows
            if spare:
                pack[filled : step * size, :] = extra_ref[z, :, cols].astype(BF)
            for j in range(size):
                m = rank ^ j
                n = min(step, pack.shape[0] - j * step)
                for par, ref in ((0, even_ref), (1, odd_ref)):
                    @pl.when(lax.rem(m, 2) == par)
                    def _(ref=ref):
                        ref[lax.div(m, 2), z, :, cols] = pack[j * step : (j + 1) * step, :]
        return 0

    lax.fori_loop(0, cols_total // block, column, 0)


def grads(lefts, rights, rows_z, size, count, step, block, extra=None):
    cols = rights[0][0].shape[1]
    tokens = STEPS * lefts[0][0].shape[0]
    k = len(lefts)
    plan = [(i, i, n) for i, n in enumerate(rows_z)]
    pairs_n = max(size // 2, 1)
    args = [x for l in lefts for x in l] + [x for r in rights for x in r] + ([extra] if extra is not None else [])
    specs = [VMEM] * (k * STEPS) + [ANY] * (k * STEPS) + ([VMEM] if extra is not None else [])
    return call(
        functools.partial(grads_kernel, size, count, step, extra is not None, block, k, plan),
        [shaped(pairs_n, count, step, cols, dtype=BF)] * 2,
        args,
        specs,
        [pltpu.VMEM((n * count, tokens), BF) for n in rows_z]
        + [pltpu.VMEM((tokens, cols), BF) for _ in rows_z]
        + [pltpu.VMEM((step * size, block), BF), pltpu.SemaphoreType.DMA((k * STEPS,))],
        2 * tokens * sum(rows_z) * count * cols,
        58,
    )


def finish_kernel(rows, step, spots, splits, *refs):
    segments, outs = refs[: len(spots)], refs[len(spots) :]
    rank = lax.axis_index("dp")
    size = lax.axis_size("dp")
    edges = []
    at = 0
    for n in splits:
        edges.append((at, at + n))
        at += n
    for (m, first, n), segment in zip(spots, segments):
        for j in range(size):
            lo = j * step + first
            pieces = []
            for out, (start, stop) in zip(outs, edges):
                a, b = max(lo, start), min(lo + n, stop)
                if a < b:
                    pieces.append((out, a - start, a - lo, b - a))
            if pieces:
                @pl.when(rank == j ^ m)
                def _(pieces=pieces, segment=segment):
                    for out, to, frm, k in pieces:
                        out[to : to + k, :] = segment[frm : frm + k, :].astype(F32)


def finish(segments, splits, step):
    cols = segments[0][3].shape[1]
    spots = [s[:3] for s in segments]
    return call(
        functools.partial(finish_kernel, sum(splits), step, spots, splits),
        [shaped(n, cols) for n in splits],
        [s[3] for s in segments],
        [VMEM] * len(segments),
        [],
        0,
        32,
    )


def reduce_weight(even, odd, size, count, z):
    halves = gather_halves(even, odd, size)
    summed = jnp.concatenate([add_up(a, b).astype(BF) for a, b in halves], axis=0)
    mine = lax.dynamic_index_in_dim(summed, z, 0, keepdims=False)
    terms = [mine]
    for k in range(1, count):
        out = lax.dynamic_index_in_dim(summed, lax.rem(z + k, count), 0, keepdims=False)
        terms.append(lax.ppermute(out, "fsdp", [(i, (i + k) % count) for i in range(count)]))
    return add_up(*terms).astype(BF)


def per_device(
    tokens,
    cotangent,
    route_depth,
    lengths,
    qkv_weight,
    out_weight,
    gate_up_weight,
    down_weight,
    attn_gain,
    ffn_gain,
    router_weight,
):
    rows = tokens.shape[1]
    half = rows // 2
    size, count = lax.axis_size("dp"), lax.axis_size("fsdp")
    rank, z = lax.axis_index("dp"), lax.axis_index("fsdp")
    group_rows = rows * size
    rows_z, down_z = qkv_weight.shape[0], down_weight.shape[0]

    kv_cols = KV_HEADS * HEAD
    keys = qkv_weight[:, D : D + kv_cols].reshape(rows_z, KV_HEADS, HEAD)
    values = qkv_weight[:, D + kv_cols :].reshape(rows_z, KV_HEADS, HEAD)
    kv_packed = jnp.concatenate([keys, values], axis=2).reshape(rows_z, KV_COLS)
    step_q, step_od = slice_rows(rows_z, size), slice_rows(rows_z + down_z, size)
    spare = step_q * size - rows_z
    extra = jnp.concatenate([attn_gain[None], ffn_gain[None], router_weight.T], axis=0)
    extra = jnp.pad(extra, ((0, spare - extra.shape[0]), (0, ALL_COLS - rows_z)))
    qkv_packed = jnp.concatenate([qkv_weight[:, :D], jnp.zeros((rows_z, Q_COLS - D), BF), kv_packed], axis=1)
    qkv_full = jnp.concatenate([qkv_packed, extra], axis=0)
    od_full = jnp.concatenate(
        [out_weight, down_weight, jnp.zeros((step_od * size - rows_z - down_z, D), BF)], axis=0
    )
    gu_full = jnp.pad(gate_up_weight, ((0, spare), (0, 0)))
    w_q, w_od, w_gu = gather_weights(
        [(qkv_full, [qkv_full]), (od_full, [out_weight, down_weight]), (gu_full, [gate_up_weight])], size, count, rank
    )
    extras = w_q[:, rows_z : rows_z + 5, :rows_z].astype(F32)
    extras = jnp.transpose(extras, (1, 0, 2)).reshape(5, D)
    gain_one, gain_two = extras[0:1], extras[1:2]

    hidden = zig(tokens[0], size, rank).astype(F32)
    depth_all = lax.all_gather(route_depth[0], "dp", axis=0, tiled=True)
    index = jnp.arange(group_rows, dtype=jnp.int32)
    lengths_here = lengths[0]
    ends = [jnp.sum(lengths_here[: i + 1]) for i in range(lengths_here.shape[0])]
    start = functools.reduce(jnp.add, [jnp.where(index >= e, lengths_here[i], 0) for i, e in enumerate(ends)])
    mine = lambda x: jnp.concatenate(
        [
            lax.dynamic_slice_in_dim(x, rank * half, half),
            lax.dynamic_slice_in_dim(x, (2 * size - 1 - rank) * half, half),
        ]
    )
    index_here, start_here, depth_here = mine(index), mine(start), mine(depth_all)
    tj = [jnp.where(depth_all > r, index, FAR).reshape(group_rows // KEYS, KEYS) for r in range(STEPS)]
    zeros = jnp.zeros_like(index_here)
    meta = [
        jnp.stack([index_here, start_here, (depth_here > r).astype(jnp.int32)] + [zeros] * 5, axis=1) for r in range(STEPS)
    ]
    frequency = jnp.exp(jnp.arange(HEAD // 2, dtype=F32) * (-2.0 * math.log(10000.0) / HEAD))
    angles = (index_here - start_here).astype(F32)[:, None] * frequency[None, :]
    cos, sin = jnp.cos(angles), jnp.sin(angles)
    cos = jnp.concatenate([cos] * 4, axis=1)
    sin = jnp.concatenate([-sin, sin, -sin, sin], axis=1)

    saved = []
    for r in range(STEPS):
        n1, q, kv = norm_qkv(hidden, gain_one, cos, sin, w_q)
        segments = spread(kv, 0, half, size)
        o, logs = attend(q, segments, tj[r], meta[r], size)
        ob, m, n2, gu_saved, g, new = post(o, hidden, gain_two, extras[2 + r : 3 + r], meta[r], w_od, w_gu)
        saved.append((hidden, n1, q, segments, o, logs, ob, m, n2, gu_saved, g, new))
        hidden = new
    hidden_out = unzig(hidden.astype(BF), size, rank).astype(F32)

    dh = zig(cotangent[0], size, rank).astype(F32)
    kept = [None] * STEPS
    gains_one, gains_two, routers = [], [], [None] * STEPS
    for r in reversed(range(STEPS)):
        hidden, n1, q, segments, o, logs, ob, m, n2, gu_saved, g, new = saved[r]
        dfb, dgu, inner, dm, datt, dob, dz, sums = ffn_back(dh, hidden, new, g, meta[r], gu_saved, m, gain_two, w_od, w_gu)
        routers[r] = sums[0]
        gains_two.append(sums[1])
        if r == 0:
            mid = kept[1:]
            gu_parts = grads(
                [[n2] + [k["n2"] for k in mid]], [[dgu] + [k["dgu"] for k in mid]], [rows_z], size, count, step_q, 640
            )
            od_parts = grads(
                [[ob] + [k["ob"] for k in mid], [inner] + [k["inner"] for k in mid]],
                [[datt] + [k["datt"] for k in mid], [dfb] + [k["dfb"] for k in mid]],
                [rows_z, down_z],
                size,
                count,
                step_od,
                D,
            )
        dq, even, odd = attend_back(q, o, dob, logs, tj[r], meta[r], cos, sin, segments, size)
        parts = gather_halves(even, odd, size)
        parts = [tuple(x.reshape(KV_COLS, half) for x in p) for p in parts]
        dp, dh, gain_sum = qkv_back(dq, parts, cos, sin, hidden, dh, dm, dz, extras[2 + r : 3 + r], gain_one, w_q)
        gains_one.append(gain_sum[0])
        kept[r] = dict(n1=n1, n2=n2, ob=ob, dgu=dgu, inner=inner, dfb=dfb, datt=datt, dp=dp)
    input_grad = unzig(dh.astype(BF), size, rank).astype(F32)

    small = jnp.stack([sum(gains_one), sum(gains_two), *routers], axis=0)
    small = jnp.transpose(small.reshape(5, count, rows_z), (1, 0, 2))
    small = jnp.pad(small, ((0, 0), (0, spare - 5), (0, ALL_COLS - rows_z)))
    q_parts = grads([[k["n1"] for k in kept]], [[k["dp"] for k in kept]], [rows_z], size, count, step_q, ALL_COLS // 13, small)

    results = []
    for (even, odd), step, splits in (
        (gu_parts, step_q, [rows_z]),
        (od_parts, step_od, [rows_z, down_z]),
        (q_parts, step_q, [rows_z, spare]),
    ):
        mine_sum = reduce_weight(even, odd, size, count, z)
        results.append(finish(spread(mine_sum, 0, split_at(step), size), splits, step))
    (gate_up_grad,), (out_grad, down_grad), (qkv_packed, small) = results
    kv = qkv_packed[:, Q_COLS:].reshape(rows_z, KV_HEADS, 2, HEAD)
    qkv_grad = jnp.concatenate(
        [qkv_packed[:, :D], kv[:, :, 0].reshape(rows_z, kv_cols), kv[:, :, 1].reshape(rows_z, kv_cols)], axis=1
    )
    small = small[:5, :rows_z]
    return (
        hidden_out[None],
        input_grad[None],
        qkv_grad,
        out_grad,
        gate_up_grad,
        down_grad,
        small[0],
        small[1],
        small[2:5].T,
    )


def solution(mesh):
    placed = (
        P("fsdp", "dp", None),
        P("fsdp", "dp", None),
        P("fsdp", "dp"),
        P("fsdp", None),
        P("fsdp", None),
        P("fsdp", None),
        P("fsdp", None),
        P("fsdp", None),
        P("fsdp"),
        P("fsdp"),
        P("fsdp", None),
    )
    return jax.shard_map(
        per_device,
        mesh=mesh,
        in_specs=placed,
        out_specs=(
            P("fsdp", "dp", None),
            P("fsdp", "dp", None),
            P("fsdp", None),
            P("fsdp", None),
            P("fsdp", None),
            P("fsdp", None),
            P("fsdp"),
            P("fsdp"),
            P("fsdp", None),
        ),
        check_vma=False,
    )
```

time: 1660 us -> 880 us (0.53)
  waiting for transfers between devices: 811 us -> 219 us
  matrix products: 385 us -> 0 us
  Pallas kernels: 0 us -> 317 us
  starting transfers between devices: 1.94 us -> 136 us
  other arithmetic: 136 us -> 43.3 us
  loops' own time: 72.8 us -> 0 us
  blocking collectives: 55.9 us -> 8.62 us
  local copies, waits for them, and re-layouts: 174 us -> 141 us
    dot_general x126 -> x0, matrix products: 385 us -> none  [the longest x12 52.8 us: block_scores(): jnp.einsum('qkgh,nkh->kgqn', grouped, keys_part, preferred_element_type=j...]
    reduce_scatter x6 -> x0, waiting for transfers between devices: 364 us -> none  [the longest x1 170 us: per_device(): lax.psum_scatter(gate_total.astype(jnp.bfloat16), 'fsdp', scatter_dimensi...]
    all_gather x7 -> x0, waiting for transfers between devices: 317 us -> none  [the longest x1 123 us: per_device(): lax.all_gather(gate_up_weight, 'fsdp', axis=0, tiled=True)]
    pallas_call x0 -> x27, Pallas kernels: none -> 317 us  [call(): pl.pallas_call(kernel, out_shape=outs, in_specs=specs, out_specs=out_spec...]
    ppermute x0 -> x137, waiting for transfers between devices: none -> 219 us  [the longest x36 73.9 us: gather_weights(): lax.ppermute(a, axis, perm)]
    ppermute x0 -> x137, starting transfers between devices: none -> 136 us  [the longest x36 37.9 us: gather_weights(): lax.ppermute(a, axis, perm)]
    another operation x9 -> x0, loops' own time: 72.8 us -> none  [the longest x3 24.7 us: per_device(): lax.scan(key_step, jnp.zeros((rows_dev, KV_HEADS, per_kv, HEAD), jnp.floa...]
    unnamed x18 -> x0, waiting for transfers between devices: 67.9 us -> none
  transfers between devices with their start and end apart: 16 -> 137, of which waited for: 15 -> 40; matrix products, arithmetic and copies ran while one was open for 12% -> 12% of each run, Pallas kernels for 0% -> 12%
where the time goes in v2:
time: 880 us; the launch traced here: 868 us
  Pallas kernels  317 us (36%)
  waiting for transfers between devices  219 us (25%)
  local copies, waits for them, and re-layouts  141 us (16%)
  starting transfers between devices  136 us (15%)
  other arithmetic  43.3 us (5%)
    pallas_call x27, Pallas kernels, call(): pl.pallas_call(kernel, out_shape=outs, in_specs=specs, out_specs=out_spec...  317 us
    unnamed x402, local copies, waits for them, and re-layouts  85 us
    ppermute x36, waiting for transfers between devices, gather_weights(): lax.ppermute(a, axis, perm)  73.9 us
    ppermute x6, waiting for transfers between devices, gather_halves(): last_x = lax.ppermute(next_x, 'dp', pairs(size, 2))  54.9 us
    ppermute x36, starting transfers between devices, gather_weights(): lax.ppermute(a, axis, perm)  37.9 us
    ppermute x6, waiting for transfers between devices, gather_halves(): got_x = lax.ppermute(send_x, 'dp', pairs(size, 2))  22.1 us
    ppermute x9, starting transfers between devices, reduce_weight(): lax.ppermute(out, 'fsdp', [(i, (i + k) % count) for i in range(count)])  21.8 us
    ppermute x12, waiting for transfers between devices, spread(): got[b, 0] = (rows, lax.ppermute(piece, 'dp', pairs(size, b)))  21.2 us
  transfers between devices with their start and end apart: 137, of which 40 were waited for; matrix products, arithmetic and copies ran while one was open for 12% of the time, Pallas kernels for 12%

profile of v2, /device:TPU:0, one launch (start us, length us, event | category | flops | bytes accessed | tf_op | source)
XLA Modules:
  0.0 867.6 jit_solution(8377853015908030757)
XLA Ops:
  29.7 8.1 collective-permute-done.8
  68.2 13.8 %collective-permute-done.18 = bf16[32,5120]{1,0:T(8,128)(2,1)S(1)} collective-permute-done((bf16[32,5120]{1,0:T(8,128)(2,1)}, bf16[32,5120]{1,0:T(8,128)(2,1)S(1)}, u32[]{:S(2)}, u32[]{:S(2)}) %collective-permute-start.18) | collective-permute-done | bytes 327712 | tf_op jit(solution)/shard_map/ppermute | solution.py:266
  94.4 24.3 %collective-permute-done.23.refs_6_ = bf16[3,48,960]{2,1,0:T(8,128)(2,1)} collective-permute-done((bf16[3,48,960]{2,1,0:T(8,128)(2,1)S(1)}, bf16[3,48,960]{2,1,0:T(8,128)(2,1)}, u32[]{:S(2)}, u32[]{:S(2)}) %collective-permute-start.23) | collective-permute-done | bytes 276512 | tf_op jit(solution)/shard_map/ppermute | solution.py:266
  139.6 7.6 collective-permute-done.29.refs_1_
  150.3 10.6 %collective-permute-done.40.refs_4_ = bf16[3,16,5120]{2,1,0:T(8,128)(2,1)} collective-permute-done((bf16[3,16,5120]{2,1,0:T(8,128)(2,1)S(1)}, bf16[3,16,5120]{2,1,0:T(8,128)(2,1)}, u32[]{:S(2)}, u32[]{:S(2)}) %collective-permute-start.40) | collective-permute-done | bytes 491552 | tf_op jit(solution)/shard_map/ppermute | solution.py:266
  161.0 8.6 all-gather
  189.6 18.8 %shard_map.180 = (bf16[256,1920]{1,0:T(8,128)(2,1)S(1)}, f32[2,384,128]{2,1,0:T(8,128)S(1)}) custom-call(bf16[256,1920]{1,0:T(8,128)(2,1)S(1)} %copy-done.135, s32[4,512]{1,0:T(4,128)S(1)} %copy-done.123, s32[256,8]{1,0:T(8,128)S(1)} %copy-done.43, bf16[256,640]{1,0:T(8,128)(2,1)} %get-tuple-element.208.refs_0_, ...), custom_call_target="tpu_custom_call" | custom-call | flops 2013265920 | bytes 4997120 | tf_op jit(solution)/shard_map/pallas_call | solution.py:52
  226.5 8.1 shard_map.183
  244.1 8.2 collective-permute-done.47.refs_1_
  268.3 18.7 %shard_map.185 = (bf16[256,1920]{1,0:T(8,128)(2,1)S(1)}, f32[2,384,128]{2,1,0:T(8,128)S(1)}) custom-call(bf16[256,1920]{1,0:T(8,128)(2,1)S(1)} %copy-done.138, s32[4,512]{1,0:T(4,128)S(1)} %copy-done.125, s32[256,8]{1,0:T(8,128)S(1)} %copy-done.46, bf16[256,640]{1,0:T(8,128)(2,1)} %get-tuple-element.237.refs_0_, ...), custom_call_target="tpu_custom_call" | custom-call | flops 2013265920 | bytes 4997120 | tf_op jit(solution)/shard_map/pallas_call | solution.py:52
  287.8 8.5 shard_map.186
  332.9 18.9 %shard_map.188 = (bf16[256,1920]{1,0:T(8,128)(2,1)S(1)}, f32[2,384,128]{2,1,0:T(8,128)S(1)}) custom-call(bf16[256,1920]{1,0:T(8,128)(2,1)S(1)} %copy-done.141, s32[4,512]{1,0:T(4,128)S(1)} %copy-done.127, s32[256,8]{1,0:T(8,128)S(1)} %copy-done.48, bf16[256,640]{1,0:T(8,128)(2,1)} %get-tuple-element.241.refs_0_, ...), custom_call_target="tpu_custom_call" | custom-call | flops 2013265920 | bytes 4997120 | tf_op jit(solution)/shard_map/pallas_call | solution.py:52
  351.8 8.1 shard_map.189
  363.5 14.8 %shard_map.190 = (bf16[256,960]{1,0:T(8,128)(2,1)S(1)}, bf16[256,5120]{1,0:T(8,128)(2,1)}, bf16[256,2560]{1,0:T(8,128)(2,1)}, f32[256,960]{1,0:T(8,128)}, bf16[2...) custom-call(f32[256,960]{1,0:T(8,128)} %maximum_convert_fusion.2.dh_ref, ...), custom_call_target="tpu_custom_call" | custom-call | flops 4278190080 | bytes 31083776 | tf_op jit(solution)/shard_map/pallas_call | solution.py:52
  379.0 28.4 %shard_map.191 = (bf16[256,1024]{1,0:T(8,128)(2,1)S(1)}, bf16[4,2,640,128]{3,2,1,0:T(8,128)(2,1)}, bf16[4,2,640,128]{3,2,1,0:T(8,128)(2,1)}) custom-call(bf16[256,1920]{1,0:T(8,128)(2,1)S(1)} %copy-done.142, bf16[256,1920]{1,0:T(8,128)(2,1)S(1)} %get-tuple-element.242.o_ref, bf16[256,1920]{1,0:T(8,128)(2,1)} %get-tuple-element.247.dob_ref, ...), custom_call_target="tpu_custom_call" | custom-call | flops 5033164800 | bytes 9388032 | tf_op jit(solution)/shard_map/pallas_call | solution.py:52
  414.2 8.2 collective-permute-done.70
  434.8 14.8 %shard_map.193 = (bf16[256,960]{1,0:T(8,128)(2,1)S(1)}, bf16[256,5120]{1,0:T(8,128)(2,1)}, bf16[256,2560]{1,0:T(8,128)(2,1)}, f32[256,960]{1,0:T(8,128)}, bf16[2...) custom-call(f32[256,960]{1,0:T(8,128)} %copy-done.23, ...), custom_call_target="tpu_custom_call" | custom-call | flops 4278190080 | bytes 31083776 | tf_op jit(solution)/shard_map/pallas_call | solution.py:52
  450.4 28.6 %shard_map.194 = (bf16[256,1024]{1,0:T(8,128)(2,1)S(1)}, bf16[4,2,640,128]{3,2,1,0:T(8,128)(2,1)}, bf16[4,2,640,128]{3,2,1,0:T(8,128)(2,1)}) custom-call(bf16[256,1920]{1,0:T(8,128)(2,1)S(1)} %copy-done.139, bf16[256,1920]{1,0:T(8,128)(2,1)S(1)} %copy-done.61, bf16[256,1920]{1,0:T(8,128)(2,1)} %get-tuple-element.258.dob_ref, f32[2,384,128]{2,1,0:T(8,128)S(1)} %copy-done.164, ...), custom_call_target="tpu_custom_call" | custom-call | flops 5033164800 | bytes 9388032 | tf_op jit(solution)/shard_map/pallas_call | solution.py:52
  486.5 7.2 collective-permute-done.75
  506.8 14.8 %shard_map.196 = (bf16[256,960]{1,0:T(8,128)(2,1)S(1)}, bf16[256,5120]{1,0:T(8,128)(2,1)}, bf16[256,2560]{1,0:T(8,128)(2,1)}, f32[256,960]{1,0:T(8,128)}, bf16[2...) custom-call(f32[256,960]{1,0:T(8,128)} %copy-done.21, ...), custom_call_target="tpu_custom_call" | custom-call | flops 4278190080 | bytes 31083776 | tf_op jit(solution)/shard_map/pallas_call | solution.py:52
  522.3 28.5 %shard_map.197 = (bf16[256,1024]{1,0:T(8,128)(2,1)S(1)}, bf16[4,2,640,128]{3,2,1,0:T(8,128)(2,1)}, bf16[4,2,640,128]{3,2,1,0:T(8,128)(2,1)}) custom-call(bf16[256,1920]{1,0:T(8,128)(2,1)S(1)} %copy-done.136, bf16[256,1920]{1,0:T(8,128)(2,1)S(1)} %copy-done.59, bf16[256,1920]{1,0:T(8,128)(2,1)} %get-tuple-element.269.dob_ref, f32[2,384,128]{2,1,0:T(8,128)S(1)} %copy-done.162, ...), custom_call_target="tpu_custom_call" | custom-call | flops 5033164800 | bytes 9388032 | tf_op jit(solution)/shard_map/pallas_call | solution.py:52
  551.0 28.7 %shard_map.203 = (bf16[4,4,32,5120]{3,2,1,0:T(8,128)(2,1)}, bf16[4,4,32,5120]{3,2,1,0:T(8,128)(2,1)}) custom-call(bf16[256,960]{1,0:T(8,128)(2,1)} %copy-done.150, bf16[256,960]{1,0:T(8,128)(2,1)} %copy-done.152, bf16[256,960]{1,0:T(8,128)(2,1)} %copy-done.156, bf16[256,5120]{1,0:T(8,128)(2,1)} %get-tuple-element.310.refs_3_, ...), custom_call_target="tpu_custom_call" | custom-call | flops 7549747200 | bytes 19824640 | tf_op jit(solution)/shard_map/pallas_call | solution.py:52
  584.0 14.6 %shard_map.201 = (bf16[4,4,112,960]{3,2,1,0:T(8,128)(2,1)}, bf16[4,4,112,960]{3,2,1,0:T(8,128)(2,1)}) custom-call(bf16[256,1024]{1,0:T(8,128)(2,1)} %copy-done.149, bf16[256,1024]{1,0:T(8,128)(2,1)} %copy-done.151, bf16[256,1024]{1,0:T(8,128)(2,1)} %copy-done.153, bf16[256,2560]{1,0:T(8,128)(2,1)} %get-tuple-element.295.refs_3_, ...), custom_call_target="tpu_custom_call" | custom-call | flops 5190451200 | bytes 15335424 | tf_op jit(solution)/shard_map/pallas_call | solution.py:52
  623.7 24.5 %shard_map.199 = (bf16[4,4,32,1664]{3,2,1,0:T(8,128)(2,1)}, bf16[4,4,32,1664]{3,2,1,0:T(8,128)(2,1)}) custom-call(bf16[256,960]{1,0:T(8,128)(2,1)} %copy-done.146, bf16[256,960]{1,0:T(8,128)(2,1)} %copy-done.147, bf16[256,960]{1,0:T(8,128)(2,1)} %copy-done.148, bf16[256,1664]{1,0:T(8,128)(2,1)} %copy-done.145, bf16[256,1664]{1,0:T(8,128)(2,1)} %copy-done.144, ...), custom_call_target="tpu_custom_call" | custom-call | flops 2453667840 | bytes 7864320 | tf_op jit(solution)/shard_map/pallas_call | solution.py:52
  659.7 6.7 collective-permute-done.87
  675.4 42.5 %collective-permute-done.90 = bf16[2,32,1664]{2,1,0:T(8,128)(2,1)S(1)} collective-permute-done((bf16[2,32,1664]{2,1,0:T(8,128)(2,1)S(1)}, bf16[2,32,1664]{2,1,0:T(8,128)(2,1)S(1)}, u32[]{:S(2)}, u32[]{:S(2)}) %collective-permute-start.90) | collective-permute-done | bytes 213024 | tf_op jit(solution)/shard_map/ppermute | solution.py:130
  719.0 5.5 collective-permute-start.91
  739.8 5.6 collective-permute-done.105
  751.6 5.9 collective-permute-done.122
  757.8 5.6 collective-permute-done.124
  778.4 12.5 %collective-permute-done.109 = bf16[112,960]{1,0:T(8,128)(2,1)S(1)} collective-permute-done((bf16[112,960]{1,0:T(8,128)(2,1)S(1)}, bf16[112,960]{1,0:T(8,128)(2,1)S(1)}, u32[]{:S(2)}, u32[]{:S(2)}) %collective-permute-start.109) | collective-permute-done | bytes 215072 | tf_op jit(solution)/shard_map/ppermute | solution.py:869
  801.0 6.1 collective-permute-start.97
  (808 shorter events, 398.4 us)
Async XLA Ops:
  39.1 44.5 %collective-permute-start.15 = (bf16[3,112,960]{2,1,0:T(8,128)(2,1)S(1)}, bf16[3,112,960]{2,1,0:T(8,128)(2,1)S(1)}, u32[]{:S(2)}, u32[]{:S(2)}) collective-permute-start(bf16[3,112,960]{2,1,0:T(8,128)(2,1)S(1)} %pad_maximum_fusion.6.refs_2_), channel_id=1, source_target_pairs={{0,8},{4,12},{8,0},{12,4},{16,24},{20,28},{24,16},{28,20},{1,9},{5... | collective-permute-start | bytes 1935368 | tf_op jit(solution)/shard_map/ppermute | solution.py:266
  40.6 43.0 %collective-permute-start.16 = (bf16[3,112,960]{2,1,0:T(8,128)(2,1)S(1)}, bf16[3,112,960]{2,1,0:T(8,128)(2,1)S(1)}, u32[]{:S(2)}, u32[]{:S(2)}) collective-permute-start(bf16[3,112,960]{2,1,0:T(8,128)(2,1)S(1)} %pad_maximum_fusion.6.refs_2_), channel_id=1, source_target_pairs={{0,16},{4,20},{8,24},{12,28},{16,0},{20,4},{24,8},{28,12},{1,17},{... | collective-permute-start | bytes 1935368 | tf_op jit(solution)/shard_map/ppermute | solution.py:266
  58.1 23.9 %collective-permute-start.18 = (bf16[32,5120]{1,0:T(8,128)(2,1)}, bf16[32,5120]{1,0:T(8,128)(2,1)S(1)}, u32[]{:S(2)}, u32[]{:S(2)}) collective-permute-start(bf16[32,5120]{1,0:T(8,128)(2,1)} %pad_dynamic-slice_fusion), channel_id=1, source_target_pairs={{0,2},{1,3},{2,0},{3,1},{4,6},{5,7},{6,4},{7,5},{8,10},{9,11},{10,... | collective-permute-start | bytes 983048 | tf_op jit(solution)/shard_map/ppermute | solution.py:266
  59.8 23.8 %collective-permute-start.19 = (bf16[32,5120]{1,0:T(8,128)(2,1)}, bf16[32,5120]{1,0:T(8,128)(2,1)S(1)}, u32[]{:S(2)}, u32[]{:S(2)}) collective-permute-start(bf16[32,5120]{1,0:T(8,128)(2,1)} %pad_dynamic-slice_fusion), channel_id=1, source_target_pairs={{0,3},{1,0},{2,1},{3,2},{4,7},{5,4},{6,5},{7,6},{8,11},{9,8},{10,9... | collective-permute-start | bytes 983048 | tf_op jit(solution)/shard_map/ppermute | solution.py:266
  86.3 32.4 %collective-permute-start.22 = (bf16[3,64,960]{2,1,0:T(8,128)(2,1)S(1)}, bf16[3,64,960]{2,1,0:T(8,128)(2,1)}, u32[]{:S(2)}, u32[]{:S(2)}) collective-permute-start(bf16[3,64,960]{2,1,0:T(8,128)(2,1)S(1)} %slice.564), channel_id=1, source_target_pairs={{0,16},{4,20},{8,24},{12,28},{16,0},{20,4},{24,8},{28,12},{1,17},{... | collective-permute-start | bytes 1105928 | tf_op jit(solution)/shard_map/ppermute | solution.py:266
  87.1 35.6 %collective-permute-start.27 = (bf16[3,32,5120]{2,1,0:T(8,128)(2,1)S(1)}, bf16[3,32,5120]{2,1,0:T(8,128)(2,1)S(1)}, u32[]{:S(2)}, u32[]{:S(2)}) collective-permute-start(bf16[3,32,5120]{2,1,0:T(8,128)(2,1)S(1)} %pad_maximum_fusion.3.refs_1_), channel_id=1, source_target_pairs={{0,8},{4,12},{8,0},{12,4},{16,24},{20,28},{24,16},{28,20},{1,9},{5... | collective-permute-start | bytes 2949128 | tf_op jit(solution)/shard_map/ppermute | solution.py:266
  88.8 33.9 %collective-permute-start.28 = (bf16[3,32,5120]{2,1,0:T(8,128)(2,1)S(1)}, bf16[3,32,5120]{2,1,0:T(8,128)(2,1)}, u32[]{:S(2)}, u32[]{:S(2)}) collective-permute-start(bf16[3,32,5120]{2,1,0:T(8,128)(2,1)S(1)} %pad_maximum_fusion.3.refs_1_), channel_id=1, source_target_pairs={{0,16},{4,20},{8,24},{12,28},{16,0},{20,4},{24,8},{28,12},{1,17},{... | collective-permute-start | bytes 2949128 | tf_op jit(solution)/shard_map/ppermute | solution.py:266
  90.5 28.2 %collective-permute-start.23 = (bf16[3,48,960]{2,1,0:T(8,128)(2,1)S(1)}, bf16[3,48,960]{2,1,0:T(8,128)(2,1)}, u32[]{:S(2)}, u32[]{:S(2)}) collective-permute-start(bf16[3,48,960]{2,1,0:T(8,128)(2,1)S(1)} %slice.565), channel_id=1, source_target_pairs={{0,8},{4,12},{8,0},{12,4},{16,24},{20,28},{24,16},{28,20},{1,9},{5... | collective-permute-start | bytes 829448 | tf_op jit(solution)/shard_map/ppermute | solution.py:266
  94.2 28.4 %collective-permute-start.24 = (bf16[3,112,960]{2,1,0:T(8,128)(2,1)S(1)}, bf16[3,112,960]{2,1,0:T(8,128)(2,1)}, u32[]{:S(2)}, u32[]{:S(2)}) collective-permute-start(bf16[3,112,960]{2,1,0:T(8,128)(2,1)S(1)} %pad_maximum_fusion.6.refs_2_), channel_id=1, source_target_pairs={{0,4},{4,0},{8,12},{12,8},{16,20},{20,16},{24,28},{28,24},{1,5},{5... | collective-permute-start | bytes 1935368 | tf_op jit(solution)/shard_map/ppermute | solution.py:266
  137.2 35.0 %collective-permute-start.42 = (bf16[3,32,5120]{2,1,0:T(8,128)(2,1)S(1)}, bf16[3,32,5120]{2,1,0:T(8,128)(2,1)S(1)}, u32[]{:S(2)}, u32[]{:S(2)}) collective-permute-start(bf16[3,32,5120]{2,1,0:T(8,128)(2,1)S(1)} %copy-done.28), channel_id=1, source_target_pairs={{0,4},{4,0},{8,12},{12,8},{16,20},{20,16},{24,28},{28,24},{1,5},{5... | collective-permute-start | bytes 2949128 | tf_op jit(solution)/shard_map/ppermute | solution.py:266
  139.1 35.7 %collective-permute-start.43 = (bf16[3,32,5120]{2,1,0:T(8,128)(2,1)S(1)}, bf16[3,32,5120]{2,1,0:T(8,128)(2,1)S(1)}, u32[]{:S(2)}, u32[]{:S(2)}) collective-permute-start(bf16[3,32,5120]{2,1,0:T(8,128)(2,1)S(1)} %copy-done.33), channel_id=1, source_target_pairs={{0,4},{4,0},{8,12},{12,8},{16,20},{20,16},{24,28},{28,24},{1,5},{5... | collective-permute-start | bytes 2949128 | tf_op jit(solution)/shard_map/ppermute | solution.py:266
  147.2 33.5 %collective-permute-start.44 = (bf16[3,32,5120]{2,1,0:T(8,128)(2,1)}, bf16[3,32,5120]{2,1,0:T(8,128)(2,1)}, u32[]{:S(2)}, u32[]{:S(2)}) collective-permute-start(bf16[3,32,5120]{2,1,0:T(8,128)(2,1)} %collective-permute-done.28.refs_3_), channel_id=1, source_target_pairs={{0,4},{4,0},{8,12},{12,8},{16,20},{20,16},{24,28},{28,24},{1,5},{5... | collective-permute-start | bytes 2949128 | tf_op jit(solution)/shard_map/ppermute | solution.py:266
  180.9 37.6 %collective-permute-start.45 = (bf16[3,16,5120]{2,1,0:T(8,128)(2,1)}, bf16[3,16,5120]{2,1,0:T(8,128)(2,1)}, u32[]{:S(2)}, u32[]{:S(2)}) collective-permute-start(bf16[3,16,5120]{2,1,0:T(8,128)(2,1)} %collective-permute-done.40.refs_4_), channel_id=1, source_target_pairs={{0,4},{4,0},{8,12},{12,8},{16,20},{20,16},{24,28},{28,24},{1,5},{5... | collective-permute-start | bytes 1474568 | tf_op jit(solution)/shard_map/ppermute | solution.py:266
  181.2 37.3 %collective-permute-start.46 = (bf16[3,16,5120]{2,1,0:T(8,128)(2,1)}, bf16[3,16,5120]{2,1,0:T(8,128)(2,1)}, u32[]{:S(2)}, u32[]{:S(2)}) collective-permute-start(bf16[3,16,5120]{2,1,0:T(8,128)(2,1)} %copy-done.76), channel_id=1, source_target_pairs={{0,4},{4,0},{8,12},{12,8},{16,20},{20,16},{24,28},{28,24},{1,5},{5... | collective-permute-start | bytes 1474568 | tf_op jit(solution)/shard_map/ppermute | solution.py:266
  550.9 29.3 %collective-permute-start.79 = (bf16[4,2,640,128]{3,2,1,0:T(8,128)(2,1)}, bf16[4,2,640,128]{3,2,1,0:T(8,128)(2,1)}, u32[]{:S(2)}, u32[]{:S(2)}) collective-permute-start(bf16[4,2,640,128]{3,2,1,0:T(8,128)(2,1)} %get-tuple-element.273), channel_id=1, source_target_pairs={{0,4},{4,0},{8,12},{12,8},{16,20},{20,16},{24,28},{28,24},{1,5},{5... | collective-permute-start | bytes 3932168 | tf_op jit(solution)/shard_map/ppermute | solution.py:115
  579.7 88.4 %collective-permute-start.120 = (bf16[4,4,32,5120]{3,2,1,0:T(8,128)(2,1)}, bf16[4,4,32,5120]{3,2,1,0:T(8,128)(2,1)}, u32[]{:S(2)}, u32[]{:S(2)}) collective-permute-start(bf16[4,4,32,5120]{3,2,1,0:T(8,128)(2,1)} %get-tuple-element.314), channel_id=1, source_target_pairs={{0,4},{4,0},{8,12},{12,8},{16,20},{20,16},{24,28},{28,24},{1,5},{5... | collective-permute-start | bytes 15728648 | tf_op jit(solution)/shard_map/ppermute | solution.py:115
  598.6 57.6 %collective-permute-start.103 = (bf16[4,4,112,960]{3,2,1,0:T(8,128)(2,1)}, bf16[4,4,112,960]{3,2,1,0:T(8,128)(2,1)}, u32[]{:S(2)}, u32[]{:S(2)}) collective-permute-start(bf16[4,4,112,960]{3,2,1,0:T(8,128)(2,1)} %get-tuple-element.305), channel_id=1, source_target_pairs={{0,4},{4,0},{8,12},{12,8},{16,20},{20,16},{24,28},{28,24},{1,5},{5... | collective-permute-start | bytes 10321928 | tf_op jit(solution)/shard_map/ppermute | solution.py:115
  659.0 60.1 %collective-permute-start.104 = (bf16[2,2,112,960]{3,2,1,0:T(8,128)(2,1)S(1)}, bf16[2,2,112,960]{3,2,1,0:T(8,128)(2,1)S(1)}, u32[]{:S(2)}, u32[]{:S(2)}) collective-permute-start(bf16[2,2,112,960]{3,2,1,0:T(8,128)(2,1)S(1)} %pad_maximum_fusion.4), channel_id=1, source_target_pairs={{0,8},{4,12},{8,0},{12,4},{16,24},{20,28},{24,16},{28,20},{1,9},{5... | collective-permute-start | bytes 2580488 | tf_op jit(solution)/shard_map/ppermute | solution.py:125
  670.8 58.7 %collective-permute-start.121 = (bf16[2,2,32,5120]{3,2,1,0:T(8,128)(2,1)S(1)}, bf16[2,2,32,5120]{3,2,1,0:T(8,128)(2,1)S(1)}, u32[]{:S(2)}, u32[]{:S(2)}) collective-permute-start(bf16[2,2,32,5120]{3,2,1,0:T(8,128)(2,1)S(1)} %pad_maximum_fusion), channel_id=1, source_target_pairs={{0,8},{4,12},{8,0},{12,4},{16,24},{20,28},{24,16},{28,20},{1,9},{5... | collective-permute-start | bytes 3932168 | tf_op jit(solution)/shard_map/ppermute | solution.py:125
  672.0 59.2 %collective-permute-start.123 = (bf16[2,2,32,5120]{3,2,1,0:T(8,128)(2,1)S(1)}, bf16[2,2,32,5120]{3,2,1,0:T(8,128)(2,1)S(1)}, u32[]{:S(2)}, u32[]{:S(2)}) collective-permute-start(bf16[2,2,32,5120]{3,2,1,0:T(8,128)(2,1)S(1)} %pad_maximum_fusion.1), channel_id=1, source_target_pairs={{0,16},{4,20},{8,24},{12,28},{16,0},{20,4},{24,8},{28,12},{1,17},{... | collective-permute-start | bytes 3932168 | tf_op jit(solution)/shard_map/ppermute | solution.py:126
  673.5 51.0 %collective-permute-start.106 = (bf16[2,2,112,960]{3,2,1,0:T(8,128)(2,1)S(1)}, bf16[2,2,112,960]{3,2,1,0:T(8,128)(2,1)S(1)}, u32[]{:S(2)}, u32[]{:S(2)}) collective-permute-start(bf16[2,2,112,960]{3,2,1,0:T(8,128)(2,1)S(1)} %pad_maximum_fusion.5), channel_id=1, source_target_pairs={{0,16},{4,20},{8,24},{12,28},{16,0},{20,4},{24,8},{28,12},{1,17},{... | collective-permute-start | bytes 2580488 | tf_op jit(solution)/shard_map/ppermute | solution.py:126
  674.3 43.7 %collective-permute-start.90 = (bf16[2,32,1664]{2,1,0:T(8,128)(2,1)S(1)}, bf16[2,32,1664]{2,1,0:T(8,128)(2,1)S(1)}, u32[]{:S(2)}, u32[]{:S(2)}) collective-permute-start(bf16[2,32,1664]{2,1,0:T(8,128)(2,1)S(1)} %get-tuple-element.383), channel_id=1, source_target_pairs={{0,8},{4,12},{8,0},{12,4},{16,24},{20,28},{24,16},{28,20},{1,9},{5... | collective-permute-start | bytes 638984 | tf_op jit(solution)/shard_map/ppermute | solution.py:130
  717.9 50.2 %collective-permute-start.65 = (bf16[128,960]{1,0:T(8,128)(2,1)S(1)}, bf16[128,960]{1,0:T(8,128)(2,1)S(1)}, u32[]{:S(2)}, u32[]{:S(2)}) collective-permute-start(bf16[128,960]{1,0:T(8,128)(2,1)S(1)} %get-tuple-element.433), channel_id=1, source_target_pairs={{0,0},{8,4},{16,8},{24,12},{28,16},{20,20},{12,24},{4,28},{1,1},{9... | collective-permute-start | bytes 737288 | tf_op jit(solution)/shard_map/ppermute | solution.py:167
  737.5 26.0 %collective-permute-start.124 = (bf16[2,32,5120]{2,1,0:T(8,128)(2,1)S(1)}, bf16[2,32,5120]{2,1,0:T(8,128)(2,1)S(1)}, u32[]{:S(2)}, u32[]{:S(2)}) collective-permute-start(bf16[2,32,5120]{2,1,0:T(8,128)(2,1)S(1)} %get-tuple-element.367), channel_id=1, source_target_pairs={{0,8},{4,12},{8,0},{12,4},{16,24},{20,28},{24,16},{28,20},{1,9},{5... | collective-permute-start | bytes 1966088 | tf_op jit(solution)/shard_map/ppermute | solution.py:130
  768.1 22.8 %collective-permute-start.109 = (bf16[112,960]{1,0:T(8,128)(2,1)S(1)}, bf16[112,960]{1,0:T(8,128)(2,1)S(1)}, u32[]{:S(2)}, u32[]{:S(2)}) collective-permute-start(bf16[112,960]{1,0:T(8,128)(2,1)S(1)} %get-tuple-element.423), channel_id=1, source_target_pairs={{0,2},{1,3},{2,0},{3,1},{4,6},{5,7},{6,4},{7,5},{8,10},{9,11},{10,... | collective-permute-start | bytes 645128 | tf_op jit(solution)/shard_map/ppermute | solution.py:869
  768.2 23.3 %collective-permute-start.110 = (bf16[112,960]{1,0:T(8,128)(2,1)S(1)}, bf16[112,960]{1,0:T(8,128)(2,1)S(1)}, u32[]{:S(2)}, u32[]{:S(2)}) collective-permute-start(bf16[112,960]{1,0:T(8,128)(2,1)S(1)} %get-tuple-element.424), channel_id=1, source_target_pairs={{0,3},{1,0},{2,1},{3,2},{4,7},{5,4},{6,5},{7,6},{8,11},{9,8},{10,9... | collective-permute-start | bytes 645128 | tf_op jit(solution)/shard_map/ppermute | solution.py:869
  770.6 30.4 %collective-permute-start.125 = (bf16[32,5120]{1,0:T(8,128)(2,1)S(1)}, bf16[32,5120]{1,0:T(8,128)(2,1)S(1)}, u32[]{:S(2)}, u32[]{:S(2)}) collective-permute-start(bf16[32,5120]{1,0:T(8,128)(2,1)S(1)} %get-tuple-element.419), channel_id=1, source_target_pairs={{0,1},{1,2},{2,3},{3,0},{4,5},{5,6},{6,7},{7,4},{8,9},{9,10},{10,1... | collective-permute-start | bytes 983048 | tf_op jit(solution)/shard_map/ppermute | solution.py:869
  770.7 36.4 %collective-permute-start.126 = (bf16[32,5120]{1,0:T(8,128)(2,1)S(1)}, bf16[32,5120]{1,0:T(8,128)(2,1)S(1)}, u32[]{:S(2)}, u32[]{:S(2)}) collective-permute-start(bf16[32,5120]{1,0:T(8,128)(2,1)S(1)} %get-tuple-element.420), channel_id=1, source_target_pairs={{0,2},{1,3},{2,0},{3,1},{4,6},{5,7},{6,4},{7,5},{8,10},{9,11},{10,... | collective-permute-start | bytes 983048 | tf_op jit(solution)/shard_map/ppermute | solution.py:869
  774.1 33.1 %collective-permute-start.127 = (bf16[32,5120]{1,0:T(8,128)(2,1)S(1)}, bf16[32,5120]{1,0:T(8,128)(2,1)S(1)}, u32[]{:S(2)}, u32[]{:S(2)}) collective-permute-start(bf16[32,5120]{1,0:T(8,128)(2,1)S(1)} %get-tuple-element.421), channel_id=1, source_target_pairs={{0,3},{1,0},{2,1},{3,2},{4,7},{5,4},{6,5},{7,6},{8,11},{9,8},{10,9... | collective-permute-start | bytes 983048 | tf_op jit(solution)/shard_map/ppermute | solution.py:869
  809.4 25.9 %collective-permute-start.128 = (bf16[32,5120]{1,0:T(8,128)(2,1)S(1)}, bf16[32,5120]{1,0:T(8,128)(2,1)S(1)}, u32[]{:S(2)}, u32[]{:S(2)}) collective-permute-start(bf16[32,5120]{1,0:T(8,128)(2,1)S(1)} %fusion.10.refs_0_), channel_id=1, source_target_pairs={{0,8},{4,12},{8,0},{12,4},{16,24},{20,28},{24,16},{28,20},{1,9},{5... | collective-permute-start | bytes 983048 | tf_op jit(solution)/shard_map/ppermute | solution.py:93
  811.5 24.4 %collective-permute-start.129 = (bf16[32,5120]{1,0:T(8,128)(2,1)S(1)}, bf16[32,5120]{1,0:T(8,128)(2,1)}, u32[]{:S(2)}, u32[]{:S(2)}) collective-permute-start(bf16[32,5120]{1,0:T(8,128)(2,1)S(1)} %fusion.10.refs_0_), channel_id=1, source_target_pairs={{0,16},{4,20},{8,24},{12,28},{16,0},{20,4},{24,8},{28,12},{1,17},{... | collective-permute-start | bytes 983048 | tf_op jit(solution)/shard_map/ppermute | solution.py:93
  840.2 22.9 %collective-permute-start.132 = (bf16[32,5120]{1,0:T(8,128)(2,1)S(1)}, bf16[32,5120]{1,0:T(8,128)(2,1)}, u32[]{:S(2)}, u32[]{:S(2)}) collective-permute-start(bf16[32,5120]{1,0:T(8,128)(2,1)S(1)} %fusion.10.refs_0_), channel_id=1, source_target_pairs={{0,4},{4,0},{8,12},{12,8},{16,20},{20,16},{24,28},{28,24},{1,5},{5... | collective-permute-start | bytes 983048 | tf_op jit(solution)/shard_map/ppermute | solution.py:105
  (302 other events, 2778.7 us)

commit v3 on v2

--- a/solution.py
+++ b/solution.py
@@ -29,7 +29,7 @@
 SCALE = HEAD**-0.5
 BF = jnp.bfloat16
 F32 = jnp.float32
-ANY = pl.BlockSpec(memory_space=pl.ANY)
+ANY = pl.BlockSpec(memory_space=pltpu.HBM)
 VMEM = pl.BlockSpec(memory_space=pltpu.VMEM)
 MIB = 1 << 20
 
@@ -77,70 +77,194 @@
     return lax.optimization_barrier((*values, *others))[: len(values)]
 
 
-def spread_first(piece, axis, size):
-    return {b: lax.ppermute(piece, "dp", pairs(size, b)) for b in outer_bits(size)}
-
-
 def part(x, axis, start, stop):
     return lax.slice_in_dim(x, start, stop, axis=axis)
 
 
-def spread(piece, axis, split, size):
-    rows = piece.shape[axis]
-    got = {(0, 0): (rows, piece)}
-    bits = outer_bits(size)
-    for b in bits:
-        got[b, 0] = (rows, lax.ppermute(piece, "dp", pairs(size, b)))
-    if len(bits) == 2:
-        got[6, 0] = (split, lax.ppermute(part(got[2, 0][1], axis, 0, split), "dp", pairs(size, 4)))
-        got[6, split] = (rows - split, lax.ppermute(part(got[4, 0][1], axis, split, rows), "dp", pairs(size, 2)))
-    else:
-        for m in range(0, size, 2):
-            if (m, 0) not in got:
-                low_bit = m & -m
-                got[m, 0] = (rows, lax.ppermute(got[m ^ low_bit, 0][1], "dp", pairs(size, low_bit)))
-    if size > 1:
-        for m, first in list(got):
-            n, x = got[m, first]
-            got[m | 1, first] = (n, lax.ppermute(x, "dp", pairs(size, 1)))
-    return [(m, first, n, x) for (m, first), (n, x) in got.items()]
-
-
 def add_up(*terms):
     return functools.reduce(jnp.add, [t.astype(F32) for t in terms])
 
 
-def gather_halves(even, odd, size):
-    if size > 1:
-        got = lax.ppermute(odd, "dp", pairs(size, 1))
-    else:
-        got = jnp.zeros_like(even)
-    cut = even.shape[1] // 2
-    bits = outer_bits(size)
-    if len(bits) == 2:
-        both = lambda m, h: add_up(even[m, h], got[m, h])
-        lo, hi = slice(0, cut), slice(cut, None)
-        send_x = jnp.stack([both(1, lo), both(3, lo)]).astype(BF)
-        send_y = jnp.stack([both(2, hi), both(3, hi)]).astype(BF)
-        got_x = lax.ppermute(send_x, "dp", pairs(size, 2))
-        got_y = lax.ppermute(send_y, "dp", pairs(size, 4))
-        next_y = add_up(even[2, lo], got[2, lo], got_x[1]).astype(BF)
-        next_x = add_up(even[1, hi], got[1, hi], got_y[1]).astype(BF)
-        last_y = lax.ppermute(next_y, "dp", pairs(size, 4))
-        last_x = lax.ppermute(next_x, "dp", pairs(size, 2))
-        return (
-            (add_up(even[0, lo], got[0, lo], got_x[0]).astype(BF), last_y),
-            (add_up(even[0, hi], got[0, hi], got_y[0]).astype(BF), last_x),
-        )
-    held = [add_up(even[m], got[m]) for m in range(even.shape[0])]
-    while len(held) > 1:
-        n = len(held) // 2
-        send = jnp.stack(held[n:]).astype(BF)
-        came = lax.ppermute(send, "dp", pairs(size, 2 * n))
-        held = [add_up(held[m], came[m]) for m in range(n)]
-    whole = held[0].astype(BF)
-    zero = jnp.zeros_like(whole)
-    return ((whole[:cut], zero[:cut]), (whole[cut:], zero[cut:]))
+class Flow:
+    def __init__(self):
+        self.hold = ()
+
+    def start(self, *jobs, also=()):
+        for job, stage in jobs:
+            sends = job.sends(stage)
+            if not sends:
+                job.under_way[stage] = []
+                continue
+            arrays = tie([x[1] for x in sends] + list(also), *self.hold)
+            arrays, also = arrays[: len(sends)], arrays[len(sends) :]
+            job.under_way[stage] = [
+                (key, lax.ppermute(x, axis, perm)) for (key, _, axis, perm), x in zip(sends, arrays)
+            ]
+        return also
+
+    def wait(self, *jobs, also=()):
+        flat = [(job, key, x) for job, stage in jobs for key, x in job.under_way.pop(stage)]
+        values = tie([x for _, _, x in flat] + list(also)) if flat or also else ()
+        for (job, key, _), x in zip(flat, values):
+            job.got[key] = x
+        if values:
+            self.hold = tuple(values[:1]) + tuple(values[len(flat) :])
+        return values[len(flat) :]
+
+
+class Moves:
+    def __init__(self, *sends):
+        self.list, self.got, self.under_way = sends, {}, {}
+
+    def sends(self, stage):
+        return [(i, *x) for i, x in enumerate(self.list)]
+
+    def results(self):
+        return [self.got[i] for i in range(len(self.list))]
+
+
+class Spread:
+    def __init__(self, piece, axis, split, size):
+        self.size, self.axis, self.split = size, axis, split
+        self.rows = piece.shape[axis] if piece is not None else None
+        self.got, self.under_way = {}, {}
+        if piece is not None:
+            self.got[0, 0, self.rows] = piece
+
+    def sends(self, stage):
+        size, axis, n, got = self.size, self.axis, self.rows, self.got
+        bits, cut = outer_bits(size), self.split
+        if cut is None:
+            if stage == 1:
+                return [((m, 0, n), got[0, 0, n], "dp", pairs(size, m)) for m in range(1, size) if m % 2 == 0 or m == 1]
+            if stage == 2:
+                return [((m | 1, 0, n), got[m, 0, n], "dp", pairs(size, 1)) for m in range(2, size, 2)]
+            return []
+        if stage == 1:
+            return [((b, 0, n), got[0, 0, n], "dp", pairs(size, b)) for b in bits]
+        if stage == 2 and len(bits) == 2:
+            return [
+                ((6, 0, cut), part(got[2, 0, n], axis, 0, cut), "dp", pairs(size, 4)),
+                ((6, cut, n - cut), part(got[4, 0, n], axis, cut, n), "dp", pairs(size, 2)),
+            ] + [((m | 1, 0, n), got[m, 0, n], "dp", pairs(size, 1)) for m in (0, 2, 4)]
+        if stage == 2:
+            for m in range(0, size, 2):
+                if (m, 0, n) not in got:
+                    low = m & -m
+                    got[m, 0, n] = lax.ppermute(got[m ^ low, 0, n], "dp", pairs(size, low))
+            return [((m | 1, 0, n), got[m, 0, n], "dp", pairs(size, 1)) for m in range(0, size, 2)] if size > 1 else []
+        if stage == 3 and len(bits) == 2:
+            return [((7, f, k), got[6, f, k], "dp", pairs(size, 1)) for f, k in ((0, cut), (cut, n - cut))]
+        return []
+
+    def segments(self):
+        return [(*key, x) for key, x in self.got.items() if key[0] != "z"]
+
+
+class Gather(Spread):
+    def __init__(self, full, owns, size, count, rank, straight=False):
+        super().__init__(None, 1, None, size)
+        self.count, self.rows, self.owns = count, full.shape[0] // size, owns
+        self.split = None if straight else split_at(self.rows)
+        self.piece = lax.dynamic_slice_in_dim(full, rank * self.rows, self.rows)
+
+    def sends(self, stage):
+        n = self.count
+        if stage == 0:
+            return [(("z", k), self.piece, "fsdp", [(i, (i + k) % n) for i in range(n)]) for k in range(1, n)]
+        if stage == 1:
+            self.got[0, 0, self.rows] = jnp.stack([self.got["z", k] for k in range(1, n)])
+        return super().sends(stage)
+
+    def whole(self):
+        return assemble(self.owns, self.segments(), self.count, self.rows, self.size)
+
+
+class Fold:
+    def __init__(self, even, odd, size, straight=False):
+        self.even, self.odd, self.size, self.straight = even, odd, size, straight
+        self.got, self.under_way = {}, {}
+        self.cut = even.shape[1] // 2
+
+    def both(self, m, h):
+        return add_up(self.even[m, h], self.got[0][m, h]) if self.size > 1 else self.even[m, h].astype(F32)
+
+    def sends(self, stage):
+        size, got = self.size, self.got
+        lo, hi = slice(0, self.cut), slice(self.cut, None)
+        if stage == 0:
+            return [(0, self.odd, "dp", pairs(size, 1))] if size > 1 else []
+        if self.straight:
+            if stage != 1:
+                return []
+            every = slice(None)
+            return [
+                (("far", m), self.both(m, every).astype(BF), "dp", pairs(size, 2 * m)) for m in range(1, self.even.shape[0])
+            ]
+        if len(outer_bits(size)) != 2:
+            return []
+        if stage == 1:
+            send_x = jnp.stack([self.both(1, lo), self.both(3, lo)]).astype(BF)
+            send_y = jnp.stack([self.both(2, hi), self.both(3, hi)]).astype(BF)
+            return [("x", send_x, "dp", pairs(size, 2)), ("y", send_y, "dp", pairs(size, 4))]
+        next_y = add_up(self.both(2, lo), got["x"][1]).astype(BF)
+        next_x = add_up(self.both(1, hi), got["y"][1]).astype(BF)
+        return [("yy", next_y, "dp", pairs(size, 4)), ("xx", next_x, "dp", pairs(size, 2))]
+
+    def terms(self):
+        return [self.both(0, slice(None)).astype(BF)] + [self.got["far", m] for m in range(1, self.even.shape[0])]
+
+    def halves(self):
+        size, got = self.size, self.got
+        lo, hi = slice(0, self.cut), slice(self.cut, None)
+        if self.straight:
+            others = [got["far", m] for m in range(1, self.even.shape[0])]
+            return tuple((self.both(0, h).astype(BF), *[x[h] for x in others]) for h in (lo, hi))
+        if len(outer_bits(size)) == 2:
+            return (
+                (add_up(self.both(0, lo), got["x"][0]).astype(BF), got["yy"]),
+                (add_up(self.both(0, hi), got["y"][0]).astype(BF), got["xx"]),
+            )
+        held = [self.both(m, slice(None)) for m in range(self.even.shape[0])]
+        while len(held) > 1:
+            n = len(held) // 2
+            came = lax.ppermute(jnp.stack(held[n:]).astype(BF), "dp", pairs(size, 2 * n))
+            held = [add_up(held[m], came[m]) for m in range(n)]
+        whole = held[0].astype(BF)
+        zero = jnp.zeros_like(whole)
+        return ((whole[lo], zero[lo]), (whole[hi], zero[hi]))
+
+
+class Total(Fold):
+    def __init__(self, even, odd, size, count, z, straight=False):
+        super().__init__(even, odd, size, straight)
+        self.count, self.z, self.spread = count, z, None
+
+    def sends(self, stage):
+        n = self.count
+        if stage < 3:
+            return super().sends(stage)
+        if stage == 3:
+            self.summed = jnp.concatenate([add_up(*terms).astype(BF) for terms in self.halves()], axis=0)
+            return [
+                (
+                    ("z", k),
+                    lax.dynamic_index_in_dim(self.summed, lax.rem(self.z + k, n), 0, keepdims=False),
+                    "fsdp",
+                    [(i, (i + k) % n) for i in range(n)],
+                )
+                for k in range(1, n)
+            ]
+        if stage == 4:
+            mine = lax.dynamic_index_in_dim(self.summed, self.z, 0, keepdims=False)
+            mine = add_up(mine, *[self.got["z", k] for k in range(1, n)]).astype(BF)
+            self.spread = Spread(mine, 0, None, self.size)
+            self.spread.got.update(self.got)
+            self.got = self.spread.got
+        return self.spread.sends(stage - 3)
+
+    def segments(self):
+        return [(*key, x) for key, x in self.got.items() if isinstance(key, tuple) and isinstance(key[0], int)]
 
 
 def zig_pairs(size):
@@ -150,11 +274,14 @@
     return ([(s, owner(2 * s)) for s in range(size)], [(s, owner(2 * s + 1)) for s in range(size)])
 
 
-def zig(x, size, rank):
+def zig(x, size):
     half = x.shape[0] // 2
     to_lo, to_hi = zig_pairs(size)
-    lo = lax.ppermute(x[:half], "dp", to_lo)
-    hi = lax.ppermute(x[half:], "dp", to_hi)
+    return Moves((x[:half], "dp", to_lo), (x[half:], "dp", to_hi))
+
+
+def zigged(moves, rank):
+    lo, hi = moves.results()
     swap = rank % 2 == 1
     return jnp.concatenate([jnp.where(swap, hi, lo), jnp.where(swap, lo, hi)], axis=0)
 
@@ -164,9 +291,14 @@
     to_lo, to_hi = zig_pairs(size)
     swap = rank % 2 == 1
     first, second = x[:half], x[half:]
-    lo = lax.ppermute(jnp.where(swap, second, first), "dp", [(b, a) for a, b in to_lo])
-    hi = lax.ppermute(jnp.where(swap, first, second), "dp", [(b, a) for a, b in to_hi])
-    return jnp.concatenate([lo, hi], axis=0)
+    return Moves(
+        (jnp.where(swap, second, first), "dp", [(b, a) for a, b in to_lo]),
+        (jnp.where(swap, first, second), "dp", [(b, a) for a, b in to_hi]),
+    )
+
+
+def unzigged(moves):
+    return jnp.concatenate(moves.results(), axis=0)
 
 
 def slice_rows(rows, size):
@@ -217,62 +349,6 @@
         0,
         14,
     )[0]
-
-
-def gather_weights(jobs, size, count, rank):
-    shifts = [[(i, (i + k) % count) for i in range(count)] for k in range(1, count)]
-    total = len(jobs)
-    steps = [full.shape[0] // size for full, _ in jobs]
-    bits = outer_bits(size)
-    state = [{} for _ in jobs]
-    results = [None] * total
-    hold = None
-    def stage(w, s):
-        st, step = state[w], steps[w]
-        cut = split_at(step)
-        if s == 0:
-            piece = lax.dynamic_slice_in_dim(jobs[w][0], rank * step, step)
-            return [(("z", k), piece, "fsdp", shift) for k, shift in enumerate(shifts)]
-        if s == 1:
-            st[0, 0, step] = jnp.stack([st["z", k] for k in range(count - 1)])
-            return [((b, 0, step), st[0, 0, step], "dp", pairs(size, b)) for b in bits]
-        if s == 2 and len(bits) == 2:
-            return [
-                ((6, 0, cut), part(st[2, 0, step], 1, 0, cut), "dp", pairs(size, 4)),
-                ((6, cut, step - cut), part(st[4, 0, step], 1, cut, step), "dp", pairs(size, 2)),
-            ] + [((m | 1, 0, step), st[m, 0, step], "dp", pairs(size, 1)) for m in (0, 2, 4)]
-        if s == 2:
-            for m in range(0, size, 2):
-                if (m, 0, step) not in st:
-                    low = m & -m
-                    st[m, 0, step] = lax.ppermute(st[m ^ low, 0, step], "dp", pairs(size, low))
-            return [((m | 1, 0, step), st[m, 0, step], "dp", pairs(size, 1)) for m in range(0, size, 2)]
-        if s == 3 and len(bits) == 2:
-            return [((7, f, n), st[6, f, n], "dp", pairs(size, 1)) for f, n in ((0, cut), (cut, step - cut))]
-        return []
-
-    for phase in range(total + 4):
-        sends, keys = [], []
-        for w in range(total):
-            s = phase - w
-            if 0 <= s < 4:
-                for key, *send in stage(w, s):
-                    keys.append((w, key))
-                    sends.append(send)
-        if sends:
-            arrays = [s[0] for s in sends]
-            if hold is not None:
-                arrays = tie(arrays, *hold)
-            got = [lax.ppermute(a, axis, perm) for a, (_, axis, perm) in zip(arrays, sends)]
-            got = lax.optimization_barrier(tuple(got))
-            hold = got[:1]
-            for (w, key), g in zip(keys, got):
-                state[w][key] = g
-        w = phase - 3
-        if 0 <= w < total:
-            segments = [(*k, v) for k, v in state[w].items() if k[0] != "z"]
-            results[w] = assemble(jobs[w][1], segments, count, steps[w], size)
-    return results
 
 
 def lane_of(shape):
@@ -346,6 +422,11 @@
     return copies
 
 
+def key_index(depth_ref, kb, step_no):
+    depth = depth_ref[pl.ds(kb, 1), :]
+    return jnp.where(depth > step_no, lane_of(depth.shape) + kb * KEYS, FAR)
+
+
 def chunk_of(a, rank, size):
     return jnp.where(a == 0, rank, 2 * size - 1 - rank)
 
@@ -356,7 +437,7 @@
     )
 
 
-def attend_kernel(spots, size, q_ref, tj_ref, meta_ref, *refs):
+def attend_kernel(spots, size, step_no, q_ref, tj_ref, meta_ref, *refs):
     segments, (o_ref, l_ref, kv_ref, kv1_ref, sems) = refs[: len(spots)], refs[len(spots) :]
     rank = lax.axis_index("dp")
     half = q_ref.shape[0] // 2
@@ -391,7 +472,7 @@
             def block(kb, carry):
                 top, acc = carry
                 keys = pl.ds(pl.multiple_of(kb * KEYS, KEYS), KEYS)
-                tj = tj_ref[pl.ds(kb, 1), :]
+                tj = key_index(tj_ref, kb, step_no)
                 s = dot_nt(q3, kv_ref[keys, cols])
                 s = jnp.where((tj <= ti) & (tj >= si), s, LOW)
                 new = jnp.maximum(top, jnp.max(s, axis=-1, keepdims=True))
@@ -418,14 +499,14 @@
     lax.fori_loop(0, 2, one, 0)
 
 
-def attend(q, segments, tj, meta, size):
+def attend(q, segments, tj, meta, step_no, size):
     rows = q.shape[0]
     half = rows // 2
     total = tj.size
     spots = [s[:3] for s in segments]
     n = sum(s[1] // half for s in [(0, x[2]) for x in spots])
     return call(
-        functools.partial(attend_kernel, spots, size),
+        functools.partial(attend_kernel, spots, size, step_no),
         [shaped(rows, PAD_Q, dtype=BF), shaped(2, GROUPED * half, LANES)],
         [q, tj, meta, *[s[3] for s in segments]],
         [VMEM] * 3 + [ANY] * len(segments),
@@ -435,7 +516,7 @@
     )
 
 
-def post_kernel(o_ref, hid_ref, gain_ref, router_ref, meta_ref, od_any, gu_any, *refs):
+def post_kernel(step_no, o_ref, hid_ref, gain_ref, router_ref, meta_ref, od_any, gu_any, *refs):
     ob_ref, m_ref, n2_ref, gu_ref, g_ref, new_ref, wo_ref, wd_ref, wgu_ref, sems, inner_ref = refs
     count = od_any.shape[0]
     r_out, r_down = D // count, FF // count
@@ -487,7 +568,7 @@
     total = att + dot(inner_ref[...], wd_ref[...])
     gate = jax.nn.sigmoid(jnp.sum(h * router_ref[...], axis=-1, keepdims=True))
     g_ref[...] = jnp.broadcast_to(gate, g_ref.shape)
-    live = meta_ref[:, 2:3] > 0
+    live = meta_ref[:, 2:3] > step_no
     new_ref[...] = h + jnp.where(live, gate * total, 0.0)
 
 
@@ -500,10 +581,10 @@
     ]
 
 
-def post(o, h, gain, router, meta, od, gu):
+def post(o, h, gain, router, meta, step_no, od, gu):
     rows = h.shape[0]
     return call(
-        post_kernel,
+        functools.partial(post_kernel, step_no),
         [
             shaped(rows, Q_COLS, dtype=BF),
             shaped(rows, D),
@@ -520,7 +601,7 @@
     )
 
 
-def ffn_back_kernel(dh_ref, hid_ref, new_ref, g_ref, meta_ref, gu_ref, m_ref, gain_ref, od_any, gu_any, *refs):
+def ffn_back_kernel(step_no, dh_ref, hid_ref, new_ref, g_ref, meta_ref, gu_ref, m_ref, gain_ref, od_any, gu_any, *refs):
     dfb_ref, dgu_ref, inner_ref, dm_ref, datt_ref, dob_ref, dz_ref, sums_ref, wo_ref, wd_ref, wgu_ref, sems = refs
     count = od_any.shape[0]
     r_out, r_down = D // count, FF // count
@@ -543,7 +624,7 @@
     wo_ref[D:, :] = jnp.zeros((Q_COLS - D, D), BF)
     rows = hid_ref.shape[0]
     dh, h = dh_ref[...], hid_ref[...]
-    live = meta_ref[:, 2:3] > 0
+    live = meta_ref[:, 2:3] > step_no
     gate = g_ref[:, 0:1]
     du = jnp.where(live, gate * dh, 0.0)
     dz = (1.0 - gate) * jnp.sum(dh * (new_ref[...] - h), axis=-1, keepdims=True)
@@ -587,10 +668,10 @@
             dob_ref[:, LANES * (2 * b + 1) : LANES * (2 * b + 2)] = jnp.where(low, 0.0, x).astype(BF)
 
 
-def ffn_back(dh, h, new, g, meta, gu_saved, m, gain, od, gu):
+def ffn_back(dh, h, new, g, meta, step_no, gu_saved, m, gain, od, gu):
     rows = h.shape[0]
     return call(
-        ffn_back_kernel,
+        functools.partial(ffn_back_kernel, step_no),
         [
             shaped(rows, D, dtype=BF),
             shaped(rows, 2 * FF, dtype=BF),
@@ -609,7 +690,7 @@
     )
 
 
-def attend_back_kernel(spots, size, q_ref, o_ref, dob_ref, l_ref, tj_ref, meta_ref, cos_ref, sin_ref, *refs):
+def attend_back_kernel(spots, size, step_no, q_ref, o_ref, dob_ref, l_ref, tj_ref, meta_ref, cos_ref, sin_ref, *refs):
     segments, refs = refs[: len(spots)], refs[len(spots) :]
     dq_ref, even_ref, odd_ref, kv_ref, dkv_ref, wide_ref, sems = refs
     rank = lax.axis_index("dp")
@@ -645,7 +726,7 @@
 
             def block(kb, acc):
                 keys = pl.ds(pl.multiple_of(kb * KEYS, KEYS), KEYS)
-                tj = tj_ref[pl.ds(kb, 1), :]
+                tj = key_index(tj_ref, kb, step_no)
                 kv = kv_ref[keys, cols]
                 s = dot_nt(q3, kv)
                 p = jnp.exp(jnp.where((tj <= ti) & (tj >= si), s - log3, LOW))
@@ -681,7 +762,7 @@
                 ref[lax.div(m, 2), side] = dkv_ref[chunk // per, :, at : at + half].astype(BF)
 
 
-def attend_back(q, o, dob, logs, tj, meta, cos, sin, segments, size):
+def attend_back(q, o, dob, logs, tj, meta, step_no, cos, sin, segments, size):
     rows = q.shape[0]
     half = rows // 2
     total = tj.size
@@ -689,7 +770,7 @@
     n = sum(x[2] // half for x in spots)
     pairs_n = max(size // 2, 1)
     return call(
-        functools.partial(attend_back_kernel, spots, size),
+        functools.partial(attend_back_kernel, spots, size, step_no),
         [
             shaped(rows, Q_COLS, dtype=BF),
             shaped(pairs_n, 2, KV_COLS, half, dtype=BF),
@@ -708,7 +789,12 @@
     )
 
 
-def qkv_back_kernel(dq_ref, a0, b0, a1, b1, cos_ref, sin_ref, hid_ref, dh_ref, dm_ref, dz_ref, router_ref, gain_ref, w_any, *refs):
+def qkv_back_kernel(n_terms, dq_ref, *refs):
+    terms, refs = refs[:n_terms], refs[n_terms:]
+    qkv_back_rest(dq_ref, terms, *refs)
+
+
+def qkv_back_rest(dq_ref, terms, cos_ref, sin_ref, hid_ref, dh_ref, dm_ref, dz_ref, router_ref, gain_ref, w_any, *refs):
     dp_ref, new_ref, sums_ref, w_ref, sems = refs
     rows_z = D // w_any.shape[0]
     copies = load_rows(w_any, (0, rows_z), w_ref, sems, 0)
@@ -719,13 +805,13 @@
     dp_ref[:, :Q_COLS] = dq_ref[...]
     lanes = lane_of((half, LANES))
     low = lanes < HEAD
-    for i, (a, b) in enumerate(((a0, b0), (a1, b1))):
+    for i in range(2):
         at = slice(i * half, (i + 1) * half)
         cos = jnp.where(low, cos_ref[at, :], 1.0)
         sin = jnp.where(low, sin_ref[at, :], 0.0)
         for h in range(KV_HEADS):
             cols = slice(LANES * h, LANES * (h + 1))
-            x = (a[cols, :].astype(F32) + b[cols, :].astype(F32)).T
+            x = add_up(*[t[i, cols, :] for t in terms]).T
             dp_ref[at, Q_COLS + LANES * h : Q_COLS + LANES * (h + 1)] = (x * cos - swap_halves(x, lanes) * sin).astype(BF)
     for c in copies:
         c.wait()
@@ -740,82 +826,96 @@
 
 def qkv_back(dq, parts, cos, sin, h, dh, dm, dz, router, gain, w):
     rows = h.shape[0]
-    (a0, b0), (a1, b1) = parts
     return call(
-        qkv_back_kernel,
+        functools.partial(qkv_back_kernel, len(parts)),
         [shaped(rows, ALL_COLS, dtype=BF), shaped(rows, D), shaped(1, D)],
-        [dq, a0, b0, a1, b1, cos, sin, h, dh, dm, dz, router, gain, w],
-        [VMEM] * 13 + [ANY],
+        [dq, *parts, cos, sin, h, dh, dm, dz, router, gain, w],
+        [VMEM] * (9 + len(parts)) + [ANY],
         [pltpu.VMEM((D, ALL_COLS), BF), pltpu.SemaphoreType.DMA((w.shape[0],))],
         2 * rows * D * ALL_COLS,
         24,
     )
 
 
-def grads_kernel(size, count, step, spare, block, lefts_n, plan, *refs):
-    lefts, rights = refs[: lefts_n * STEPS], refs[lefts_n * STEPS : 2 * lefts_n * STEPS]
-    refs = refs[2 * lefts_n * STEPS :]
+def grads_kernel(size, count, step, rows_z, block, *refs):
+    n, total = len(rows_z), sum(rows_z)
+    lefts, rights, refs = refs[: n * STEPS], refs[n * STEPS : 2 * n * STEPS], refs[2 * n * STEPS :]
+    spare = step * size - total if len(refs) > 3 + 3 * n else 0
     extra_ref, refs = (refs[0], refs[1:]) if spare else (None, refs)
     even_ref, odd_ref = refs[:2]
-    left_t, right_s, pack = refs[2 : 2 + lefts_n], refs[2 + lefts_n : 2 + 2 * lefts_n], refs[2 + 2 * lefts_n]
-    sems = refs[-1]
+    left_t, right_s, packs, sems = refs[2 : 2 + n], refs[2 + n : 2 + 2 * n], refs[2 + 2 * n : 2 + 3 * n], refs[-1]
     rank = lax.axis_index("dp")
     copies = []
-    for i in range(lefts_n):
+    for i in range(n):
         for r in range(STEPS):
-            n = rights[i * STEPS + r].shape[0]
-            c = pltpu.make_async_copy(rights[i * STEPS + r], right_s[i].at[pl.ds(r * n, n)], sems.at[len(copies)])
+            src = rights[i * STEPS + r]
+            c = pltpu.make_async_copy(src, right_s[i].at[pl.ds(r * src.shape[0], src.shape[0])], sems.at[len(copies)])
             c.start()
             copies.append(c)
-    for i in range(lefts_n):
+    for i in range(n):
+        wide = left_t[i].shape[0]
         for r in range(STEPS):
             src = lefts[i * STEPS + r]
-            n = src.shape[0]
-            for b in range(left_t[i].shape[0] // LANES + (1 if left_t[i].shape[0] % LANES else 0)):
-                lo, hi = b * LANES, min((b + 1) * LANES, left_t[i].shape[0])
-                left_t[i][lo:hi, r * n : (r + 1) * n] = src[:, lo:hi].astype(F32).T.astype(BF)
+            k = src.shape[0]
+            for lo in range(0, wide, LANES):
+                hi = min(lo + LANES, wide)
+                left_t[i][lo:hi, r * k : (r + 1) * k] = src[:, lo:hi].astype(F32).T.astype(BF)
     for c in copies:
         c.wait()
-    cols_total = right_s[0].shape[1]
-    filled = sum(rows for _, _, rows in plan)
-
-    def column(cb, _):
-        cols = pl.ds(pl.multiple_of(cb * block, LANES), block)
+
+    def put(j, z, first, cols, value):
+        m = rank ^ j
+        for par, ref in ((0, even_ref), (1, odd_ref)):
+
+            @pl.when(lax.rem(m, 2) == par)
+            def _(ref=ref):
+                ref[lax.div(m, 2), z, first : first + value.shape[0], cols] = value
+
+    def column(cols):
+        for i, rows in enumerate(rows_z):
+            tall = rows * count if rows * count <= 1024 else rows
+            for top in range(0, rows * count, tall):
+                packs[i][top : top + tall, :] = dot(left_t[i][top : top + tall, :], right_s[i][:, cols]).astype(BF)
         for z in range(count):
-            at = 0
-            for i, _, rows in plan:
-                pack[at : at + rows, :] = dot(left_t[i][z * rows : (z + 1) * rows, :], right_s[i][:, cols]).astype(BF)
-                at += rows
-            if spare:
-                pack[filled : step * size, :] = extra_ref[z, :, cols].astype(BF)
             for j in range(size):
-                m = rank ^ j
-                n = min(step, pack.shape[0] - j * step)
-                for par, ref in ((0, even_ref), (1, odd_ref)):
-                    @pl.when(lax.rem(m, 2) == par)
-                    def _(ref=ref):
-                        ref[lax.div(m, 2), z, :, cols] = pack[j * step : (j + 1) * step, :]
-        return 0
-
-    lax.fori_loop(0, cols_total // block, column, 0)
+                at = 0
+                for i, rows in enumerate(rows_z):
+                    a, b = max(j * step, at), min((j + 1) * step, at + rows)
+                    if a < b:
+                        top = z * rows + a - at
+                        put(j, z, a - j * step, cols, packs[i][top : top + b - a, :])
+                    at += rows
+                a, b = max(j * step, at), (j + 1) * step
+                if spare and a < b:
+                    put(j, z, a - j * step, cols, extra_ref[z, a - at : b - at, cols].astype(BF))
+
+    wide = right_s[0].shape[1]
+    if wide == block:
+        column(slice(0, wide))
+    else:
+
+        def body(cb, _):
+            column(pl.ds(pl.multiple_of(cb * block, LANES), block))
+            return 0
+
+        lax.fori_loop(0, wide // block, body, 0)
 
 
 def grads(lefts, rights, rows_z, size, count, step, block, extra=None):
     cols = rights[0][0].shape[1]
     tokens = STEPS * lefts[0][0].shape[0]
     k = len(lefts)
-    plan = [(i, i, n) for i, n in enumerate(rows_z)]
-    pairs_n = max(size // 2, 1)
     args = [x for l in lefts for x in l] + [x for r in rights for x in r] + ([extra] if extra is not None else [])
     specs = [VMEM] * (k * STEPS) + [ANY] * (k * STEPS) + ([VMEM] if extra is not None else [])
     return call(
-        functools.partial(grads_kernel, size, count, step, extra is not None, block, k, plan),
-        [shaped(pairs_n, count, step, cols, dtype=BF)] * 2,
+        functools.partial(grads_kernel, size, count, step, rows_z, block),
+        [shaped(max(size // 2, 1), count, step, cols, dtype=BF)] * 2,
         args,
         specs,
         [pltpu.VMEM((n * count, tokens), BF) for n in rows_z]
         + [pltpu.VMEM((tokens, cols), BF) for _ in rows_z]
-        + [pltpu.VMEM((step * size, block), BF), pltpu.SemaphoreType.DMA((k * STEPS,))],
+        + [pltpu.VMEM((n * count, block), BF) for n in rows_z]
+        + [pltpu.SemaphoreType.DMA((k * STEPS,))],
         2 * tokens * sum(rows_z) * count * cols,
         58,
     )
@@ -859,17 +959,6 @@
     )
 
 
-def reduce_weight(even, odd, size, count, z):
-    halves = gather_halves(even, odd, size)
-    summed = jnp.concatenate([add_up(a, b).astype(BF) for a, b in halves], axis=0)
-    mine = lax.dynamic_index_in_dim(summed, z, 0, keepdims=False)
-    terms = [mine]
-    for k in range(1, count):
-        out = lax.dynamic_index_in_dim(summed, lax.rem(z + k, count), 0, keepdims=False)
-        terms.append(lax.ppermute(out, "fsdp", [(i, (i + k) % count) for i in range(count)]))
-    return add_up(*terms).astype(BF)
-
-
 def per_device(
     tokens,
     cotangent,
@@ -904,15 +993,30 @@
         [out_weight, down_weight, jnp.zeros((step_od * size - rows_z - down_z, D), BF)], axis=0
     )
     gu_full = jnp.pad(gate_up_weight, ((0, spare), (0, 0)))
-    w_q, w_od, w_gu = gather_weights(
-        [(qkv_full, [qkv_full]), (od_full, [out_weight, down_weight]), (gu_full, [gate_up_weight])], size, count, rank
-    )
+    flow = Flow()
+    get_q = Gather(qkv_full, [qkv_full], size, count, rank, True)
+    get_od = Gather(od_full, [out_weight, down_weight], size, count, rank)
+    get_gu = Gather(gu_full, [gate_up_weight], size, count, rank)
+    token_moves = zig(tokens[0], size)
+    get_depth = Spread(route_depth, 0, None, size)
+    flow.start((get_q, 0), (token_moves, 0), (get_depth, 1))
+    flow.wait((get_q, 0), (get_depth, 1))
+    flow.start((get_q, 1), (get_od, 0), (get_depth, 2))
+    flow.wait((get_q, 1), (token_moves, 0), (get_depth, 2))
+    flow.start((get_q, 2))
+    flow.wait((get_od, 0))
+    flow.start((get_od, 1), (get_gu, 0))
+    flow.wait((get_q, 2))
+    w_q = get_q.whole()
     extras = w_q[:, rows_z : rows_z + 5, :rows_z].astype(F32)
     extras = jnp.transpose(extras, (1, 0, 2)).reshape(5, D)
     gain_one, gain_two = extras[0:1], extras[1:2]
 
-    hidden = zig(tokens[0], size, rank).astype(F32)
-    depth_all = lax.all_gather(route_depth[0], "dp", axis=0, tiled=True)
+    hidden = zigged(token_moves, rank).astype(F32)
+    depth_all = jnp.concatenate([x for _, _, _, x in sorted(get_depth.segments(), key=lambda x: x[0])], axis=0).astype(F32)
+    order = (rank ^ jnp.arange(size)[:, None]) == jnp.arange(size)[None, :]
+    depth_all = jnp.dot(order.astype(F32), depth_all, precision=lax.Precision.HIGHEST)
+    depth_all = depth_all.astype(jnp.int32).reshape(group_rows)
     index = jnp.arange(group_rows, dtype=jnp.int32)
     lengths_here = lengths[0]
     ends = [jnp.sum(lengths_here[: i + 1]) for i in range(lengths_here.shape[0])]
@@ -924,11 +1028,8 @@
         ]
     )
     index_here, start_here, depth_here = mine(index), mine(start), mine(depth_all)
-    tj = [jnp.where(depth_all > r, index, FAR).reshape(group_rows // KEYS, KEYS) for r in range(STEPS)]
-    zeros = jnp.zeros_like(index_here)
-    meta = [
-        jnp.stack([index_here, start_here, (depth_here > r).astype(jnp.int32)] + [zeros] * 5, axis=1) for r in range(STEPS)
-    ]
+    depth_rows = depth_all.reshape(group_rows // KEYS, KEYS)
+    meta = jnp.stack([index_here, start_here, depth_here] + [jnp.zeros_like(index_here)] * 5, axis=1)
     frequency = jnp.exp(jnp.arange(HEAD // 2, dtype=F32) * (-2.0 * math.log(10000.0) / HEAD))
     angles = (index_here - start_here).astype(F32)[:, None] * frequency[None, :]
     cos, sin = jnp.cos(angles), jnp.sin(angles)
@@ -938,27 +1039,64 @@
     saved = []
     for r in range(STEPS):
         n1, q, kv = norm_qkv(hidden, gain_one, cos, sin, w_q)
-        segments = spread(kv, 0, half, size)
-        o, logs = attend(q, segments, tj[r], meta[r], size)
-        ob, m, n2, gu_saved, g, new = post(o, hidden, gain_two, extras[2 + r : 3 + r], meta[r], w_od, w_gu)
+        get_kv = Spread(kv, 0, None, size)
+        if r == 0:
+            flow.wait(also=(n1,))
+            flow.start((get_kv, 1))
+            flow.wait((get_od, 1))
+            flow.start((get_od, 2))
+            flow.wait((get_kv, 1))
+            flow.start((get_kv, 2))
+            flow.wait((get_od, 2), (get_gu, 0))
+            flow.start((get_gu, 1), (get_od, 3))
+            flow.wait((get_kv, 2), (get_od, 3))
+        else:
+            flow.start((get_kv, 1))
+            if r == 1:
+                cotangent_moves = zig(cotangent[0], size)
+                flow.wait((get_kv, 1))
+                flow.start((get_kv, 2), (cotangent_moves, 0))
+                flow.wait((get_kv, 2), (cotangent_moves, 0))
+            else:
+                flow.wait((get_kv, 1))
+                flow.start((get_kv, 2))
+                flow.wait((get_kv, 2))
+        segments = get_kv.segments()
+        o, logs = attend(q, segments, depth_rows, meta, r, size)
+        if r == 0:
+            w_od = get_od.whole()
+            (o, w_od) = flow.wait((get_gu, 1), also=(o, w_od))
+            flow.start((get_gu, 2))
+            flow.wait((get_gu, 2))
+            flow.start((get_gu, 3))
+            flow.wait((get_gu, 3))
+            w_gu = get_gu.whole()
+        ob, m, n2, gu_saved, g, new = post(o, hidden, gain_two, extras[2 + r : 3 + r], meta, r, w_od, w_gu)
         saved.append((hidden, n1, q, segments, o, logs, ob, m, n2, gu_saved, g, new))
         hidden = new
-    hidden_out = unzig(hidden.astype(BF), size, rank).astype(F32)
-
-    dh = zig(cotangent[0], size, rank).astype(F32)
+    out_moves = unzig(hidden.astype(BF), size, rank)
+    flow.start((out_moves, 0))
+
+    dh = zigged(cotangent_moves, rank).astype(F32)
     kept = [None] * STEPS
     gains_one, gains_two, routers = [], [], [None] * STEPS
     for r in reversed(range(STEPS)):
         hidden, n1, q, segments, o, logs, ob, m, n2, gu_saved, g, new = saved[r]
-        dfb, dgu, inner, dm, datt, dob, dz, sums = ffn_back(dh, hidden, new, g, meta[r], gu_saved, m, gain_two, w_od, w_gu)
+        dfb, dgu, inner, dm, datt, dob, dz, sums = ffn_back(dh, hidden, new, g, meta, r, gu_saved, m, gain_two, w_od, w_gu)
         routers[r] = sums[0]
         gains_two.append(sums[1])
+        dq, even, odd = attend_back(q, o, dob, logs, depth_rows, meta, r, cos, sin, segments, size)
+        sum_kv = Fold(even, odd, size, True)
+        flow.start((sum_kv, 0))
         if r == 0:
             mid = kept[1:]
-            gu_parts = grads(
-                [[n2] + [k["n2"] for k in mid]], [[dgu] + [k["dgu"] for k in mid]], [rows_z], size, count, step_q, 640
+            even, odd = grads(
+                [[n2] + [k["n2"] for k in mid]], [[dgu] + [k["dgu"] for k in mid]], [rows_z], size, count, step_q, 1280
             )
-            od_parts = grads(
+            sum_gu = Total(even, odd, size, count, z)
+            flow.wait((sum_kv, 0), also=(even,))
+            flow.start((sum_kv, 1), (sum_gu, 0))
+            even, odd = grads(
                 [[ob] + [k["ob"] for k in mid], [inner] + [k["inner"] for k in mid]],
                 [[datt] + [k["datt"] for k in mid], [dfb] + [k["dfb"] for k in mid]],
                 [rows_z, down_z],
@@ -967,28 +1105,50 @@
                 step_od,
                 D,
             )
-        dq, even, odd = attend_back(q, o, dob, logs, tj[r], meta[r], cos, sin, segments, size)
-        parts = gather_halves(even, odd, size)
-        parts = [tuple(x.reshape(KV_COLS, half) for x in p) for p in parts]
+            sum_od = Total(even, odd, size, count, z)
+            flow.wait((sum_kv, 1), (sum_gu, 0), also=(even,))
+            (dq,) = flow.start((sum_gu, 1), (sum_od, 0), also=(dq,))
+        else:
+            flow.wait((sum_kv, 0), *(((out_moves, 0),) if r == STEPS - 1 else ()))
+            flow.start((sum_kv, 1))
+            flow.wait((sum_kv, 1))
+        parts = sum_kv.terms()
         dp, dh, gain_sum = qkv_back(dq, parts, cos, sin, hidden, dh, dm, dz, extras[2 + r : 3 + r], gain_one, w_q)
+        if r == 0:
+            in_moves = unzig(dh.astype(BF), size, rank)
+            flow.start((in_moves, 0))
         gains_one.append(gain_sum[0])
         kept[r] = dict(n1=n1, n2=n2, ob=ob, dgu=dgu, inner=inner, dfb=dfb, datt=datt, dp=dp)
-    input_grad = unzig(dh.astype(BF), size, rank).astype(F32)
 
     small = jnp.stack([sum(gains_one), sum(gains_two), *routers], axis=0)
     small = jnp.transpose(small.reshape(5, count, rows_z), (1, 0, 2))
     small = jnp.pad(small, ((0, 0), (0, spare - 5), (0, ALL_COLS - rows_z)))
-    q_parts = grads([[k["n1"] for k in kept]], [[k["dp"] for k in kept]], [rows_z], size, count, step_q, ALL_COLS // 13, small)
-
-    results = []
-    for (even, odd), step, splits in (
-        (gu_parts, step_q, [rows_z]),
-        (od_parts, step_od, [rows_z, down_z]),
-        (q_parts, step_q, [rows_z, spare]),
-    ):
-        mine_sum = reduce_weight(even, odd, size, count, z)
-        results.append(finish(spread(mine_sum, 0, split_at(step), size), splits, step))
-    (gate_up_grad,), (out_grad, down_grad), (qkv_packed, small) = results
+    even, odd = grads([[k["n1"] for k in kept]], [[k["dp"] for k in kept]], [rows_z], size, count, step_q, ALL_COLS, small)
+    sum_q = Total(even, odd, size, count, z, True)
+    flow.wait((sum_gu, 1), (sum_od, 0), also=(even,))
+    flow.start((sum_gu, 2), (sum_q, 0))
+    flow.wait((sum_gu, 2), (sum_q, 0))
+    flow.start((sum_gu, 3), (sum_od, 1))
+    flow.wait((sum_od, 1), (in_moves, 0))
+    flow.start((sum_od, 2))
+    flow.wait((sum_od, 2))
+    flow.start((sum_od, 3), (sum_q, 1))
+    flow.wait((sum_gu, 3))
+    flow.start((sum_gu, 4))
+    flow.wait((sum_q, 1), (sum_od, 3))
+    flow.start((sum_q, 3), (sum_od, 4))
+    flow.wait((sum_gu, 4))
+    flow.start((sum_gu, 5))
+    flow.wait((sum_q, 3), (sum_od, 4), (sum_gu, 5))
+    flow.start((sum_q, 4), (sum_od, 5))
+    (gate_up_grad,) = finish(sum_gu.segments(), [rows_z], step_q)
+    flow.wait((sum_q, 4), (sum_od, 5), also=(gate_up_grad,))
+    flow.start((sum_q, 5))
+    out_grad, down_grad = finish(sum_od.segments(), [rows_z, down_z], step_od)
+    flow.wait((sum_q, 5))
+    qkv_packed, small = finish(sum_q.segments(), [rows_z, spare], step_q)
+    hidden_out = unzigged(out_moves).astype(F32)
+    input_grad = unzigged(in_moves).astype(F32)
     kv = qkv_packed[:, Q_COLS:].reshape(rows_z, KV_HEADS, 2, HEAD)
     qkv_grad = jnp.concatenate(
         [qkv_packed[:, :D], kv[:, :, 0].reshape(rows_z, kv_cols), kv[:, :, 1].reshape(rows_z, kv_cols)], axis=1

time: 880 us -> 787 us (0.89)
  local copies, waits for them, and re-layouts: 141 us -> 103 us
  waiting for transfers between devices: 219 us -> 185 us
  Pallas kernels: 317 us -> 291 us
  other arithmetic: 43.3 us -> 52.7 us
  starting transfers between devices: 136 us -> 145 us
    ppermute x137 -> x126, waiting for transfers between devices: 219 us -> 185 us  [start(): lax.ppermute(x, axis, perm)]
    pallas_call x27, Pallas kernels: 317 us -> 291 us  [call(): pl.pallas_call(kernel, out_shape=outs, in_specs=specs, out_specs=out_spec...]
    slice x18 -> x4, local copies, waits for them, and re-layouts: 15.4 us -> 5.88 us  [part(): return lax.slice_in_dim(x, start, stop, axis=axis)]
    ppermute x137 -> x126, starting transfers between devices: 136 us -> 145 us  [start(): lax.ppermute(x, axis, perm)]
    convert_element_type x19 -> x18, other arithmetic: 15.3 us -> 24.3 us  [the longest x3 7.2 us: sends(): add_up(*terms).astype(BF)]
    unnamed x402 -> x385, local copies, waits for them, and re-layouts: 85 us -> 77.5 us
  transfers between devices with their start and end apart: 137 -> 126, of which waited for: 40 -> 42; matrix products, arithmetic and copies ran while one was open for 12% -> 9% of each run, Pallas kernels for 12% -> 10%
where the time goes in v3:
time: 787 us; the launch traced here: 780 us
  Pallas kernels  291 us (37%)
  waiting for transfers between devices  185 us (24%)
  starting transfers between devices  145 us (18%)
  local copies, waits for them, and re-layouts  103 us (13%)
  other arithmetic  52.7 us (7%)
    pallas_call x27, Pallas kernels, call(): pl.pallas_call(kernel, out_shape=outs, in_specs=specs, out_specs=out_spec...  291 us
    ppermute x126, waiting for transfers between devices, start(): lax.ppermute(x, axis, perm)  185 us
    ppermute x126, starting transfers between devices, start(): lax.ppermute(x, axis, perm)  145 us
    unnamed x385, local copies, waits for them, and re-layouts  77.5 us
  transfers between devices with their start and end apart: 126, of which 42 were waited for; matrix products, arithmetic and copies ran while one was open for 9% of the time, Pallas kernels for 10%

profile of v3, /device:TPU:0, one launch (start us, length us, event | category | flops | bytes accessed | tf_op | source)
XLA Modules:
  0.0 780.1 jit_solution(3836992145063087153)
XLA Ops:
  40.0 7.5 collective-permute-done.8
  58.0 6.3 collective-permute-done.24.refs_4_
  118.2 8.2 %collective-permute-done.36.refs_3_ = bf16[256,640]{1,0:T(8,128)(2,1)S(1)} collective-permute-done((bf16[256,640]{1,0:T(8,128)(2,1)S(1)}, bf16[256,640]{1,0:T(8,128)(2,1)S(1)}, u32[]{:S(2)}, u32[]{:S(2)}) %collective-permute-start.36) | collective-permute-done | bytes 327712 | tf_op jit(solution)/shard_map/ppermute | solution.py:101
  141.3 20.6 %shard_map.180 = (bf16[256,1920]{1,0:T(8,128)(2,1)S(1)}, f32[2,384,128]{2,1,0:T(8,128)S(1)}) custom-call(bf16[256,1920]{1,0:T(8,128)(2,1)S(1)} %copy-done.91, s32[4,512]{1,0:T(4,128)S(1)} %reshape_reshape.3.tj_ref, s32[256,8]{1,0:T(8,128)S(1)} %copy.81.meta_ref, bf16[256,640]{1,0:T(8,128)(2,1)S(1)} %copy-done.117, bf16[256,640]{1,0:T(8,128)(2,1)S(1)} %copy-done.120, ...), custom_call_target="tpu_custom_call" | custom-call | flops 2013265920 | bytes 4997120 | tf_op jit(solution)/shard_map/pallas_call | solution.py:52
  167.4 12.0 %collective-permute-done.43.refs_4_ = bf16[3,16,5120]{2,1,0:T(8,128)(2,1)} collective-permute-done((bf16[3,16,5120]{2,1,0:T(8,128)(2,1)S(1)}, bf16[3,16,5120]{2,1,0:T(8,128)(2,1)}, u32[]{:S(2)}, u32[]{:S(2)}) %collective-permute-start.43) | collective-permute-done | bytes 491552 | tf_op jit(solution)/shard_map/ppermute | solution.py:101
  199.1 8.2 %shard_map.183 = (bf16[256,1024]{1,0:T(8,128)(2,1)S(1)}, f32[256,960]{1,0:T(8,128)S(1)}, bf16[256,960]{1,0:T(8,128)(2,1)S(1)}, bf16[256,5120]{1,0:T(8,128)(2,1)}...) custom-call(bf16[256,1920]{1,0:T(8,128)(2,1)S(1)} %copy-done.46, f32[256,960]{1,0:T(8,128)S(1)} %copy-done.9, ...), custom_call_target="tpu_custom_call" | custom-call | flops 4278190080 | bytes 25083392 | tf_op jit(solution)/shard_map/pallas_call | solution.py:52
  223.0 6.1 collective-permute-done.52.refs_3_
  239.8 7.5 collective-permute-done.58
  251.1 19.4 %shard_map.185 = (bf16[256,1920]{1,0:T(8,128)(2,1)S(1)}, f32[2,384,128]{2,1,0:T(8,128)S(1)}) custom-call(bf16[256,1920]{1,0:T(8,128)(2,1)S(1)} %copy-done.94, s32[4,512]{1,0:T(4,128)S(1)} %copy-done.84, s32[256,8]{1,0:T(8,128)S(1)} %copy.81.meta_ref, bf16[256,640]{1,0:T(8,128)(2,1)S(1)} %copy-done.135, bf16[256,640]{1,0:T(8,128)(2,1)S(1)} %copy-done.138, ...), custom_call_target="tpu_custom_call" | custom-call | flops 2013265920 | bytes 4997120 | tf_op jit(solution)/shard_map/pallas_call | solution.py:52
  271.4 8.5 %shard_map.186 = (bf16[256,1024]{1,0:T(8,128)(2,1)S(1)}, f32[256,960]{1,0:T(8,128)S(1)}, bf16[256,960]{1,0:T(8,128)(2,1)S(1)}, bf16[256,5120]{1,0:T(8,128)(2,1)}...) custom-call(bf16[256,1920]{1,0:T(8,128)(2,1)S(1)} %get-tuple-element.476.o_ref, f32[256,960]{1,0:T(8,128)S(1)} %copy-done.3, ...), custom_call_target="tpu_custom_call" | custom-call | flops 4278190080 | bytes 25083392 | tf_op jit(solution)/shard_map/pallas_call | solution.py:52
  297.1 6.3 collective-permute-done.62.refs_4_
  306.1 18.7 %shard_map.188 = (bf16[256,1920]{1,0:T(8,128)(2,1)S(1)}, f32[2,384,128]{2,1,0:T(8,128)S(1)}) custom-call(bf16[256,1920]{1,0:T(8,128)(2,1)S(1)} %copy-done.97, s32[4,512]{1,0:T(4,128)S(1)} %copy-done.85, s32[256,8]{1,0:T(8,128)S(1)} %copy.81.meta_ref, bf16[256,640]{1,0:T(8,128)(2,1)} %get-tuple-element.483.refs_0_, ...), custom_call_target="tpu_custom_call" | custom-call | flops 2013265920 | bytes 4997120 | tf_op jit(solution)/shard_map/pallas_call | solution.py:52
  324.8 8.1 %shard_map.189 = (bf16[256,1024]{1,0:T(8,128)(2,1)S(1)}, f32[256,960]{1,0:T(8,128)S(1)}, bf16[256,960]{1,0:T(8,128)(2,1)S(1)}, bf16[256,5120]{1,0:T(8,128)(2,1)}...) custom-call(bf16[256,1920]{1,0:T(8,128)(2,1)S(1)} %get-tuple-element.494.o_ref, f32[256,960]{1,0:T(8,128)S(1)} %copy-done.6, ...), custom_call_target="tpu_custom_call" | custom-call | flops 4278190080 | bytes 25083392 | tf_op jit(solution)/shard_map/pallas_call | solution.py:52
  335.7 14.9 %shard_map.190 = (bf16[256,960]{1,0:T(8,128)(2,1)S(1)}, bf16[256,5120]{1,0:T(8,128)(2,1)}, bf16[256,2560]{1,0:T(8,128)(2,1)}, f32[256,960]{1,0:T(8,128)}, bf16[2...) custom-call(f32[256,960]{1,0:T(8,128)} %maximum_convert_fusion.1.dh_ref.refs_, ...), custom_call_target="tpu_custom_call" | custom-call | flops 4278190080 | bytes 31083776 | tf_op jit(solution)/shard_map/pallas_call | solution.py:52
  352.2 28.5 %shard_map.191 = (bf16[256,1024]{1,0:T(8,128)(2,1)S(1)}, bf16[4,2,640,128]{3,2,1,0:T(8,128)(2,1)}, bf16[4,2,640,128]{3,2,1,0:T(8,128)(2,1)}) custom-call(bf16[256,1920]{1,0:T(8,128)(2,1)S(1)} %copy-done.97, bf16[256,1920]{1,0:T(8,128)(2,1)S(1)} %get-tuple-element.494.o_ref, bf16[256,1920]{1,0:T(8,128)(2,1)} %get-tuple-element.501.dob_ref, ...), custom_call_target="tpu_custom_call" | custom-call | flops 5033164800 | bytes 9388032 | tf_op jit(solution)/shard_map/pallas_call | solution.py:52
  392.0 6.4 collective-permute-start.69
  406.0 10.5 %collective-permute-done.70.refs_2_ = bf16[2,640,128]{2,1,0:T(8,128)(2,1)S(1)} collective-permute-done((bf16[2,640,128]{2,1,0:T(8,128)(2,1)S(1)}, bf16[2,640,128]{2,1,0:T(8,128)(2,1)S(1)}, u32[]{:S(2)}, u32[]{:S(2)}) %collective-permute-start.70) | collective-permute-done | bytes 327712 | tf_op jit(solution)/shard_map/ppermute | solution.py:101
  421.2 14.8 %shard_map.193 = (bf16[256,960]{1,0:T(8,128)(2,1)S(1)}, bf16[256,5120]{1,0:T(8,128)(2,1)}, bf16[256,2560]{1,0:T(8,128)(2,1)}, f32[256,960]{1,0:T(8,128)}, bf16[2...) custom-call(f32[256,960]{1,0:T(8,128)} %copy-done.27, ...), custom_call_target="tpu_custom_call" | custom-call | flops 4278190080 | bytes 31083776 | tf_op jit(solution)/shard_map/pallas_call | solution.py:52
  437.6 29.0 %shard_map.194 = (bf16[256,1024]{1,0:T(8,128)(2,1)S(1)}, bf16[4,2,640,128]{3,2,1,0:T(8,128)(2,1)}, bf16[4,2,640,128]{3,2,1,0:T(8,128)(2,1)}) custom-call(bf16[256,1920]{1,0:T(8,128)(2,1)S(1)} %copy-done.95, bf16[256,1920]{1,0:T(8,128)(2,1)S(1)} %copy-done.49, bf16[256,1920]{1,0:T(8,128)(2,1)} %get-tuple-element.527.dob_ref, f32[2,384,128]{2,1,0:T(8,128)S(1)} %copy-done.143, ...), custom_call_target="tpu_custom_call" | custom-call | flops 5033164800 | bytes 9388032 | tf_op jit(solution)/shard_map/pallas_call | solution.py:52
  475.2 7.1 collective-permute-done.73.refs_1_
  482.3 6.3 collective-permute-done.74.refs_2_
  493.3 14.9 %shard_map.196 = (bf16[256,960]{1,0:T(8,128)(2,1)S(1)}, bf16[256,5120]{1,0:T(8,128)(2,1)}, bf16[256,2560]{1,0:T(8,128)(2,1)}, f32[256,960]{1,0:T(8,128)}, bf16[2...) custom-call(f32[256,960]{1,0:T(8,128)} %copy-done.25, ...), custom_call_target="tpu_custom_call" | custom-call | flops 4278190080 | bytes 31083776 | tf_op jit(solution)/shard_map/pallas_call | solution.py:52
  510.5 30.4 %shard_map.199 = (bf16[256,1024]{1,0:T(8,128)(2,1)S(1)}, bf16[4,2,640,128]{3,2,1,0:T(8,128)(2,1)}, bf16[4,2,640,128]{3,2,1,0:T(8,128)(2,1)}) custom-call(bf16[256,1920]{1,0:T(8,128)(2,1)S(1)} %copy-done.92, bf16[256,1920]{1,0:T(8,128)(2,1)S(1)} %copy-done.47, bf16[256,1920]{1,0:T(8,128)(2,1)} %get-tuple-element.562.dob_ref, f32[2,384,128]{2,1,0:T(8,128)S(1)} %copy-done.141, ...), custom_call_target="tpu_custom_call" | custom-call | flops 5033164800 | bytes 9388032 | tf_op jit(solution)/shard_map/pallas_call | solution.py:52
  541.8 19.4 %shard_map.198 = (bf16[4,4,32,5120]{3,2,1,0:T(8,128)(2,1)}, bf16[4,4,32,5120]{3,2,1,0:T(8,128)(2,1)}) custom-call(bf16[256,960]{1,0:T(8,128)(2,1)} %copy-done.105, bf16[256,960]{1,0:T(8,128)(2,1)} %copy-done.107, bf16[256,960]{1,0:T(8,128)(2,1)} %copy-done.111, bf16[256,5120]{1,0:T(8,128)(2,1)} %get-tuple-element.558.refs_3_, ...), custom_call_target="tpu_custom_call" | custom-call | flops 7549747200 | bytes 19824640 | tf_op jit(solution)/shard_map/pallas_call | solution.py:52
  567.7 14.2 %shard_map.197 = (bf16[4,4,112,960]{3,2,1,0:T(8,128)(2,1)}, bf16[4,4,112,960]{3,2,1,0:T(8,128)(2,1)}) custom-call(bf16[256,1024]{1,0:T(8,128)(2,1)} %copy-done.104, bf16[256,1024]{1,0:T(8,128)(2,1)} %copy-done.106, bf16[256,1024]{1,0:T(8,128)(2,1)} %copy-done.108, bf16[256,2560]{1,0:T(8,128)(2,1)} %get-tuple-element.545.refs_3_, ...), custom_call_target="tpu_custom_call" | custom-call | flops 5190451200 | bytes 15335424 | tf_op jit(solution)/shard_map/pallas_call | solution.py:52
  611.4 8.5 %shard_map.201 = (bf16[4,4,32,1664]{3,2,1,0:T(8,128)(2,1)}, bf16[4,4,32,1664]{3,2,1,0:T(8,128)(2,1)}) custom-call(bf16[256,960]{1,0:T(8,128)(2,1)} %copy-done.101, bf16[256,960]{1,0:T(8,128)(2,1)} %copy-done.102, bf16[256,960]{1,0:T(8,128)(2,1)} %copy-done.103, bf16[256,1664]{1,0:T(8,128)(2,1)} %copy-done.100, bf16[256,1664]{1,0:T(8,128)(2,1)} %copy-done.99, ...), custom_call_target="tpu_custom_call" | custom-call | flops 2453667840 | bytes 7864320 | tf_op jit(solution)/shard_map/pallas_call | solution.py:52
  631.3 10.8 %collective-permute-done.84 = bf16[2,32,5120]{2,1,0:T(8,128)(2,1)S(1)} collective-permute-done((bf16[2,32,5120]{2,1,0:T(8,128)(2,1)}, bf16[2,32,5120]{2,1,0:T(8,128)(2,1)S(1)}, u32[]{:S(2)}, u32[]{:S(2)}) %collective-permute-start.84) | collective-permute-done | bytes 655392 | tf_op jit(solution)/shard_map/ppermute | solution.py:101
  653.7 7.2 collective-permute-done.106
  664.6 8.6 %collective-permute-done.107 = bf16[32,5120]{1,0:T(8,128)(2,1)S(1)} collective-permute-done((bf16[32,5120]{1,0:T(8,128)(2,1)S(1)}, bf16[32,5120]{1,0:T(8,128)(2,1)S(1)}, u32[]{:S(2)}, u32[]{:S(2)}) %collective-permute-start.107) | collective-permute-done | bytes 327712 | tf_op jit(solution)/shard_map/ppermute | solution.py:101
  689.0 6.1 collective-permute-done.91
  718.7 7.1 collective-permute-done.97
  741.1 6.6 collective-permute-done.100
  (733 shorter events, 388.3 us)
Async XLA Ops:
  3.0 21.2 %collective-permute-start = (bf16[32,1664]{1,0:T(8,128)(2,1)S(1)}, bf16[32,1664]{1,0:T(8,128)(2,1)S(1)}, u32[]{:S(2)}, u32[]{:S(2)}) collective-permute-start(bf16[32,1664]{1,0:T(8,128)(2,1)S(1)} %fusion.62), channel_id=1, source_target_pairs={{0,1},{1,2},{2,3},{3,0},{4,5},{5,6},{6,7},{7,4},{8,9},{9,10},{10,1... | collective-permute-start | bytes 319496 | tf_op jit(solution)/shard_map/ppermute | solution.py:101
  28.5 19.0 %collective-permute-start.8 = (bf16[112,960]{1,0:T(8,128)(2,1)S(1)}, bf16[112,960]{1,0:T(8,128)(2,1)S(1)}, u32[]{:S(2)}, u32[]{:S(2)}) collective-permute-start(bf16[112,960]{1,0:T(8,128)(2,1)S(1)} %fusion.56), channel_id=1, source_target_pairs={{0,2},{1,3},{2,0},{3,1},{4,6},{5,7},{6,4},{7,5},{8,10},{9,11},{10,... | collective-permute-start | bytes 645128 | tf_op jit(solution)/shard_map/ppermute | solution.py:101
  28.8 19.5 %collective-permute-start.9 = (bf16[112,960]{1,0:T(8,128)(2,1)S(1)}, bf16[112,960]{1,0:T(8,128)(2,1)S(1)}, u32[]{:S(2)}, u32[]{:S(2)}) collective-permute-start(bf16[112,960]{1,0:T(8,128)(2,1)S(1)} %fusion.56), channel_id=1, source_target_pairs={{0,3},{1,0},{2,1},{3,2},{4,7},{5,4},{6,5},{7,6},{8,11},{9,8},{10,9... | collective-permute-start | bytes 645128 | tf_op jit(solution)/shard_map/ppermute | solution.py:101
  32.9 19.5 %collective-permute-start.27 = (bf16[128,960]{1,0:T(8,128)(2,1)S(1)}, bf16[128,960]{1,0:T(8,128)(2,1)S(1)}, u32[]{:S(2)}, u32[]{:S(2)}) collective-permute-start(bf16[128,960]{1,0:T(8,128)(2,1)S(1)} %bitcast.149), channel_id=1, source_target_pairs={{0,4},{4,12},{8,20},{12,28},{16,24},{20,16},{24,8},{28,0},{1,5},{5... | collective-permute-start | bytes 737288 | tf_op jit(solution)/shard_map/ppermute | solution.py:101
  33.2 19.8 %collective-permute-start.22 = (bf16[3,32,1664]{2,1,0:T(8,128)(2,1)S(1)}, bf16[3,32,1664]{2,1,0:T(8,128)(2,1)S(1)}, u32[]{:S(2)}, u32[]{:S(2)}) collective-permute-start(bf16[3,32,1664]{2,1,0:T(8,128)(2,1)S(1)} %pad_maximum_fusion.8.refs_1_), channel_id=1, source_target_pairs={{0,4},{4,0},{8,12},{12,8},{16,20},{20,16},{24,28},{28,24},{1,5},{5... | collective-permute-start | bytes 958472 | tf_op jit(solution)/shard_map/ppermute | solution.py:101
  52.5 19.5 %collective-permute-start.10 = (bf16[3,112,960]{2,1,0:T(8,128)(2,1)}, bf16[3,112,960]{2,1,0:T(8,128)(2,1)}, u32[]{:S(2)}, u32[]{:S(2)}) collective-permute-start(bf16[3,112,960]{2,1,0:T(8,128)(2,1)} %pad_maximum_fusion.6.refs_2_), channel_id=1, source_target_pairs={{0,8},{4,12},{8,0},{12,4},{16,24},{20,28},{24,16},{28,20},{1,9},{5... | collective-permute-start | bytes 1935368 | tf_op jit(solution)/shard_map/ppermute | solution.py:101
  53.0 24.6 %collective-permute-start.11 = (bf16[3,112,960]{2,1,0:T(8,128)(2,1)}, bf16[3,112,960]{2,1,0:T(8,128)(2,1)}, u32[]{:S(2)}, u32[]{:S(2)}) collective-permute-start(bf16[3,112,960]{2,1,0:T(8,128)(2,1)} %pad_maximum_fusion.6.refs_2_), channel_id=1, source_target_pairs={{0,16},{4,20},{8,24},{12,28},{16,0},{20,4},{24,8},{28,12},{1,17},{... | collective-permute-start | bytes 1935368 | tf_op jit(solution)/shard_map/ppermute | solution.py:101
  64.2 22.4 %collective-permute-start.31 = (bf16[3,32,1664]{2,1,0:T(8,128)(2,1)S(1)}, bf16[3,32,1664]{2,1,0:T(8,128)(2,1)S(1)}, u32[]{:S(2)}, u32[]{:S(2)}) collective-permute-start(bf16[3,32,1664]{2,1,0:T(8,128)(2,1)S(1)} %collective-permute-done.23.refs_3_), channel_id=1, source_target_pairs={{0,4},{4,0},{8,12},{12,8},{16,20},{20,16},{24,28},{28,24},{1,5},{5... | collective-permute-start | bytes 958472 | tf_op jit(solution)/shard_map/ppermute | solution.py:101
  64.3 22.5 %collective-permute-start.32 = (bf16[3,32,1664]{2,1,0:T(8,128)(2,1)S(1)}, bf16[3,32,1664]{2,1,0:T(8,128)(2,1)S(1)}, u32[]{:S(2)}, u32[]{:S(2)}) collective-permute-start(bf16[3,32,1664]{2,1,0:T(8,128)(2,1)S(1)} %collective-permute-done.24.refs_4_), channel_id=1, source_target_pairs={{0,4},{4,0},{8,12},{12,8},{16,20},{20,16},{24,28},{28,24},{1,5},{5... | collective-permute-start | bytes 958472 | tf_op jit(solution)/shard_map/ppermute | solution.py:101
  68.3 19.7 %collective-permute-start.33 = (bf16[3,32,1664]{2,1,0:T(8,128)(2,1)S(1)}, bf16[3,32,1664]{2,1,0:T(8,128)(2,1)S(1)}, u32[]{:S(2)}, u32[]{:S(2)}) collective-permute-start(bf16[3,32,1664]{2,1,0:T(8,128)(2,1)S(1)} %collective-permute-done.25.refs_5_), channel_id=1, source_target_pairs={{0,4},{4,0},{8,12},{12,8},{16,20},{20,16},{24,28},{28,24},{1,5},{5... | collective-permute-start | bytes 958472 | tf_op jit(solution)/shard_map/ppermute | solution.py:101
  72.0 23.7 %collective-permute-start.18 = (bf16[32,5120]{1,0:T(8,128)(2,1)}, bf16[32,5120]{1,0:T(8,128)(2,1)S(1)}, u32[]{:S(2)}, u32[]{:S(2)}) collective-permute-start(bf16[32,5120]{1,0:T(8,128)(2,1)} %pad_dynamic-slice_fusion), channel_id=1, source_target_pairs={{0,2},{1,3},{2,0},{3,1},{4,6},{5,7},{6,4},{7,5},{8,10},{9,11},{10,... | collective-permute-start | bytes 983048 | tf_op jit(solution)/shard_map/ppermute | solution.py:101
  86.7 22.1 %collective-permute-start.14 = (bf16[3,112,960]{2,1,0:T(8,128)(2,1)}, bf16[3,112,960]{2,1,0:T(8,128)(2,1)}, u32[]{:S(2)}, u32[]{:S(2)}) collective-permute-start(bf16[3,112,960]{2,1,0:T(8,128)(2,1)} %pad_maximum_fusion.6.refs_2_), channel_id=1, source_target_pairs={{0,4},{4,0},{8,12},{12,8},{16,20},{20,16},{24,28},{28,24},{1,5},{5... | collective-permute-start | bytes 1935368 | tf_op jit(solution)/shard_map/ppermute | solution.py:101
  87.5 21.6 %collective-permute-start.15 = (bf16[3,112,960]{2,1,0:T(8,128)(2,1)}, bf16[3,112,960]{2,1,0:T(8,128)(2,1)}, u32[]{:S(2)}, u32[]{:S(2)}) collective-permute-start(bf16[3,112,960]{2,1,0:T(8,128)(2,1)} %collective-permute-done.10.refs_3_), channel_id=1, source_target_pairs={{0,4},{4,0},{8,12},{12,8},{16,20},{20,16},{24,28},{28,24},{1,5},{5... | collective-permute-start | bytes 1935368 | tf_op jit(solution)/shard_map/ppermute | solution.py:101
  88.0 23.1 %collective-permute-start.16 = (bf16[3,112,960]{2,1,0:T(8,128)(2,1)}, bf16[3,112,960]{2,1,0:T(8,128)(2,1)}, u32[]{:S(2)}, u32[]{:S(2)}) collective-permute-start(bf16[3,112,960]{2,1,0:T(8,128)(2,1)} %collective-permute-done.11.refs_4_), channel_id=1, source_target_pairs={{0,4},{4,0},{8,12},{12,8},{16,20},{20,16},{24,28},{28,24},{1,5},{5... | collective-permute-start | bytes 1935368 | tf_op jit(solution)/shard_map/ppermute | solution.py:101
  112.2 50.7 %collective-permute-start.20 = (bf16[3,32,5120]{2,1,0:T(8,128)(2,1)}, bf16[3,32,5120]{2,1,0:T(8,128)(2,1)}, u32[]{:S(2)}, u32[]{:S(2)}) collective-permute-start(bf16[3,32,5120]{2,1,0:T(8,128)(2,1)} %pad_maximum_fusion.3.refs_1_), channel_id=1, source_target_pairs={{0,8},{4,12},{8,0},{12,4},{16,24},{20,28},{24,16},{28,20},{1,9},{5... | collective-permute-start | bytes 2949128 | tf_op jit(solution)/shard_map/ppermute | solution.py:101
  114.1 48.7 %collective-permute-start.21 = (bf16[3,32,5120]{2,1,0:T(8,128)(2,1)}, bf16[3,32,5120]{2,1,0:T(8,128)(2,1)}, u32[]{:S(2)}, u32[]{:S(2)}) collective-permute-start(bf16[3,32,5120]{2,1,0:T(8,128)(2,1)} %pad_maximum_fusion.3.refs_1_), channel_id=1, source_target_pairs={{0,16},{4,20},{8,24},{12,28},{16,0},{20,4},{24,8},{28,12},{1,17},{... | collective-permute-start | bytes 2949128 | tf_op jit(solution)/shard_map/ppermute | solution.py:101
  541.8 19.5 %collective-permute-start.76 = (bf16[4,2,640,128]{3,2,1,0:T(8,128)(2,1)}, bf16[4,2,640,128]{3,2,1,0:T(8,128)(2,1)}, u32[]{:S(2)}, u32[]{:S(2)}) collective-permute-start(bf16[4,2,640,128]{3,2,1,0:T(8,128)(2,1)} %get-tuple-element.566), channel_id=1, source_target_pairs={{0,4},{4,0},{8,12},{12,8},{16,20},{20,16},{24,28},{28,24},{1,5},{5... | collective-permute-start | bytes 3932168 | tf_op jit(solution)/shard_map/ppermute | solution.py:101
  561.2 21.3 %collective-permute-start.80 = (bf16[4,4,32,5120]{3,2,1,0:T(8,128)(2,1)}, bf16[4,4,32,5120]{3,2,1,0:T(8,128)(2,1)}, u32[]{:S(2)}, u32[]{:S(2)}) collective-permute-start(bf16[4,4,32,5120]{3,2,1,0:T(8,128)(2,1)} %get-tuple-element.573), channel_id=1, source_target_pairs={{0,4},{4,0},{8,12},{12,8},{16,20},{20,16},{24,28},{28,24},{1,5},{5... | collective-permute-start | bytes 15728648 | tf_op jit(solution)/shard_map/ppermute | solution.py:101
  588.5 32.5 %collective-permute-start.83 = (bf16[4,4,112,960]{3,2,1,0:T(8,128)(2,1)}, bf16[4,4,112,960]{3,2,1,0:T(8,128)(2,1)}, u32[]{:S(2)}, u32[]{:S(2)}) collective-permute-start(bf16[4,4,112,960]{3,2,1,0:T(8,128)(2,1)} %get-tuple-element.582), channel_id=1, source_target_pairs={{0,4},{4,0},{8,12},{12,8},{16,20},{20,16},{24,28},{28,24},{1,5},{5... | collective-permute-start | bytes 10321928 | tf_op jit(solution)/shard_map/ppermute | solution.py:101
  588.5 31.5 %collective-permute-start.81 = (bf16[2,2,32,5120]{3,2,1,0:T(8,128)(2,1)}, bf16[2,2,32,5120]{3,2,1,0:T(8,128)(2,1)}, u32[]{:S(2)}, u32[]{:S(2)}) collective-permute-start(bf16[2,2,32,5120]{3,2,1,0:T(8,128)(2,1)} %pad_maximum_fusion), channel_id=1, source_target_pairs={{0,8},{4,12},{8,0},{12,4},{16,24},{20,28},{24,16},{28,20},{1,9},{5... | collective-permute-start | bytes 3932168 | tf_op jit(solution)/shard_map/ppermute | solution.py:101
  589.7 31.2 %collective-permute-start.82 = (bf16[2,2,32,5120]{3,2,1,0:T(8,128)(2,1)}, bf16[2,2,32,5120]{3,2,1,0:T(8,128)(2,1)}, u32[]{:S(2)}, u32[]{:S(2)}) collective-permute-start(bf16[2,2,32,5120]{3,2,1,0:T(8,128)(2,1)} %pad_maximum_fusion.1), channel_id=1, source_target_pairs={{0,16},{4,20},{8,24},{12,28},{16,0},{20,4},{24,8},{28,12},{1,17},{... | collective-permute-start | bytes 3932168 | tf_op jit(solution)/shard_map/ppermute | solution.py:101
  620.9 21.5 %collective-permute-start.86 = (bf16[4,4,32,1664]{3,2,1,0:T(8,128)(2,1)}, bf16[4,4,32,1664]{3,2,1,0:T(8,128)(2,1)S(1)}, u32[]{:S(2)}, u32[]{:S(2)}) collective-permute-start(bf16[4,4,32,1664]{3,2,1,0:T(8,128)(2,1)} %get-tuple-element.608), channel_id=1, source_target_pairs={{0,4},{4,0},{8,12},{12,8},{16,20},{20,16},{24,28},{28,24},{1,5},{5... | collective-permute-start | bytes 5111816 | tf_op jit(solution)/shard_map/ppermute | solution.py:101
  642.5 36.4 %collective-permute-start.87 = (bf16[2,2,112,960]{3,2,1,0:T(8,128)(2,1)}, bf16[2,2,112,960]{3,2,1,0:T(8,128)(2,1)}, u32[]{:S(2)}, u32[]{:S(2)}) collective-permute-start(bf16[2,2,112,960]{3,2,1,0:T(8,128)(2,1)} %pad_maximum_fusion.4), channel_id=1, source_target_pairs={{0,8},{4,12},{8,0},{12,4},{16,24},{20,28},{24,16},{28,20},{1,9},{5... | collective-permute-start | bytes 2580488 | tf_op jit(solution)/shard_map/ppermute | solution.py:101
  643.6 35.3 %collective-permute-start.88 = (bf16[2,2,112,960]{3,2,1,0:T(8,128)(2,1)}, bf16[2,2,112,960]{3,2,1,0:T(8,128)(2,1)}, u32[]{:S(2)}, u32[]{:S(2)}) collective-permute-start(bf16[2,2,112,960]{3,2,1,0:T(8,128)(2,1)} %pad_maximum_fusion.5), channel_id=1, source_target_pairs={{0,16},{4,20},{8,24},{12,28},{16,0},{20,4},{24,8},{28,12},{1,17},{... | collective-permute-start | bytes 2580488 | tf_op jit(solution)/shard_map/ppermute | solution.py:101
  649.3 23.9 %collective-permute-start.107 = (bf16[32,5120]{1,0:T(8,128)(2,1)S(1)}, bf16[32,5120]{1,0:T(8,128)(2,1)S(1)}, u32[]{:S(2)}, u32[]{:S(2)}) collective-permute-start(bf16[32,5120]{1,0:T(8,128)(2,1)S(1)} %get-tuple-element.645), channel_id=1, source_target_pairs={{0,2},{1,3},{2,0},{3,1},{4,6},{5,7},{6,4},{7,5},{8,10},{9,11},{10,... | collective-permute-start | bytes 983048 | tf_op jit(solution)/shard_map/ppermute | solution.py:101
  652.6 22.0 %collective-permute-start.108 = (bf16[32,5120]{1,0:T(8,128)(2,1)S(1)}, bf16[32,5120]{1,0:T(8,128)(2,1)}, u32[]{:S(2)}, u32[]{:S(2)}) collective-permute-start(bf16[32,5120]{1,0:T(8,128)(2,1)S(1)} %get-tuple-element.646), channel_id=1, source_target_pairs={{0,3},{1,0},{2,1},{3,2},{4,7},{5,4},{6,5},{7,6},{8,11},{9,8},{10,9... | collective-permute-start | bytes 983048 | tf_op jit(solution)/shard_map/ppermute | solution.py:101
  688.7 18.6 %collective-permute-start.109 = (bf16[32,5120]{1,0:T(8,128)(2,1)S(1)}, bf16[32,5120]{1,0:T(8,128)(2,1)S(1)}, u32[]{:S(2)}, u32[]{:S(2)}) collective-permute-start(bf16[32,5120]{1,0:T(8,128)(2,1)S(1)} %fusion.10.refs_0_), channel_id=1, source_target_pairs={{0,4},{4,0},{8,12},{12,8},{16,20},{20,16},{24,28},{28,24},{1,5},{5... | collective-permute-start | bytes 983048 | tf_op jit(solution)/shard_map/ppermute | solution.py:101
  688.7 19.2 %collective-permute-start.110 = (bf16[32,5120]{1,0:T(8,128)(2,1)S(1)}, bf16[32,5120]{1,0:T(8,128)(2,1)S(1)}, u32[]{:S(2)}, u32[]{:S(2)}) collective-permute-start(bf16[32,5120]{1,0:T(8,128)(2,1)S(1)} %fusion.10.refs_0_), channel_id=1, source_target_pairs={{0,8},{4,12},{8,0},{12,4},{16,24},{20,28},{24,16},{28,20},{1,9},{5... | collective-permute-start | bytes 983048 | tf_op jit(solution)/shard_map/ppermute | solution.py:101
  688.8 19.1 %collective-permute-start.111 = (bf16[32,5120]{1,0:T(8,128)(2,1)S(1)}, bf16[32,5120]{1,0:T(8,128)(2,1)S(1)}, u32[]{:S(2)}, u32[]{:S(2)}) collective-permute-start(bf16[32,5120]{1,0:T(8,128)(2,1)S(1)} %fusion.10.refs_0_), channel_id=1, source_target_pairs={{0,16},{4,20},{8,24},{12,28},{16,0},{20,4},{24,8},{28,12},{1,17},{... | collective-permute-start | bytes 983048 | tf_op jit(solution)/shard_map/ppermute | solution.py:101
  707.3 21.9 %collective-permute-start.93 = (bf16[4,32,1664]{2,1,0:T(8,128)(2,1)S(1)}, bf16[4,32,1664]{2,1,0:T(8,128)(2,1)S(1)}, u32[]{:S(2)}, u32[]{:S(2)}) collective-permute-start(bf16[4,32,1664]{2,1,0:T(8,128)(2,1)S(1)} %get-tuple-element.623), channel_id=1, source_target_pairs={{0,8},{4,12},{8,0},{12,4},{16,24},{20,28},{24,16},{28,20},{1,9},{5... | collective-permute-start | bytes 1277960 | tf_op jit(solution)/shard_map/ppermute | solution.py:101
  707.9 21.7 %collective-permute-start.94 = (bf16[4,32,1664]{2,1,0:T(8,128)(2,1)S(1)}, bf16[4,32,1664]{2,1,0:T(8,128)(2,1)S(1)}, u32[]{:S(2)}, u32[]{:S(2)}) collective-permute-start(bf16[4,32,1664]{2,1,0:T(8,128)(2,1)S(1)} %get-tuple-element.624), channel_id=1, source_target_pairs={{0,16},{4,20},{8,24},{12,28},{16,0},{20,4},{24,8},{28,12},{1,17},{... | collective-permute-start | bytes 1277960 | tf_op jit(solution)/shard_map/ppermute | solution.py:101
  707.9 21.7 %collective-permute-start.95 = (bf16[4,32,1664]{2,1,0:T(8,128)(2,1)S(1)}, bf16[4,32,1664]{2,1,0:T(8,128)(2,1)S(1)}, u32[]{:S(2)}, u32[]{:S(2)}) collective-permute-start(bf16[4,32,1664]{2,1,0:T(8,128)(2,1)S(1)} %get-tuple-element.625), channel_id=1, source_target_pairs={{0,24},{4,28},{8,16},{12,20},{16,8},{20,12},{24,0},{28,4},{1,25},{... | collective-permute-start | bytes 1277960 | tf_op jit(solution)/shard_map/ppermute | solution.py:101
  (282 other events, 2761.7 us)

commit v4 on v3

--- a/solution.py
+++ b/solution.py
@@ -21,7 +21,7 @@
 KV_COLS = 640
 ALL_COLS = Q_COLS + KV_COLS
 PAD_Q = HEADS * LANES
-KEYS = 512
+KEYS = 1024
 FF_BLOCK = 512
 FAR = 1 << 30
 LOW = -1e30
@@ -31,6 +31,7 @@
 F32 = jnp.float32
 ANY = pl.BlockSpec(memory_space=pltpu.HBM)
 VMEM = pl.BlockSpec(memory_space=pltpu.VMEM)
+SMEM = pl.BlockSpec(memory_space=pltpu.SMEM)
 MIB = 1 << 20
 
 
@@ -409,44 +410,78 @@
     )
 
 
-def kv_copies(spots, segments, kv_ref, sems, size, rank, half):
+def kv_copies(spots, segments, kv_ref, sems, size, rank, half, cap):
     copies = []
     for (m, first, n), segment in zip(spots, segments):
         for start in range(first, first + n, half):
             owner = rank ^ m
             chunk = owner if start == 0 else 2 * size - 1 - owner
-            at = pl.multiple_of(chunk * half, half)
+            at = pl.multiple_of(chunk * cap, cap)
             copies.append(
-                pltpu.make_async_copy(segment.at[pl.ds(start - first, half)], kv_ref.at[pl.ds(at, half)], sems.at[len(copies)])
+                pltpu.make_async_copy(segment.at[pl.ds(start - first, cap)], kv_ref.at[pl.ds(at, cap)], sems.at[len(copies)])
             )
     return copies
 
 
-def key_index(depth_ref, kb, step_no):
-    depth = depth_ref[pl.ds(kb, 1), :]
-    return jnp.where(depth > step_no, lane_of(depth.shape) + kb * KEYS, FAR)
+def key_index(keys_ref, kb, step_no, cap, half):
+    blocks = keys_ref.shape[0] // 3
+    base, to_depth = (0, blocks) if cap == half else (2 * blocks, blocks // 2)
+    depth = keys_ref[pl.ds(base + to_depth + kb, 1), :]
+    return jnp.where(depth > step_no, keys_ref[pl.ds(base + kb, 1), :], FAR)
+
+
+def by_cap(flag_ref, step_no, half, body):
+    few = flag_ref[0, step_no] > 0
+
+    @pl.when(few)
+    def _():
+        body(half // 2)
+
+    @pl.when(jnp.logical_not(few))
+    def _():
+        body(half)
 
 
 def chunk_of(a, rank, size):
     return jnp.where(a == 0, rank, 2 * size - 1 - rank)
 
 
+def head_cols(h, heads=1):
+    return pl.ds(pl.multiple_of(h * heads * LANES, LANES), heads * LANES)
+
+
 def stack3(ref, at, half, h):
-    return jnp.concatenate(
-        [ref[pl.ds(at, half), LANES * (GROUPED * h + g) : LANES * (GROUPED * h + g + 1)] for g in range(GROUPED)], axis=0
-    )
-
-
-def attend_kernel(spots, size, step_no, q_ref, tj_ref, meta_ref, *refs):
+    x = ref[pl.ds(at, half), head_cols(h, GROUPED)]
+    return jnp.concatenate([x[:, LANES * g : LANES * (g + 1)] for g in range(GROUPED)], axis=0)
+
+
+def beside3(x, half):
+    return jnp.concatenate([x[g * half : (g + 1) * half] for g in range(GROUPED)], axis=1)
+
+
+def attend_kernel(spots, size, step_no, flag_ref, q_ref, keys_ref, meta_ref, *refs):
     segments, (o_ref, l_ref, kv_ref, kv1_ref, sems) = refs[: len(spots)], refs[len(spots) :]
+    half = q_ref.shape[0] // 2
+    by_cap(
+        flag_ref,
+        step_no,
+        half,
+        functools.partial(
+            attend_body, spots, size, step_no, q_ref, keys_ref, meta_ref, segments, o_ref, l_ref, kv_ref, kv1_ref, sems, half
+        ),
+    )
+
+
+def attend_body(
+    spots, size, step_no, q_ref, keys_ref, meta_ref, segments, o_ref, l_ref, kv_ref, kv1_ref, sems, half, cap
+):
     rank = lax.axis_index("dp")
-    half = q_ref.shape[0] // 2
-    copies = kv_copies(spots, segments, kv_ref, sems, size, rank, half)
+    copies = kv_copies(spots, segments, kv_ref, sems, size, rank, half, cap)
     for c in copies:
         c.start()
     for c in copies:
         c.wait()
-    blocks = tj_ref.shape[0]
+    rows = GROUPED * cap
 
     def ones(i, _):
         at = pl.ds(pl.multiple_of(i * KEYS, KEYS), KEYS)
@@ -456,23 +491,25 @@
             kv1_ref[at, cols] = jnp.where(lane_of(x.shape) < HEAD, jnp.ones_like(x), x)
         return 0
 
-    lax.fori_loop(0, blocks, ones, 0)
+    lax.fori_loop(0, 2 * size * cap // KEYS, ones, 0)
 
     def one(a, _):
         at = pl.multiple_of(a * half, half)
-        used = lax.div(chunk_of(a, rank, size) * half + half + KEYS - 1, KEYS)
-        ti = jnp.concatenate([meta_ref[pl.ds(at, half), 0:1]] * GROUPED, axis=0)
-        si = jnp.concatenate([meta_ref[pl.ds(at, half), 1:2]] * GROUPED, axis=0)
-        lanes = lane_of((GROUPED * half, LANES))
-        logs = jnp.zeros((GROUPED * half, LANES), F32)
-        for h in range(KV_HEADS):
-            cols = slice(LANES * h, LANES * (h + 1))
-            q3 = stack3(q_ref, at, half, h)
+        used = lax.div(chunk_of(a, rank, size) * cap + cap + KEYS - 1, KEYS)
+        ti = jnp.concatenate([meta_ref[pl.ds(at, cap), 0:1]] * GROUPED, axis=0)
+        si = jnp.concatenate([meta_ref[pl.ds(at, cap), 1:2]] * GROUPED, axis=0)
+        lanes = lane_of((rows, LANES))
+        if cap < half:
+            o_ref[pl.ds(at + cap, half - cap), :] = jnp.zeros((half - cap, PAD_Q), BF)
+
+        def head(h, logs):
+            cols = head_cols(h)
+            q3 = stack3(q_ref, at, cap, h)
 
             def block(kb, carry):
                 top, acc = carry
                 keys = pl.ds(pl.multiple_of(kb * KEYS, KEYS), KEYS)
-                tj = key_index(tj_ref, kb, step_no)
+                tj = key_index(keys_ref, kb, step_no, cap, half)
                 s = dot_nt(q3, kv_ref[keys, cols])
                 s = jnp.where((tj <= ti) & (tj >= si), s, LOW)
                 new = jnp.maximum(top, jnp.max(s, axis=-1, keepdims=True))
@@ -481,35 +518,33 @@
                 return new, acc
 
             top, acc = lax.fori_loop(
-                0,
-                used,
-                block,
-                (jnp.full((GROUPED * half, 1), START_MAX, F32), jnp.zeros((GROUPED * half, LANES), F32)),
+                0, used, block, (jnp.full((rows, 1), START_MAX, F32), jnp.zeros((rows, LANES), F32))
             )
             total = acc[:, 0:1]
             some = total > 0.0
             safe = jnp.where(some, total, 1.0)
-            o = jnp.where((lanes >= HEAD) & some, acc / safe, 0.0).astype(BF)
-            logs = jnp.where(lanes == h, top + jnp.log(safe), logs)
-            for g in range(GROUPED):
-                o_ref[pl.ds(at, half), LANES * (GROUPED * h + g) : LANES * (GROUPED * h + g + 1)] = o[g * half : (g + 1) * half]
-        l_ref[a] = logs
+            o = jnp.where((lanes >= HEAD) & some, acc / safe, 0.0)
+            o_ref[pl.ds(at, cap), head_cols(h, GROUPED)] = beside3(o, cap).astype(BF)
+            return jnp.where(lanes == h, top + jnp.log(safe), logs)
+
+        logs = lax.fori_loop(0, KV_HEADS, head, jnp.zeros((rows, LANES), F32))
+        l_ref[a, 0:rows, :] = logs
         return 0
 
     lax.fori_loop(0, 2, one, 0)
 
 
-def attend(q, segments, tj, meta, step_no, size):
+def attend(flags, q, segments, keys, meta, step_no, size):
     rows = q.shape[0]
     half = rows // 2
-    total = tj.size
+    total = keys.size // 3
     spots = [s[:3] for s in segments]
-    n = sum(s[1] // half for s in [(0, x[2]) for x in spots])
+    n = sum(x[2] // half for x in spots)
     return call(
         functools.partial(attend_kernel, spots, size, step_no),
         [shaped(rows, PAD_Q, dtype=BF), shaped(2, GROUPED * half, LANES)],
-        [q, tj, meta, *[s[3] for s in segments]],
-        [VMEM] * 3 + [ANY] * len(segments),
+        [flags, q, keys, meta, *[s[3] for s in segments]],
+        [SMEM] + [VMEM] * 3 + [ANY] * len(segments),
         [pltpu.VMEM((total, KV_COLS), BF), pltpu.VMEM((total, KV_COLS), BF), pltpu.SemaphoreType.DMA((n,))],
         4 * rows * total * HEADS * LANES // 2,
         32,
@@ -690,43 +725,54 @@
     )
 
 
-def attend_back_kernel(spots, size, step_no, q_ref, o_ref, dob_ref, l_ref, tj_ref, meta_ref, cos_ref, sin_ref, *refs):
+def attend_back_kernel(spots, size, step_no, flag_ref, q_ref, *refs):
+    half = q_ref.shape[0] // 2
+    by_cap(
+        flag_ref, step_no, half, functools.partial(attend_back_body, spots, size, step_no, half, (q_ref, *refs))
+    )
+
+
+def attend_back_body(spots, size, step_no, half, refs, cap):
+    q_ref, o_ref, dob_ref, l_ref, keys_ref, meta_ref, cos_ref, sin_ref, *refs = refs
     segments, refs = refs[: len(spots)], refs[len(spots) :]
     dq_ref, even_ref, odd_ref, kv_ref, dkv_ref, wide_ref, sems = refs
     rank = lax.axis_index("dp")
-    half = q_ref.shape[0] // 2
-    copies = kv_copies(spots, segments, kv_ref, sems, size, rank, half)
+    rows = GROUPED * cap
+    copies = kv_copies(spots, segments, kv_ref, sems, size, rank, half, cap)
     for c in copies:
         c.start()
-    blocks = tj_ref.shape[0]
 
     def clear(kb, _):
         for h in range(KV_HEADS):
             dkv_ref[kb, LANES * h : LANES * (h + 1), :] = jnp.zeros((LANES, KEYS), F32)
         return 0
 
-    lax.fori_loop(0, blocks, clear, 0)
+    lax.fori_loop(0, 2 * size * cap // KEYS, clear, 0)
     for c in copies:
         c.wait()
 
     def one(a, _):
         at = pl.multiple_of(a * half, half)
-        used = lax.div(chunk_of(a, rank, size) * half + half + KEYS - 1, KEYS)
-        ti = jnp.concatenate([meta_ref[pl.ds(at, half), 0:1]] * GROUPED, axis=0)
-        si = jnp.concatenate([meta_ref[pl.ds(at, half), 1:2]] * GROUPED, axis=0)
-        logs = l_ref[a]
-        for h in range(KV_HEADS):
-            cols = slice(LANES * h, LANES * (h + 1))
-            q3 = stack3(q_ref, at, half, h)
-            do3 = stack3(dob_ref, at, half, h)
-            o3 = stack3(o_ref, at, half, h)
+        used = lax.div(chunk_of(a, rank, size) * cap + cap + KEYS - 1, KEYS)
+        ti = jnp.concatenate([meta_ref[pl.ds(at, cap), 0:1]] * GROUPED, axis=0)
+        si = jnp.concatenate([meta_ref[pl.ds(at, cap), 1:2]] * GROUPED, axis=0)
+        logs = l_ref[a, 0:rows, :]
+        if cap < half:
+            wide_ref[pl.ds(at + cap, half - cap), :] = jnp.zeros((half - cap, PAD_Q), F32)
+        lanes = lane_of(logs.shape)
+
+        def head(h, _):
+            cols = head_cols(h)
+            q3 = stack3(q_ref, at, cap, h)
+            do3 = stack3(dob_ref, at, cap, h)
+            o3 = stack3(o_ref, at, cap, h)
             delta = jnp.sum(do3.astype(F32) * o3.astype(F32), axis=-1, keepdims=True)
-            log3 = logs[:, h : h + 1]
-            both_t = jnp.concatenate([q3.astype(F32).T, do3.astype(F32).T], axis=1).astype(BF)
+            log3 = jnp.sum(jnp.where(lanes == h, logs, 0.0), axis=-1, keepdims=True)
+            both_t = jnp.concatenate([q3.astype(F32), do3.astype(F32)], axis=0).T.astype(BF)
 
             def block(kb, acc):
                 keys = pl.ds(pl.multiple_of(kb * KEYS, KEYS), KEYS)
-                tj = key_index(tj_ref, kb, step_no)
+                tj = key_index(keys_ref, kb, step_no, cap, half)
                 kv = kv_ref[keys, cols]
                 s = dot_nt(q3, kv)
                 p = jnp.exp(jnp.where((tj <= ti) & (tj >= si), s - log3, LOW))
@@ -736,9 +782,11 @@
                 dkv_ref[kb, cols, :] += dot(both_t, both)
                 return acc + dot(ds, kv)
 
-            acc = lax.fori_loop(0, used, block, jnp.zeros((GROUPED * half, LANES), F32))
-            for g in range(GROUPED):
-                wide_ref[pl.ds(at, half), LANES * (GROUPED * h + g) : LANES * (GROUPED * h + g + 1)] = acc[g * half : (g + 1) * half]
+            acc = lax.fori_loop(0, used, block, jnp.zeros((rows, LANES), F32))
+            wide_ref[pl.ds(at, cap), head_cols(h, GROUPED)] = beside3(acc, cap)
+            return 0
+
+        lax.fori_loop(0, KV_HEADS, head, 0)
         return 0
 
     lax.fori_loop(0, 2, one, 0)
@@ -750,22 +798,35 @@
         other = pltpu.roll(wide_ref[:, LANES * (2 * b + 1) : LANES * (2 * b + 2)], HEAD, 1) if 2 * b + 1 < HEADS else 0.0
         x = jnp.where(low, x, other) * SCALE
         dq_ref[:, LANES * b : LANES * (b + 1)] = (x * cos - swap_halves(x, lanes) * sin).astype(BF)
-    per = KEYS // half
-    for chunk in range(2 * size):
-        owner = min(chunk, 2 * size - 1 - chunk)
-        side = 0 if chunk < size else 1
-        m = rank ^ owner
-        at = (chunk % per) * half
-        for par, ref in ((0, even_ref), (1, odd_ref)):
-            @pl.when(lax.rem(m, 2) == par)
-            def _(ref=ref):
-                ref[lax.div(m, 2), side] = dkv_ref[chunk // per, :, at : at + half].astype(BF)
-
-
-def attend_back(q, o, dob, logs, tj, meta, step_no, cos, sin, segments, size):
+    per = KEYS // cap
+
+    def hand_out(kb, _):
+        for i in range(per):
+            chunk = kb * per + i
+            owner = jnp.minimum(chunk, 2 * size - 1 - chunk)
+            side = (chunk >= size).astype(jnp.int32)
+            m = rank ^ owner
+            at = i * cap
+            tile, shift = at // half * half, at % half
+            x = dkv_ref[kb, :, tile : tile + half]
+            if shift:
+                x = pltpu.roll(x, half - shift, 1)
+            if cap < half:
+                x = jnp.where(lane_of(x.shape) < cap, x, 0.0)
+            for par, ref in ((0, even_ref), (1, odd_ref)):
+
+                @pl.when(lax.rem(m, 2) == par)
+                def _(ref=ref, x=x):
+                    ref[lax.div(m, 2), side] = x.astype(BF)
+        return 0
+
+    lax.fori_loop(0, 2 * size * cap // KEYS, hand_out, 0)
+
+
+def attend_back(flags, q, o, dob, logs, keys, meta, step_no, cos, sin, segments, size):
     rows = q.shape[0]
     half = rows // 2
-    total = tj.size
+    total = keys.size // 3
     spots = [s[:3] for s in segments]
     n = sum(x[2] // half for x in spots)
     pairs_n = max(size // 2, 1)
@@ -776,8 +837,8 @@
             shaped(pairs_n, 2, KV_COLS, half, dtype=BF),
             shaped(pairs_n, 2, KV_COLS, half, dtype=BF),
         ],
-        [q, o, dob, logs, tj, meta, cos, sin, *[s[3] for s in segments]],
-        [VMEM] * 8 + [ANY] * len(segments),
+        [flags, q, o, dob, logs, keys, meta, cos, sin, *[s[3] for s in segments]],
+        [SMEM] + [VMEM] * 8 + [ANY] * len(segments),
         [
             pltpu.VMEM((total, KV_COLS), BF),
             pltpu.VMEM((total // KEYS, KV_COLS, KEYS), F32),
@@ -1012,23 +1073,39 @@
     extras = jnp.transpose(extras, (1, 0, 2)).reshape(5, D)
     gain_one, gain_two = extras[0:1], extras[1:2]
 
-    hidden = zigged(token_moves, rank).astype(F32)
     depth_all = jnp.concatenate([x for _, _, _, x in sorted(get_depth.segments(), key=lambda x: x[0])], axis=0).astype(F32)
     order = (rank ^ jnp.arange(size)[:, None]) == jnp.arange(size)[None, :]
     depth_all = jnp.dot(order.astype(F32), depth_all, precision=lax.Precision.HIGHEST)
     depth_all = depth_all.astype(jnp.int32).reshape(group_rows)
-    index = jnp.arange(group_rows, dtype=jnp.int32)
+    chunks = depth_all.reshape(2 * size, half)
+    earlier = jnp.arange(half)[None, :] < jnp.arange(half)[:, None]
+    other, own = chunks[:, None, :], chunks[:, :, None]
+    place = jnp.sum(((other > own) | ((other == own) & earlier[None])).astype(jnp.int32), axis=2)
+    at_place = place[:, None, :] == jnp.arange(half)[None, :, None]
+    index = jnp.sum(jnp.where(at_place, jnp.arange(group_rows, dtype=jnp.int32).reshape(2 * size, 1, half), 0), axis=2)
+    depth_all = jnp.sum(jnp.where(at_place, other, 0), axis=2)
     lengths_here = lengths[0]
     ends = [jnp.sum(lengths_here[: i + 1]) for i in range(lengths_here.shape[0])]
-    start = functools.reduce(jnp.add, [jnp.where(index >= e, lengths_here[i], 0) for i, e in enumerate(ends)])
     mine = lambda x: jnp.concatenate(
-        [
-            lax.dynamic_slice_in_dim(x, rank * half, half),
-            lax.dynamic_slice_in_dim(x, (2 * size - 1 - rank) * half, half),
-        ]
-    )
-    index_here, start_here, depth_here = mine(index), mine(start), mine(depth_all)
-    depth_rows = depth_all.reshape(group_rows // KEYS, KEYS)
+        [lax.dynamic_slice_in_dim(x, rank, 1), lax.dynamic_slice_in_dim(x, 2 * size - 1 - rank, 1)]
+    )
+    index_here, depth_here = mine(index).reshape(rows), mine(depth_all).reshape(rows)
+    start_here = functools.reduce(
+        jnp.add, [jnp.where(index_here >= e, lengths_here[i], 0) for i, e in enumerate(ends)]
+    )
+    sorting = (mine(place)[:, None, :] == jnp.arange(half)[None, :, None]).astype(BF)
+    arrange = lambda x: jnp.einsum("cpi,cid->cpd", sorting, x.reshape(2, half, D), preferred_element_type=F32).reshape(rows, D)
+    restore = lambda x: jnp.einsum(
+        "cpi,cpd->cid", sorting, x.astype(BF).reshape(2, half, D), preferred_element_type=F32
+    ).astype(BF).reshape(rows, D)
+    hidden = arrange(zigged(token_moves, rank))
+    counts = jnp.sum((depth_all[None] > jnp.arange(STEPS)[:, None, None]).astype(jnp.int32), axis=2)
+    flags = (jnp.max(counts, axis=1) <= half // 2).astype(jnp.int32)[None]
+    blocks = group_rows // KEYS
+    front = lambda x: x[:, : half // 2].reshape(blocks // 2, KEYS)
+    key_rows = jnp.concatenate(
+        [index.reshape(blocks, KEYS), depth_all.reshape(blocks, KEYS), front(index), front(depth_all)], axis=0
+    )
     meta = jnp.stack([index_here, start_here, depth_here] + [jnp.zeros_like(index_here)] * 5, axis=1)
     frequency = jnp.exp(jnp.arange(HEAD // 2, dtype=F32) * (-2.0 * math.log(10000.0) / HEAD))
     angles = (index_here - start_here).astype(F32)[:, None] * frequency[None, :]
@@ -1062,7 +1139,7 @@
                 flow.start((get_kv, 2))
                 flow.wait((get_kv, 2))
         segments = get_kv.segments()
-        o, logs = attend(q, segments, depth_rows, meta, r, size)
+        o, logs = attend(flags, q, segments, key_rows, meta, r, size)
         if r == 0:
             w_od = get_od.whole()
             (o, w_od) = flow.wait((get_gu, 1), also=(o, w_od))
@@ -1074,10 +1151,10 @@
         ob, m, n2, gu_saved, g, new = post(o, hidden, gain_two, extras[2 + r : 3 + r], meta, r, w_od, w_gu)
         saved.append((hidden, n1, q, segments, o, logs, ob, m, n2, gu_saved, g, new))
         hidden = new
-    out_moves = unzig(hidden.astype(BF), size, rank)
+    out_moves = unzig(restore(hidden), size, rank)
     flow.start((out_moves, 0))
 
-    dh = zigged(cotangent_moves, rank).astype(F32)
+    dh = arrange(zigged(cotangent_moves, rank))
     kept = [None] * STEPS
     gains_one, gains_two, routers = [], [], [None] * STEPS
     for r in reversed(range(STEPS)):
@@ -1085,7 +1162,7 @@
         dfb, dgu, inner, dm, datt, dob, dz, sums = ffn_back(dh, hidden, new, g, meta, r, gu_saved, m, gain_two, w_od, w_gu)
         routers[r] = sums[0]
         gains_two.append(sums[1])
-        dq, even, odd = attend_back(q, o, dob, logs, depth_rows, meta, r, cos, sin, segments, size)
+        dq, even, odd = attend_back(flags, q, o, dob, logs, key_rows, meta, r, cos, sin, segments, size)
         sum_kv = Fold(even, odd, size, True)
         flow.start((sum_kv, 0))
         if r == 0:
@@ -1115,7 +1192,7 @@
         parts = sum_kv.terms()
         dp, dh, gain_sum = qkv_back(dq, parts, cos, sin, hidden, dh, dm, dz, extras[2 + r : 3 + r], gain_one, w_q)
         if r == 0:
-            in_moves = unzig(dh.astype(BF), size, rank)
+            in_moves = unzig(restore(dh), size, rank)
             flow.start((in_moves, 0))
         gains_one.append(gain_sum[0])
         kept[r] = dict(n1=n1, n2=n2, ob=ob, dgu=dgu, inner=inner, dfb=dfb, datt=datt, dp=dp)

time: 787 us -> 753 us (0.957)
  Pallas kernels: 291 us -> 263 us
  local copies, waits for them, and re-layouts: 103 us -> 91.8 us
    pallas_call x27, Pallas kernels: 291 us -> 263 us  [call(): pl.pallas_call(kernel, out_shape=outs, in_specs=specs, out_specs=out_spec...]
    unnamed x385 -> x344, local copies, waits for them, and re-layouts: 77.5 us -> 68.2 us
  transfers between devices with their start and end apart: 126 -> 126, of which waited for: 42 -> 41; matrix products, arithmetic and copies ran while one was open for 9% -> 9% of each run, Pallas kernels for 10% -> 11%
where the time goes in v4:
time: 753 us; the launch traced here: 743 us
  Pallas kernels  263 us (35%)
  waiting for transfers between devices  178 us (24%)
  starting transfers between devices  149 us (20%)
  local copies, waits for them, and re-layouts  91.8 us (12%)
  other arithmetic  54.2 us (7%)
    pallas_call x27, Pallas kernels, call(): pl.pallas_call(kernel, out_shape=outs, in_specs=specs, out_specs=out_spec...  263 us
    ppermute x126, waiting for transfers between devices, start(): lax.ppermute(x, axis, perm)  178 us
    ppermute x126, starting transfers between devices, start(): lax.ppermute(x, axis, perm)  149 us
    unnamed x344, local copies, waits for them, and re-layouts  68.2 us
  transfers between devices with their start and end apart: 126, of which 41 were waited for; matrix products, arithmetic and copies ran while one was open for 9% of the time, Pallas kernels for 11%

profile of v4, /device:TPU:0, one launch (start us, length us, event | category | flops | bytes accessed | tf_op | source)
XLA Modules:
  0.0 742.6 jit_solution(16438429275515633834)
XLA Ops:
  37.1 6.9 collective-permute-done.17
  112.4 9.1 %collective-permute-done.36.refs_3_.refs_10_ = bf16[256,640]{1,0:T(8,128)(2,1)} collective-permute-done((bf16[256,640]{1,0:T(8,128)(2,1)}, bf16[256,640]{1,0:T(8,128)(2,1)}, u32[]{:S(2)}, u32[]{:S(2)}) %collective-permute-start.36) | collective-permute-done | bytes 327712 | tf_op jit(solution)/shard_map/ppermute | solution.py:102
  138.0 19.8 %shard_map.180 = (bf16[256,1920]{1,0:T(8,128)(2,1)S(1)}, f32[2,384,128]{2,1,0:T(8,128)S(1)}) custom-call(s32[1,3]{1,0:T(1,128)S(1)} %fusion.99.flag_ref, bf16[256,1920]{1,0:T(8,128)(2,1)S(1)} %copy-done.87, s32[6,1024]{1,0:T(8,128)S(1)} %copy-done.79, s32[256,8]{1,0:T(8,128)S(1)} %copy.108.meta_ref.refs_4_, ...), custom_call_target="tpu_custom_call" | custom-call | flops 2013265920 | bytes 5013516 | tf_op jit(solution)/shard_map/pallas_call | solution.py:53
  163.3 12.1 %collective-permute-done.43.refs_4_ = bf16[3,16,5120]{2,1,0:T(8,128)(2,1)} collective-permute-done((bf16[3,16,5120]{2,1,0:T(8,128)(2,1)S(1)}, bf16[3,16,5120]{2,1,0:T(8,128)(2,1)}, u32[]{:S(2)}, u32[]{:S(2)}) %collective-permute-start.43) | collective-permute-done | bytes 491552 | tf_op jit(solution)/shard_map/ppermute | solution.py:102
  194.8 8.2 %shard_map.183 = (bf16[256,1024]{1,0:T(8,128)(2,1)S(1)}, f32[256,960]{1,0:T(8,128)S(1)}, bf16[256,960]{1,0:T(8,128)(2,1)S(1)}, bf16[256,5120]{1,0:T(8,128)(2,1)}...) custom-call(bf16[256,1920]{1,0:T(8,128)(2,1)S(1)} %copy-done.46, f32[256,960]{1,0:T(8,128)S(1)} %bitcast.177, ...), custom_call_target="tpu_custom_call" | custom-call | flops 4278190080 | bytes 25083392 | tf_op jit(solution)/shard_map/pallas_call | solution.py:53
  212.0 5.7 collective-permute-done.51.refs_2_.refs_9_
  231.0 7.1 collective-permute-done.58
  242.7 20.1 %shard_map.185 = (bf16[256,1920]{1,0:T(8,128)(2,1)S(1)}, f32[2,384,128]{2,1,0:T(8,128)S(1)}) custom-call(s32[1,3]{1,0:T(1,128)S(1)} %copy-done.128, bf16[256,1920]{1,0:T(8,128)(2,1)S(1)} %copy-done.90, s32[6,1024]{1,0:T(8,128)S(1)} %copy-done.80, s32[256,8]{1,0:T(8,128)S(1)} %copy.108.meta_ref.refs_4_, bf16[256,640]{1,0:T(8,128)(2,1)S(1)} %copy-done.122, ...), custom_call_target="tpu_custom_call" | custom-call | flops 2013265920 | bytes 5013516 | tf_op jit(solution)/shard_map/pallas_call | solution.py:53
  263.6 8.6 %shard_map.186 = (bf16[256,1024]{1,0:T(8,128)(2,1)S(1)}, f32[256,960]{1,0:T(8,128)S(1)}, bf16[256,960]{1,0:T(8,128)(2,1)S(1)}, bf16[256,5120]{1,0:T(8,128)(2,1)}...) custom-call(bf16[256,1920]{1,0:T(8,128)(2,1)S(1)} %get-tuple-element.476.o_ref.refs_0_, f32[256,960]{1,0:T(8,128)S(1)} %copy-done.3, ...), custom_call_target="tpu_custom_call" | custom-call | flops 4278190080 | bytes 25083392 | tf_op jit(solution)/shard_map/pallas_call | solution.py:53
  282.6 6.0 collective-permute-done.60.refs_2_.refs_9_
  288.5 6.7 collective-permute-done.61.refs_3_.refs_10_
  298.9 9.9 %shard_map.188 = (bf16[256,1920]{1,0:T(8,128)(2,1)S(1)}, f32[2,384,128]{2,1,0:T(8,128)S(1)}) custom-call(s32[1,3]{1,0:T(1,128)S(1)} %copy-done.129, bf16[256,1920]{1,0:T(8,128)(2,1)S(1)} %copy-done.93, s32[6,1024]{1,0:T(8,128)S(1)} %copy-done.81, s32[256,8]{1,0:T(8,128)S(1)} %copy.108.meta_ref.refs_4_, bf16[256,640]{1,0:T(8,128)(2,1)} %get-tuple-element.483.refs_0_.refs_7_, ...), custom_call_target="tpu_custom_call" | custom-call | flops 2013265920 | bytes 5013516 | tf_op jit(solution)/shard_map/pallas_call | solution.py:53
  308.9 8.1 %shard_map.189 = (bf16[256,1024]{1,0:T(8,128)(2,1)S(1)}, f32[256,960]{1,0:T(8,128)S(1)}, bf16[256,960]{1,0:T(8,128)(2,1)S(1)}, bf16[256,5120]{1,0:T(8,128)(2,1)}...) custom-call(bf16[256,1920]{1,0:T(8,128)(2,1)S(1)} %get-tuple-element.494.o_ref.refs_0_, f32[256,960]{1,0:T(8,128)S(1)} %copy-done.6, ...), custom_call_target="tpu_custom_call" | custom-call | flops 4278190080 | bytes 25083392 | tf_op jit(solution)/shard_map/pallas_call | solution.py:53
  319.7 14.9 %shard_map.190 = (bf16[256,960]{1,0:T(8,128)(2,1)S(1)}, bf16[256,5120]{1,0:T(8,128)(2,1)}, bf16[256,2560]{1,0:T(8,128)(2,1)}, f32[256,960]{1,0:T(8,128)}, bf16[2...) custom-call(f32[256,960]{1,0:T(8,128)} %bitcast.179, ...), custom_call_target="tpu_custom_call" | custom-call | flops 4278190080 | bytes 31083776 | tf_op jit(solution)/shard_map/pallas_call | solution.py:53
  336.2 16.5 %shard_map.191 = (bf16[256,1024]{1,0:T(8,128)(2,1)S(1)}, bf16[4,2,640,128]{3,2,1,0:T(8,128)(2,1)}, bf16[4,2,640,128]{3,2,1,0:T(8,128)(2,1)}) custom-call(s32[1,3]{1,0:T(1,128)S(1)} %copy-done.129, bf16[256,1920]{1,0:T(8,128)(2,1)S(1)} %copy-done.93, bf16[256,1920]{1,0:T(8,128)(2,1)S(1)} %get-tuple-element.494.o_ref.refs_0_, ...), custom_call_target="tpu_custom_call" | custom-call | flops 5033164800 | bytes 9404428 | tf_op jit(solution)/shard_map/pallas_call | solution.py:53
  364.2 5.8 collective-permute-start.69
  376.6 10.6 %collective-permute-done.70.refs_2_ = bf16[2,640,128]{2,1,0:T(8,128)(2,1)S(1)} collective-permute-done((bf16[2,640,128]{2,1,0:T(8,128)(2,1)S(1)}, bf16[2,640,128]{2,1,0:T(8,128)(2,1)S(1)}, u32[]{:S(2)}, u32[]{:S(2)}) %collective-permute-start.70) | collective-permute-done | bytes 327712 | tf_op jit(solution)/shard_map/ppermute | solution.py:102
  391.7 14.8 %shard_map.193 = (bf16[256,960]{1,0:T(8,128)(2,1)S(1)}, bf16[256,5120]{1,0:T(8,128)(2,1)}, bf16[256,2560]{1,0:T(8,128)(2,1)}, f32[256,960]{1,0:T(8,128)}, bf16[2...) custom-call(f32[256,960]{1,0:T(8,128)} %copy-done.27, ...), custom_call_target="tpu_custom_call" | custom-call | flops 4278190080 | bytes 31083776 | tf_op jit(solution)/shard_map/pallas_call | solution.py:53
  408.2 27.2 %shard_map.194 = (bf16[256,1024]{1,0:T(8,128)(2,1)S(1)}, bf16[4,2,640,128]{3,2,1,0:T(8,128)(2,1)}, bf16[4,2,640,128]{3,2,1,0:T(8,128)(2,1)}) custom-call(s32[1,3]{1,0:T(1,128)S(1)} %copy-done.129, bf16[256,1920]{1,0:T(8,128)(2,1)S(1)} %copy-done.91, bf16[256,1920]{1,0:T(8,128)(2,1)S(1)} %copy-done.49, bf16[256,1920]{1,0:T(8,128)(2,1)} %get-tuple-element.527.refs_1_, ...), custom_call_target="tpu_custom_call" | custom-call | flops 5033164800 | bytes 9404428 | tf_op jit(solution)/shard_map/pallas_call | solution.py:53
  444.4 7.0 collective-permute-done.73.refs_1_
  451.4 7.4 collective-permute-done.75.refs_3_
  463.3 14.8 %shard_map.196 = (bf16[256,960]{1,0:T(8,128)(2,1)S(1)}, bf16[256,5120]{1,0:T(8,128)(2,1)}, bf16[256,2560]{1,0:T(8,128)(2,1)}, f32[256,960]{1,0:T(8,128)}, bf16[2...) custom-call(f32[256,960]{1,0:T(8,128)} %copy-done.25, ...), custom_call_target="tpu_custom_call" | custom-call | flops 4278190080 | bytes 31083776 | tf_op jit(solution)/shard_map/pallas_call | solution.py:53
  480.4 27.4 %shard_map.199 = (bf16[256,1024]{1,0:T(8,128)(2,1)S(1)}, bf16[4,2,640,128]{3,2,1,0:T(8,128)(2,1)}, bf16[4,2,640,128]{3,2,1,0:T(8,128)(2,1)}) custom-call(s32[1,3]{1,0:T(1,128)S(1)} %copy-done.129, bf16[256,1920]{1,0:T(8,128)(2,1)S(1)} %copy-done.88, bf16[256,1920]{1,0:T(8,128)(2,1)S(1)} %copy-done.47, bf16[256,1920]{1,0:T(8,128)(2,1)} %get-tuple-element.562.refs_1_, ...), custom_call_target="tpu_custom_call" | custom-call | flops 5033164800 | bytes 9404428 | tf_op jit(solution)/shard_map/pallas_call | solution.py:53
  508.6 19.3 %shard_map.198 = (bf16[4,4,32,5120]{3,2,1,0:T(8,128)(2,1)}, bf16[4,4,32,5120]{3,2,1,0:T(8,128)(2,1)}) custom-call(bf16[256,960]{1,0:T(8,128)(2,1)} %copy-done.101, bf16[256,960]{1,0:T(8,128)(2,1)} %copy-done.103, bf16[256,960]{1,0:T(8,128)(2,1)} %copy-done.107, bf16[256,5120]{1,0:T(8,128)(2,1)} %get-tuple-element.558.refs_3_, ...), custom_call_target="tpu_custom_call" | custom-call | flops 7549747200 | bytes 19824640 | tf_op jit(solution)/shard_map/pallas_call | solution.py:53
  534.3 14.4 %shard_map.197 = (bf16[4,4,112,960]{3,2,1,0:T(8,128)(2,1)}, bf16[4,4,112,960]{3,2,1,0:T(8,128)(2,1)}) custom-call(bf16[256,1024]{1,0:T(8,128)(2,1)} %copy-done.100, bf16[256,1024]{1,0:T(8,128)(2,1)} %copy-done.102, bf16[256,1024]{1,0:T(8,128)(2,1)} %copy-done.104, bf16[256,2560]{1,0:T(8,128)(2,1)} %get-tuple-element.545.refs_3_, ...), custom_call_target="tpu_custom_call" | custom-call | flops 5190451200 | bytes 15335424 | tf_op jit(solution)/shard_map/pallas_call | solution.py:53
  578.4 8.5 %shard_map.201 = (bf16[4,4,32,1664]{3,2,1,0:T(8,128)(2,1)}, bf16[4,4,32,1664]{3,2,1,0:T(8,128)(2,1)}) custom-call(bf16[256,960]{1,0:T(8,128)(2,1)} %copy-done.97, bf16[256,960]{1,0:T(8,128)(2,1)} %copy-done.98, bf16[256,960]{1,0:T(8,128)(2,1)} %copy-done.99, bf16[256,1664]{1,0:T(8,128)(2,1)} %copy-done.96, bf16[256,1664]{1,0:T(8,128)(2,1)} %copy-done.95, ...), custom_call_target="tpu_custom_call" | custom-call | flops 2453667840 | bytes 7864320 | tf_op jit(solution)/shard_map/pallas_call | solution.py:53
  597.5 10.7 %collective-permute-done.84 = bf16[2,32,5120]{2,1,0:T(8,128)(2,1)} collective-permute-done((bf16[2,32,5120]{2,1,0:T(8,128)(2,1)}, bf16[2,32,5120]{2,1,0:T(8,128)(2,1)}, u32[]{:S(2)}, u32[]{:S(2)}) %collective-permute-start.84) | collective-permute-done | bytes 655392 | tf_op jit(solution)/shard_map/ppermute | solution.py:102
  623.3 7.0 collective-permute-done.106
  633.8 8.5 %collective-permute-done.107 = bf16[32,5120]{1,0:T(8,128)(2,1)S(1)} collective-permute-done((bf16[32,5120]{1,0:T(8,128)(2,1)S(1)}, bf16[32,5120]{1,0:T(8,128)(2,1)S(1)}, u32[]{:S(2)}, u32[]{:S(2)}) %collective-permute-start.107) | collective-permute-done | bytes 327712 | tf_op jit(solution)/shard_map/ppermute | solution.py:102
  658.6 6.4 collective-permute-done.91
  687.8 7.9 %collective-permute-done.97 = bf16[112,960]{1,0:T(8,128)(2,1)S(1)} collective-permute-done((bf16[112,960]{1,0:T(8,128)(2,1)S(1)}, bf16[112,960]{1,0:T(8,128)(2,1)S(1)}, u32[]{:S(2)}, u32[]{:S(2)}) %collective-permute-start.97) | collective-permute-done | bytes 215072 | tf_op jit(solution)/shard_map/ppermute | solution.py:102
  709.5 6.4 collective-permute-done.100
  (707 shorter events, 376.1 us)
Async XLA Ops:
  3.0 20.6 %collective-permute-start = (bf16[32,1664]{1,0:T(8,128)(2,1)S(1)}, bf16[32,1664]{1,0:T(8,128)(2,1)S(1)}, u32[]{:S(2)}, u32[]{:S(2)}) collective-permute-start(bf16[32,1664]{1,0:T(8,128)(2,1)S(1)} %fusion.68), channel_id=1, source_target_pairs={{0,1},{1,2},{2,3},{3,0},{4,5},{5,6},{6,7},{7,4},{8,9},{9,10},{10,1... | collective-permute-start | bytes 319496 | tf_op jit(solution)/shard_map/ppermute | solution.py:102
  25.1 18.9 %collective-permute-start.17 = (bf16[112,960]{1,0:T(8,128)(2,1)S(1)}, bf16[112,960]{1,0:T(8,128)(2,1)S(1)}, u32[]{:S(2)}, u32[]{:S(2)}) collective-permute-start(bf16[112,960]{1,0:T(8,128)(2,1)S(1)} %fusion.62), channel_id=1, source_target_pairs={{0,2},{1,3},{2,0},{3,1},{4,6},{5,7},{6,4},{7,5},{8,10},{9,11},{10,... | collective-permute-start | bytes 645128 | tf_op jit(solution)/shard_map/ppermute | solution.py:102
  25.4 19.6 %collective-permute-start.18 = (bf16[112,960]{1,0:T(8,128)(2,1)S(1)}, bf16[112,960]{1,0:T(8,128)(2,1)}, u32[]{:S(2)}, u32[]{:S(2)}) collective-permute-start(bf16[112,960]{1,0:T(8,128)(2,1)S(1)} %fusion.62), channel_id=1, source_target_pairs={{0,3},{1,0},{2,1},{3,2},{4,7},{5,4},{6,5},{7,6},{8,11},{9,8},{10,9... | collective-permute-start | bytes 645128 | tf_op jit(solution)/shard_map/ppermute | solution.py:102
  29.3 21.3 %collective-permute-start.12 = (bf16[128,960]{0,1:T(8,128)(2,1)S(1)}, bf16[128,960]{0,1:T(8,128)(2,1)S(1)}, u32[]{:S(2)}, u32[]{:S(2)}) collective-permute-start(bf16[128,960]{0,1:T(8,128)(2,1)S(1)} %get-tuple-element.369), channel_id=1, source_target_pairs={{0,4},{4,12},{8,20},{12,28},{16,24},{20,16},{24,8},{28,0},{1,5},{5... | collective-permute-start | bytes 737288 | tf_op jit(solution)/shard_map/ppermute | solution.py:102
  29.4 21.2 %collective-permute-start.7 = (bf16[3,32,1664]{2,1,0:T(8,128)(2,1)S(1)}, bf16[3,32,1664]{2,1,0:T(8,128)(2,1)S(1)}, u32[]{:S(2)}, u32[]{:S(2)}) collective-permute-start(bf16[3,32,1664]{2,1,0:T(8,128)(2,1)S(1)} %pad_maximum_fusion.8.refs_1_), channel_id=1, source_target_pairs={{0,4},{4,0},{8,12},{12,8},{16,20},{20,16},{24,28},{28,24},{1,5},{5... | collective-permute-start | bytes 958472 | tf_op jit(solution)/shard_map/ppermute | solution.py:102
  50.5 18.0 %collective-permute-start.19 = (bf16[3,112,960]{2,1,0:T(8,128)(2,1)}, bf16[3,112,960]{2,1,0:T(8,128)(2,1)}, u32[]{:S(2)}, u32[]{:S(2)}) collective-permute-start(bf16[3,112,960]{2,1,0:T(8,128)(2,1)} %pad_maximum_fusion.6.refs_2_), channel_id=1, source_target_pairs={{0,8},{4,12},{8,0},{12,4},{16,24},{20,28},{24,16},{28,20},{1,9},{5... | collective-permute-start | bytes 1935368 | tf_op jit(solution)/shard_map/ppermute | solution.py:102
  50.5 23.5 %collective-permute-start.20 = (bf16[3,112,960]{2,1,0:T(8,128)(2,1)}, bf16[3,112,960]{2,1,0:T(8,128)(2,1)}, u32[]{:S(2)}, u32[]{:S(2)}) collective-permute-start(bf16[3,112,960]{2,1,0:T(8,128)(2,1)} %pad_maximum_fusion.6.refs_2_), channel_id=1, source_target_pairs={{0,16},{4,20},{8,24},{12,28},{16,0},{20,4},{24,8},{28,12},{1,17},{... | collective-permute-start | bytes 1935368 | tf_op jit(solution)/shard_map/ppermute | solution.py:102
  62.9 20.3 %collective-permute-start.31 = (bf16[3,32,1664]{2,1,0:T(8,128)(2,1)S(1)}, bf16[3,32,1664]{2,1,0:T(8,128)(2,1)S(1)}, u32[]{:S(2)}, u32[]{:S(2)}) collective-permute-start(bf16[3,32,1664]{2,1,0:T(8,128)(2,1)S(1)} %collective-permute-done.8.refs_3_), channel_id=1, source_target_pairs={{0,4},{4,0},{8,12},{12,8},{16,20},{20,16},{24,28},{28,24},{1,5},{5... | collective-permute-start | bytes 958472 | tf_op jit(solution)/shard_map/ppermute | solution.py:102
  62.9 20.3 %collective-permute-start.32 = (bf16[3,32,1664]{2,1,0:T(8,128)(2,1)S(1)}, bf16[3,32,1664]{2,1,0:T(8,128)(2,1)S(1)}, u32[]{:S(2)}, u32[]{:S(2)}) collective-permute-start(bf16[3,32,1664]{2,1,0:T(8,128)(2,1)S(1)} %collective-permute-done.9.refs_4_), channel_id=1, source_target_pairs={{0,4},{4,0},{8,12},{12,8},{16,20},{20,16},{24,28},{28,24},{1,5},{5... | collective-permute-start | bytes 958472 | tf_op jit(solution)/shard_map/ppermute | solution.py:102
  68.5 20.5 %collective-permute-start.27 = (bf16[32,5120]{1,0:T(8,128)(2,1)}, bf16[32,5120]{1,0:T(8,128)(2,1)S(1)}, u32[]{:S(2)}, u32[]{:S(2)}) collective-permute-start(bf16[32,5120]{1,0:T(8,128)(2,1)} %pad_dynamic-slice_fusion), channel_id=1, source_target_pairs={{0,2},{1,3},{2,0},{3,1},{4,6},{5,7},{6,4},{7,5},{8,10},{9,11},{10,... | collective-permute-start | bytes 983048 | tf_op jit(solution)/shard_map/ppermute | solution.py:102
  83.2 20.3 %collective-permute-start.23 = (bf16[3,112,960]{2,1,0:T(8,128)(2,1)}, bf16[3,112,960]{2,1,0:T(8,128)(2,1)}, u32[]{:S(2)}, u32[]{:S(2)}) collective-permute-start(bf16[3,112,960]{2,1,0:T(8,128)(2,1)} %pad_maximum_fusion.6.refs_2_), channel_id=1, source_target_pairs={{0,4},{4,0},{8,12},{12,8},{16,20},{20,16},{24,28},{28,24},{1,5},{5... | collective-permute-start | bytes 1935368 | tf_op jit(solution)/shard_map/ppermute | solution.py:102
  83.3 20.5 %collective-permute-start.24 = (bf16[3,112,960]{2,1,0:T(8,128)(2,1)}, bf16[3,112,960]{2,1,0:T(8,128)(2,1)}, u32[]{:S(2)}, u32[]{:S(2)}) collective-permute-start(bf16[3,112,960]{2,1,0:T(8,128)(2,1)} %collective-permute-done.19.refs_3_), channel_id=1, source_target_pairs={{0,4},{4,0},{8,12},{12,8},{16,20},{20,16},{24,28},{28,24},{1,5},{5... | collective-permute-start | bytes 1935368 | tf_op jit(solution)/shard_map/ppermute | solution.py:102
  83.8 21.2 %collective-permute-start.25 = (bf16[3,112,960]{2,1,0:T(8,128)(2,1)}, bf16[3,112,960]{2,1,0:T(8,128)(2,1)}, u32[]{:S(2)}, u32[]{:S(2)}) collective-permute-start(bf16[3,112,960]{2,1,0:T(8,128)(2,1)} %collective-permute-done.20.refs_4_), channel_id=1, source_target_pairs={{0,4},{4,0},{8,12},{12,8},{16,20},{20,16},{24,28},{28,24},{1,5},{5... | collective-permute-start | bytes 1935368 | tf_op jit(solution)/shard_map/ppermute | solution.py:102
  103.5 18.0 %collective-permute-start.36 = (bf16[256,640]{1,0:T(8,128)(2,1)}, bf16[256,640]{1,0:T(8,128)(2,1)}, u32[]{:S(2)}, u32[]{:S(2)}) collective-permute-start(bf16[256,640]{1,0:T(8,128)(2,1)} %get-tuple-element.419.refs_0_.refs_7_), channel_id=1, source_target_pairs={{0,16},{4,20},{8,24},{12,28},{16,0},{20,4},{24,8},{28,12},{1,17},{... | collective-permute-start | bytes 983048 | tf_op jit(solution)/shard_map/ppermute | solution.py:102
  106.0 52.8 %collective-permute-start.29 = (bf16[3,32,5120]{2,1,0:T(8,128)(2,1)}, bf16[3,32,5120]{2,1,0:T(8,128)(2,1)}, u32[]{:S(2)}, u32[]{:S(2)}) collective-permute-start(bf16[3,32,5120]{2,1,0:T(8,128)(2,1)} %pad_maximum_fusion.3.refs_1_), channel_id=1, source_target_pairs={{0,8},{4,12},{8,0},{12,4},{16,24},{20,28},{24,16},{28,20},{1,9},{5... | collective-permute-start | bytes 2949128 | tf_op jit(solution)/shard_map/ppermute | solution.py:102
  108.8 50.0 %collective-permute-start.30 = (bf16[3,32,5120]{2,1,0:T(8,128)(2,1)}, bf16[3,32,5120]{2,1,0:T(8,128)(2,1)}, u32[]{:S(2)}, u32[]{:S(2)}) collective-permute-start(bf16[3,32,5120]{2,1,0:T(8,128)(2,1)} %pad_maximum_fusion.3.refs_1_), channel_id=1, source_target_pairs={{0,16},{4,20},{8,24},{12,28},{16,0},{20,4},{24,8},{28,12},{1,17},{... | collective-permute-start | bytes 2949128 | tf_op jit(solution)/shard_map/ppermute | solution.py:102
  508.6 19.3 %collective-permute-start.76 = (bf16[4,2,640,128]{3,2,1,0:T(8,128)(2,1)}, bf16[4,2,640,128]{3,2,1,0:T(8,128)(2,1)}, u32[]{:S(2)}, u32[]{:S(2)}) collective-permute-start(bf16[4,2,640,128]{3,2,1,0:T(8,128)(2,1)} %get-tuple-element.566), channel_id=1, source_target_pairs={{0,4},{4,0},{8,12},{12,8},{16,20},{20,16},{24,28},{28,24},{1,5},{5... | collective-permute-start | bytes 3932168 | tf_op jit(solution)/shard_map/ppermute | solution.py:102
  527.9 20.9 %collective-permute-start.80 = (bf16[4,4,32,5120]{3,2,1,0:T(8,128)(2,1)}, bf16[4,4,32,5120]{3,2,1,0:T(8,128)(2,1)}, u32[]{:S(2)}, u32[]{:S(2)}) collective-permute-start(bf16[4,4,32,5120]{3,2,1,0:T(8,128)(2,1)} %get-tuple-element.573), channel_id=1, source_target_pairs={{0,4},{4,0},{8,12},{12,8},{16,20},{20,16},{24,28},{28,24},{1,5},{5... | collective-permute-start | bytes 15728648 | tf_op jit(solution)/shard_map/ppermute | solution.py:102
  530.8 17.9 %collective-permute-start.77 = (bf16[2,640,128]{2,1,0:T(8,128)(2,1)S(1)}, bf16[2,640,128]{2,1,0:T(8,128)(2,1)S(1)}, u32[]{:S(2)}, u32[]{:S(2)}) collective-permute-start(bf16[2,640,128]{2,1,0:T(8,128)(2,1)S(1)} %get-tuple-element.569), channel_id=1, source_target_pairs={{0,8},{4,12},{8,0},{12,4},{16,24},{20,28},{24,16},{28,20},{1,9},{5... | collective-permute-start | bytes 983048 | tf_op jit(solution)/shard_map/ppermute | solution.py:102
  554.8 32.1 %collective-permute-start.83 = (bf16[4,4,112,960]{3,2,1,0:T(8,128)(2,1)}, bf16[4,4,112,960]{3,2,1,0:T(8,128)(2,1)}, u32[]{:S(2)}, u32[]{:S(2)}) collective-permute-start(bf16[4,4,112,960]{3,2,1,0:T(8,128)(2,1)} %get-tuple-element.582), channel_id=1, source_target_pairs={{0,4},{4,0},{8,12},{12,8},{16,20},{20,16},{24,28},{28,24},{1,5},{5... | collective-permute-start | bytes 10321928 | tf_op jit(solution)/shard_map/ppermute | solution.py:102
  554.8 32.0 %collective-permute-start.81 = (bf16[2,2,32,5120]{3,2,1,0:T(8,128)(2,1)}, bf16[2,2,32,5120]{3,2,1,0:T(8,128)(2,1)}, u32[]{:S(2)}, u32[]{:S(2)}) collective-permute-start(bf16[2,2,32,5120]{3,2,1,0:T(8,128)(2,1)} %pad_maximum_fusion), channel_id=1, source_target_pairs={{0,8},{4,12},{8,0},{12,4},{16,24},{20,28},{24,16},{28,20},{1,9},{5... | collective-permute-start | bytes 3932168 | tf_op jit(solution)/shard_map/ppermute | solution.py:102
  555.7 31.2 %collective-permute-start.82 = (bf16[2,2,32,5120]{3,2,1,0:T(8,128)(2,1)}, bf16[2,2,32,5120]{3,2,1,0:T(8,128)(2,1)}, u32[]{:S(2)}, u32[]{:S(2)}) collective-permute-start(bf16[2,2,32,5120]{3,2,1,0:T(8,128)(2,1)} %pad_maximum_fusion.1), channel_id=1, source_target_pairs={{0,16},{4,20},{8,24},{12,28},{16,0},{20,4},{24,8},{28,12},{1,17},{... | collective-permute-start | bytes 3932168 | tf_op jit(solution)/shard_map/ppermute | solution.py:102
  586.9 22.4 %collective-permute-start.86 = (bf16[4,4,32,1664]{3,2,1,0:T(8,128)(2,1)}, bf16[4,4,32,1664]{3,2,1,0:T(8,128)(2,1)S(1)}, u32[]{:S(2)}, u32[]{:S(2)}) collective-permute-start(bf16[4,4,32,1664]{3,2,1,0:T(8,128)(2,1)} %get-tuple-element.608), channel_id=1, source_target_pairs={{0,4},{4,0},{8,12},{12,8},{16,20},{20,16},{24,28},{28,24},{1,5},{5... | collective-permute-start | bytes 5111816 | tf_op jit(solution)/shard_map/ppermute | solution.py:102
  609.3 39.3 %collective-permute-start.87 = (bf16[2,2,112,960]{3,2,1,0:T(8,128)(2,1)}, bf16[2,2,112,960]{3,2,1,0:T(8,128)(2,1)}, u32[]{:S(2)}, u32[]{:S(2)}) collective-permute-start(bf16[2,2,112,960]{3,2,1,0:T(8,128)(2,1)} %pad_maximum_fusion.4), channel_id=1, source_target_pairs={{0,8},{4,12},{8,0},{12,4},{16,24},{20,28},{24,16},{28,20},{1,9},{5... | collective-permute-start | bytes 2580488 | tf_op jit(solution)/shard_map/ppermute | solution.py:102
  609.7 38.9 %collective-permute-start.88 = (bf16[2,2,112,960]{3,2,1,0:T(8,128)(2,1)}, bf16[2,2,112,960]{3,2,1,0:T(8,128)(2,1)}, u32[]{:S(2)}, u32[]{:S(2)}) collective-permute-start(bf16[2,2,112,960]{3,2,1,0:T(8,128)(2,1)} %pad_maximum_fusion.5), channel_id=1, source_target_pairs={{0,16},{4,20},{8,24},{12,28},{16,0},{20,4},{24,8},{28,12},{1,17},{... | collective-permute-start | bytes 2580488 | tf_op jit(solution)/shard_map/ppermute | solution.py:102
  618.8 23.5 %collective-permute-start.107 = (bf16[32,5120]{1,0:T(8,128)(2,1)S(1)}, bf16[32,5120]{1,0:T(8,128)(2,1)S(1)}, u32[]{:S(2)}, u32[]{:S(2)}) collective-permute-start(bf16[32,5120]{1,0:T(8,128)(2,1)S(1)} %get-tuple-element.645), channel_id=1, source_target_pairs={{0,2},{1,3},{2,0},{3,1},{4,6},{5,7},{6,4},{7,5},{8,10},{9,11},{10,... | collective-permute-start | bytes 983048 | tf_op jit(solution)/shard_map/ppermute | solution.py:102
  622.5 22.1 %collective-permute-start.108 = (bf16[32,5120]{1,0:T(8,128)(2,1)S(1)}, bf16[32,5120]{1,0:T(8,128)(2,1)}, u32[]{:S(2)}, u32[]{:S(2)}) collective-permute-start(bf16[32,5120]{1,0:T(8,128)(2,1)S(1)} %get-tuple-element.646), channel_id=1, source_target_pairs={{0,3},{1,0},{2,1},{3,2},{4,7},{5,4},{6,5},{7,6},{8,11},{9,8},{10,9... | collective-permute-start | bytes 983048 | tf_op jit(solution)/shard_map/ppermute | solution.py:102
  658.3 18.4 %collective-permute-start.110 = (bf16[32,5120]{1,0:T(8,128)(2,1)S(1)}, bf16[32,5120]{1,0:T(8,128)(2,1)S(1)}, u32[]{:S(2)}, u32[]{:S(2)}) collective-permute-start(bf16[32,5120]{1,0:T(8,128)(2,1)S(1)} %fusion.10.refs_0_), channel_id=1, source_target_pairs={{0,8},{4,12},{8,0},{12,4},{16,24},{20,28},{24,16},{28,20},{1,9},{5... | collective-permute-start | bytes 983048 | tf_op jit(solution)/shard_map/ppermute | solution.py:102
  658.4 18.3 %collective-permute-start.111 = (bf16[32,5120]{1,0:T(8,128)(2,1)S(1)}, bf16[32,5120]{1,0:T(8,128)(2,1)S(1)}, u32[]{:S(2)}, u32[]{:S(2)}) collective-permute-start(bf16[32,5120]{1,0:T(8,128)(2,1)S(1)} %fusion.10.refs_0_), channel_id=1, source_target_pairs={{0,16},{4,20},{8,24},{12,28},{16,0},{20,4},{24,8},{28,12},{1,17},{... | collective-permute-start | bytes 983048 | tf_op jit(solution)/shard_map/ppermute | solution.py:102
  676.0 22.3 %collective-permute-start.93 = (bf16[4,32,1664]{2,1,0:T(8,128)(2,1)S(1)}, bf16[4,32,1664]{2,1,0:T(8,128)(2,1)S(1)}, u32[]{:S(2)}, u32[]{:S(2)}) collective-permute-start(bf16[4,32,1664]{2,1,0:T(8,128)(2,1)S(1)} %get-tuple-element.623), channel_id=1, source_target_pairs={{0,8},{4,12},{8,0},{12,4},{16,24},{20,28},{24,16},{28,20},{1,9},{5... | collective-permute-start | bytes 1277960 | tf_op jit(solution)/shard_map/ppermute | solution.py:102
  676.7 22.2 %collective-permute-start.94 = (bf16[4,32,1664]{2,1,0:T(8,128)(2,1)S(1)}, bf16[4,32,1664]{2,1,0:T(8,128)(2,1)S(1)}, u32[]{:S(2)}, u32[]{:S(2)}) collective-permute-start(bf16[4,32,1664]{2,1,0:T(8,128)(2,1)S(1)} %get-tuple-element.624), channel_id=1, source_target_pairs={{0,16},{4,20},{8,24},{12,28},{16,0},{20,4},{24,8},{28,12},{1,17},{... | collective-permute-start | bytes 1277960 | tf_op jit(solution)/shard_map/ppermute | solution.py:102
  676.7 22.7 %collective-permute-start.95 = (bf16[4,32,1664]{2,1,0:T(8,128)(2,1)S(1)}, bf16[4,32,1664]{2,1,0:T(8,128)(2,1)S(1)}, u32[]{:S(2)}, u32[]{:S(2)}) collective-permute-start(bf16[4,32,1664]{2,1,0:T(8,128)(2,1)S(1)} %get-tuple-element.625), channel_id=1, source_target_pairs={{0,24},{4,28},{8,16},{12,20},{16,8},{20,12},{24,0},{28,4},{1,25},{... | collective-permute-start | bytes 1277960 | tf_op jit(solution)/shard_map/ppermute | solution.py:102
  (265 other events, 2274.9 us)

commit v5 on v4

--- a/solution.py
+++ b/solution.py
@@ -406,7 +406,7 @@
         [VMEM] * 4 + [ANY],
         [pltpu.VMEM((D, ALL_COLS), BF), pltpu.SemaphoreType.DMA((w.shape[0],))],
         2 * rows * D * ALL_COLS,
-        24,
+        12,
     )
 
 
@@ -547,7 +547,7 @@
         [SMEM] + [VMEM] * 3 + [ANY] * len(segments),
         [pltpu.VMEM((total, KV_COLS), BF), pltpu.VMEM((total, KV_COLS), BF), pltpu.SemaphoreType.DMA((n,))],
         4 * rows * total * HEADS * LANES // 2,
-        32,
+        20,
     )
 
 
@@ -632,7 +632,7 @@
         [VMEM] * 5 + [ANY] * 2,
         [*weight_scratch(od.shape[0]), pltpu.VMEM((rows, FF), BF)],
         2 * rows * (D * Q_COLS + 3 * D * FF),
-        48,
+        34,
     )
 
 
@@ -721,7 +721,7 @@
         [VMEM] * 8 + [ANY] * 2,
         weight_scratch(od.shape[0]),
         2 * rows * (D * Q_COLS + 3 * D * FF),
-        52,
+        40,
     )
 
 
@@ -846,7 +846,7 @@
             pltpu.SemaphoreType.DMA((n,)),
         ],
         10 * rows * total * HEADS * LANES // 2,
-        48,
+        32,
     )
 
 
@@ -894,34 +894,38 @@
         [VMEM] * (9 + len(parts)) + [ANY],
         [pltpu.VMEM((D, ALL_COLS), BF), pltpu.SemaphoreType.DMA((w.shape[0],))],
         2 * rows * D * ALL_COLS,
-        24,
+        14,
     )
 
 
 def grads_kernel(size, count, step, rows_z, block, *refs):
     n, total = len(rows_z), sum(rows_z)
     lefts, rights, refs = refs[: n * STEPS], refs[n * STEPS : 2 * n * STEPS], refs[2 * n * STEPS :]
-    spare = step * size - total if len(refs) > 3 + 3 * n else 0
+    spare = step * size - total if len(refs) > 3 + 4 * n else 0
     extra_ref, refs = (refs[0], refs[1:]) if spare else (None, refs)
     even_ref, odd_ref = refs[:2]
     left_t, right_s, packs, sems = refs[2 : 2 + n], refs[2 + n : 2 + 2 * n], refs[2 + 2 * n : 2 + 3 * n], refs[-1]
+    left_s = refs[2 + 3 * n : 2 + 4 * n]
     rank = lax.axis_index("dp")
     copies = []
-    for i in range(n):
-        for r in range(STEPS):
-            src = rights[i * STEPS + r]
-            c = pltpu.make_async_copy(src, right_s[i].at[pl.ds(r * src.shape[0], src.shape[0])], sems.at[len(copies)])
-            c.start()
-            copies.append(c)
+    for sources, targets in ((lefts, left_s), (rights, right_s)):
+        for i in range(n):
+            for r in range(STEPS):
+                src = sources[i * STEPS + r]
+                dst = targets[i].at[pl.ds(r * src.shape[0], src.shape[0]), pl.ds(0, src.shape[1])]
+                c = pltpu.make_async_copy(src, dst, sems.at[len(copies)])
+                c.start()
+                copies.append(c)
+    for c in copies[: n * STEPS]:
+        c.wait()
     for i in range(n):
         wide = left_t[i].shape[0]
         for r in range(STEPS):
-            src = lefts[i * STEPS + r]
-            k = src.shape[0]
+            k = lefts[i * STEPS + r].shape[0]
             for lo in range(0, wide, LANES):
                 hi = min(lo + LANES, wide)
-                left_t[i][lo:hi, r * k : (r + 1) * k] = src[:, lo:hi].astype(F32).T.astype(BF)
-    for c in copies:
+                left_t[i][lo:hi, r * k : (r + 1) * k] = left_s[i][r * k : (r + 1) * k, lo:hi].astype(F32).T.astype(BF)
+    for c in copies[n * STEPS :]:
         c.wait()
 
     def put(j, z, first, cols, value):
@@ -967,7 +971,7 @@
     tokens = STEPS * lefts[0][0].shape[0]
     k = len(lefts)
     args = [x for l in lefts for x in l] + [x for r in rights for x in r] + ([extra] if extra is not None else [])
-    specs = [VMEM] * (k * STEPS) + [ANY] * (k * STEPS) + ([VMEM] if extra is not None else [])
+    specs = [ANY] * (2 * k * STEPS) + ([VMEM] if extra is not None else [])
     return call(
         functools.partial(grads_kernel, size, count, step, rows_z, block),
         [shaped(max(size // 2, 1), count, step, cols, dtype=BF)] * 2,
@@ -976,7 +980,8 @@
         [pltpu.VMEM((n * count, tokens), BF) for n in rows_z]
         + [pltpu.VMEM((tokens, cols), BF) for _ in rows_z]
         + [pltpu.VMEM((n * count, block), BF) for n in rows_z]
-        + [pltpu.SemaphoreType.DMA((k * STEPS,))],
+        + [pltpu.VMEM((tokens, l[0].shape[1]), BF) for l in lefts]
+        + [pltpu.SemaphoreType.DMA((2 * k * STEPS,))],
         2 * tokens * sum(rows_z) * count * cols,
         58,
     )

time: 753 us -> 741 us (0.984)
  Pallas kernels: 263 us -> 250 us
    pallas_call x27, Pallas kernels: 263 us -> 250 us  [call(): pl.pallas_call(kernel, out_shape=outs, in_specs=specs, out_specs=out_spec...]
    unnamed x344 -> x404, local copies, waits for them, and re-layouts: 68.2 us -> 69.6 us
  transfers between devices with their start and end apart: 126 -> 126, of which waited for: 41 -> 42; matrix products, arithmetic and copies ran while one was open for 9% -> 9% of each run, Pallas kernels for 11% -> 11%
where the time goes in v5:
time: 741 us; the launch traced here: 731 us
  Pallas kernels  250 us (34%)
  waiting for transfers between devices  181 us (24%)
  starting transfers between devices  150 us (20%)
  local copies, waits for them, and re-layouts  94.3 us (13%)
  other arithmetic  49 us (7%)
    pallas_call x27, Pallas kernels, call(): pl.pallas_call(kernel, out_shape=outs, in_specs=specs, out_specs=out_spec...  250 us
    ppermute x126, waiting for transfers between devices, start(): lax.ppermute(x, axis, perm)  181 us
    ppermute x126, starting transfers between devices, start(): lax.ppermute(x, axis, perm)  150 us
    unnamed x404, local copies, waits for them, and re-layouts  69.6 us
  transfers between devices with their start and end apart: 126, of which 42 were waited for; matrix products, arithmetic and copies ran while one was open for 9% of the time, Pallas kernels for 11%

profile of v5, /device:TPU:0, one launch (start us, length us, event | category | flops | bytes accessed | tf_op | source)
XLA Modules:
  0.0 731.2 jit_solution(16414734667329760049)
XLA Ops:
  37.1 6.9 collective-permute-done.17
  54.6 6.7 collective-permute-done.9.refs_4_
  112.2 9.1 %collective-permute-done.36.refs_3_.refs_10_ = bf16[256,640]{1,0:T(8,128)(2,1)S(1)} collective-permute-done((bf16[256,640]{1,0:T(8,128)(2,1)}, bf16[256,640]{1,0:T(8,128)(2,1)S(1)}, u32[]{:S(2)}, u32[]{:S(2)}) %collective-permute-start.36) | collective-permute-done | bytes 327712 | tf_op jit(solution)/shard_map/ppermute | solution.py:102
  141.1 20.8 %shard_map.180 = (bf16[256,1920]{1,0:T(8,128)(2,1)S(1)}, f32[2,384,128]{2,1,0:T(8,128)S(1)}) custom-call(s32[1,3]{1,0:T(1,128)S(1)} %fusion.99.flag_ref, bf16[256,1920]{1,0:T(8,128)(2,1)S(1)} %copy-done.104, s32[6,1024]{1,0:T(8,128)S(1)} %pad_add_fusion.keys_ref.refs_3_, s32[256,8]{1,0:T(8,128)S(1)} %copy.108.meta_ref.refs_4_, ...), custom_call_target="tpu_custom_call" | custom-call | flops 2013265920 | bytes 5013516 | tf_op jit(solution)/shard_map/pallas_call | solution.py:53
  168.1 12.0 %collective-permute-done.43.refs_4_ = bf16[3,16,5120]{2,1,0:T(8,128)(2,1)} collective-permute-done((bf16[3,16,5120]{2,1,0:T(8,128)(2,1)S(1)}, bf16[3,16,5120]{2,1,0:T(8,128)(2,1)}, u32[]{:S(2)}, u32[]{:S(2)}) %collective-permute-start.43) | collective-permute-done | bytes 491552 | tf_op jit(solution)/shard_map/ppermute | solution.py:102
  200.8 8.5 %shard_map.183 = (bf16[256,1024]{1,0:T(8,128)(2,1)S(1)}, f32[256,960]{1,0:T(8,128)S(1)}, bf16[256,960]{1,0:T(8,128)(2,1)S(1)}, bf16[256,5120]{1,0:T(8,128)(2,1)S...) custom-call(bf16[256,1920]{1,0:T(8,128)(2,1)S(1)} %copy-done.53, f32[256,960]{1,0:T(8,128)S(1)} %bitcast.178, ...), custom_call_target="tpu_custom_call" | custom-call | flops 4278190080 | bytes 25083392 | tf_op jit(solution)/shard_map/pallas_call | solution.py:53
  217.7 7.0 collective-permute-done.51.refs_2_.refs_9_
  238.1 7.1 collective-permute-done.58
  245.9 21.9 %shard_map.185 = (bf16[256,1920]{1,0:T(8,128)(2,1)S(1)}, f32[2,384,128]{2,1,0:T(8,128)S(1)}) custom-call(s32[1,3]{1,0:T(1,128)S(1)} %copy-done.158, bf16[256,1920]{1,0:T(8,128)(2,1)S(1)} %get-tuple-element.458.q_ref, s32[6,1024]{1,0:T(8,128)S(1)} %copy-done.91, s32[256,8]{1,0:T(8,128)S(1)} %copy.108.meta_ref.refs_4_, ...), custom_call_target="tpu_custom_call" | custom-call | flops 2013265920 | bytes 5013516 | tf_op jit(solution)/shard_map/pallas_call | solution.py:53
  272.1 8.5 %shard_map.186 = (bf16[256,1024]{1,0:T(8,128)(2,1)S(1)}, f32[256,960]{1,0:T(8,128)S(1)}, bf16[256,960]{1,0:T(8,128)(2,1)S(1)}, bf16[256,5120]{1,0:T(8,128)(2,1)S...) custom-call(bf16[256,1920]{1,0:T(8,128)(2,1)S(1)} %get-tuple-element.476.o_ref.refs_0_, f32[256,960]{1,0:T(8,128)S(1)} %copy-done.8, ...), custom_call_target="tpu_custom_call" | custom-call | flops 4278190080 | bytes 25083392 | tf_op jit(solution)/shard_map/pallas_call | solution.py:53
  292.4 6.0 collective-permute-done.60.refs_2_.refs_9_
  298.4 6.7 collective-permute-done.61.refs_3_.refs_10_
  307.9 9.7 %shard_map.188 = (bf16[256,1920]{1,0:T(8,128)(2,1)S(1)}, f32[2,384,128]{2,1,0:T(8,128)S(1)}) custom-call(s32[1,3]{1,0:T(1,128)S(1)} %copy-done.159, bf16[256,1920]{1,0:T(8,128)(2,1)S(1)} %copy-done.109, s32[6,1024]{1,0:T(8,128)S(1)} %copy-done.92, s32[256,8]{1,0:T(8,128)S(1)} %copy.108.meta_ref.refs_4_, bf16[256,640]{1,0:T(8,128)(2,1)} %get-tuple-element.483.refs_0_.refs_7_, ...), custom_call_target="tpu_custom_call" | custom-call | flops 2013265920 | bytes 5013516 | tf_op jit(solution)/shard_map/pallas_call | solution.py:53
  320.7 8.7 %shard_map.189 = (bf16[256,1024]{1,0:T(8,128)(2,1)S(1)}, f32[256,960]{1,0:T(8,128)S(1)}, bf16[256,960]{1,0:T(8,128)(2,1)S(1)}, bf16[256,5120]{1,0:T(8,128)(2,1)S...) custom-call(bf16[256,1920]{1,0:T(8,128)(2,1)S(1)} %get-tuple-element.494.o_ref.refs_0_, f32[256,960]{1,0:T(8,128)S(1)} %copy-done.11, ...), custom_call_target="tpu_custom_call" | custom-call | flops 4278190080 | bytes 25083392 | tf_op jit(solution)/shard_map/pallas_call | solution.py:53
  331.0 10.6 %shard_map.190 = (bf16[256,960]{1,0:T(8,128)(2,1)S(1)}, bf16[256,5120]{1,0:T(8,128)(2,1)S(1)}, bf16[256,2560]{1,0:T(8,128)(2,1)S(1)}, f32[256,960]{1,0:T(8,128)S...) custom-call(f32[256,960]{1,0:T(8,128)S(1)} %bitcast.181, ...), custom_call_target="tpu_custom_call" | custom-call | flops 4278190080 | bytes 31083776 | tf_op jit(solution)/shard_map/pallas_call | solution.py:53
  341.7 15.1 %shard_map.191 = (bf16[256,1024]{1,0:T(8,128)(2,1)S(1)}, bf16[4,2,640,128]{3,2,1,0:T(8,128)(2,1)S(1)}, bf16[4,2,640,128]{3,2,1,0:T(8,128)(2,1)S(1)}) custom-call(s32[1,3]{1,0:T(1,128)S(1)} %copy-done.159, bf16[256,1920]{1,0:T(8,128)(2,1)S(1)} %copy-done.109, bf16[256,1920]{1,0:T(8,128)(2,1)S(1)} %get-tuple-element.494.o_ref.refs_0_, ...), custom_call_target="tpu_custom_call" | custom-call | flops 5033164800 | bytes 9404428 | tf_op jit(solution)/shard_map/pallas_call | solution.py:53
  380.9 10.6 %collective-permute-done.70.refs_2_ = bf16[2,640,128]{2,1,0:T(8,128)(2,1)S(1)} collective-permute-done((bf16[2,640,128]{2,1,0:T(8,128)(2,1)S(1)}, bf16[2,640,128]{2,1,0:T(8,128)(2,1)S(1)}, u32[]{:S(2)}, u32[]{:S(2)}) %collective-permute-start.70) | collective-permute-done | bytes 327712 | tf_op jit(solution)/shard_map/ppermute | solution.py:102
  395.0 10.6 %shard_map.193 = (bf16[256,960]{1,0:T(8,128)(2,1)S(1)}, bf16[256,5120]{1,0:T(8,128)(2,1)S(1)}, bf16[256,2560]{1,0:T(8,128)(2,1)S(1)}, f32[256,960]{1,0:T(8,128)S...) custom-call(f32[256,960]{1,0:T(8,128)S(1)} %get-tuple-element.523.dh, ...), custom_call_target="tpu_custom_call" | custom-call | flops 4278190080 | bytes 31083776 | tf_op jit(solution)/shard_map/pallas_call | solution.py:53
  407.3 26.7 %shard_map.194 = (bf16[256,1024]{1,0:T(8,128)(2,1)S(1)}, bf16[4,2,640,128]{3,2,1,0:T(8,128)(2,1)S(1)}, bf16[4,2,640,128]{3,2,1,0:T(8,128)(2,1)S(1)}) custom-call(s32[1,3]{1,0:T(1,128)S(1)} %copy-done.159, bf16[256,1920]{1,0:T(8,128)(2,1)S(1)} %copy-done.107, bf16[256,1920]{1,0:T(8,128)(2,1)S(1)} %copy-done.56, ...), custom_call_target="tpu_custom_call" | custom-call | flops 5033164800 | bytes 9404428 | tf_op jit(solution)/shard_map/pallas_call | solution.py:53
  441.1 7.0 collective-permute-done.73.refs_1_
  448.3 7.1 collective-permute-done.75.refs_3_
  458.9 10.8 %shard_map.196 = (bf16[256,960]{1,0:T(8,128)(2,1)S(1)}, bf16[256,5120]{1,0:T(8,128)(2,1)S(1)}, bf16[256,2560]{1,0:T(8,128)(2,1)S(1)}, f32[256,960]{1,0:T(8,128)S...) custom-call(f32[256,960]{1,0:T(8,128)S(1)} %get-tuple-element.541.dh, ...), custom_call_target="tpu_custom_call" | custom-call | flops 4278190080 | bytes 31083776 | tf_op jit(solution)/shard_map/pallas_call | solution.py:53
  469.9 27.0 %shard_map.199 = (bf16[256,1024]{1,0:T(8,128)(2,1)S(1)}, bf16[4,2,640,128]{3,2,1,0:T(8,128)(2,1)S(1)}, bf16[4,2,640,128]{3,2,1,0:T(8,128)(2,1)}) custom-call(s32[1,3]{1,0:T(1,128)S(1)} %copy-done.159, bf16[256,1920]{1,0:T(8,128)(2,1)S(1)} %copy-done.105, bf16[256,1920]{1,0:T(8,128)(2,1)S(1)} %copy-done.54, bf16[256,1920]{1,0:T(8,128)(2,1)S(1)} %get-tuple-element.562.refs_1_, ...), custom_call_target="tpu_custom_call" | custom-call | flops 5033164800 | bytes 9404428 | tf_op jit(solution)/shard_map/pallas_call | solution.py:53
  497.8 18.3 %shard_map.198 = (bf16[4,4,32,5120]{3,2,1,0:T(8,128)(2,1)}, bf16[4,4,32,5120]{3,2,1,0:T(8,128)(2,1)}) custom-call(bf16[256,960]{1,0:T(8,128)(2,1)} %copy-done.117, bf16[256,960]{1,0:T(8,128)(2,1)} %copy-done.119, bf16[256,960]{1,0:T(8,128)(2,1)} %copy-done.123, bf16[256,5120]{1,0:T(8,128)(2,1)} %copy-done.99, bf16[256,5120]{1,0:T(8,128)(2,1)} %copy-done.98, ...), custom_call_target="tpu_custom_call" | custom-call | flops 7549747200 | bytes 19824640 | tf_op jit(solution)/shard_map/pallas_call | solution.py:53
  522.5 14.1 %shard_map.197 = (bf16[4,4,112,960]{3,2,1,0:T(8,128)(2,1)}, bf16[4,4,112,960]{3,2,1,0:T(8,128)(2,1)}) custom-call(bf16[256,1024]{1,0:T(8,128)(2,1)} %copy-done.116, bf16[256,1024]{1,0:T(8,128)(2,1)} %copy-done.118, bf16[256,1024]{1,0:T(8,128)(2,1)} %copy-done.120, bf16[256,2560]{1,0:T(8,128)(2,1)} %copy-done.102, bf16[256,2560]{1,0:T(8,128)(2,1)} %copy-done.101, ...), custom_call_target="tpu_custom_call" | custom-call | flops 5190451200 | bytes 15335424 | tf_op jit(solution)/shard_map/pallas_call | solution.py:53
  566.2 8.7 %shard_map.201 = (bf16[4,4,32,1664]{3,2,1,0:T(8,128)(2,1)}, bf16[4,4,32,1664]{3,2,1,0:T(8,128)(2,1)}) custom-call(bf16[256,960]{1,0:T(8,128)(2,1)} %copy-done.113, bf16[256,960]{1,0:T(8,128)(2,1)} %copy-done.114, bf16[256,960]{1,0:T(8,128)(2,1)} %copy-done.115, bf16[256,1664]{1,0:T(8,128)(2,1)} %copy-done.112, bf16[256,1664]{1,0:T(8,128)(2,1)} %copy-done.111, ...), custom_call_target="tpu_custom_call" | custom-call | flops 2453667840 | bytes 7864320 | tf_op jit(solution)/shard_map/pallas_call | solution.py:53
  585.7 10.5 %collective-permute-done.84 = bf16[2,32,5120]{2,1,0:T(8,128)(2,1)} collective-permute-done((bf16[2,32,5120]{2,1,0:T(8,128)(2,1)}, bf16[2,32,5120]{2,1,0:T(8,128)(2,1)}, u32[]{:S(2)}, u32[]{:S(2)}) %collective-permute-start.84) | collective-permute-done | bytes 655392 | tf_op jit(solution)/shard_map/ppermute | solution.py:102
  611.7 6.9 collective-permute-done.106
  622.2 8.5 %collective-permute-done.107 = bf16[32,5120]{1,0:T(8,128)(2,1)S(1)} collective-permute-done((bf16[32,5120]{1,0:T(8,128)(2,1)S(1)}, bf16[32,5120]{1,0:T(8,128)(2,1)S(1)}, u32[]{:S(2)}, u32[]{:S(2)}) %collective-permute-start.107) | collective-permute-done | bytes 327712 | tf_op jit(solution)/shard_map/ppermute | solution.py:102
  646.5 6.1 collective-permute-done.91
  675.9 8.0 %collective-permute-done.97 = bf16[112,960]{1,0:T(8,128)(2,1)S(1)} collective-permute-done((bf16[112,960]{1,0:T(8,128)(2,1)S(1)}, bf16[112,960]{1,0:T(8,128)(2,1)S(1)}, u32[]{:S(2)}, u32[]{:S(2)}) %collective-permute-start.97) | collective-permute-done | bytes 215072 | tf_op jit(solution)/shard_map/ppermute | solution.py:102
  697.6 6.4 collective-permute-done.100
  (768 shorter events, 374.8 us)
Async XLA Ops:
  3.0 20.5 %collective-permute-start = (bf16[32,1664]{1,0:T(8,128)(2,1)S(1)}, bf16[32,1664]{1,0:T(8,128)(2,1)S(1)}, u32[]{:S(2)}, u32[]{:S(2)}) collective-permute-start(bf16[32,1664]{1,0:T(8,128)(2,1)S(1)} %fusion.68), channel_id=1, source_target_pairs={{0,1},{1,2},{2,3},{3,0},{4,5},{5,6},{6,7},{7,4},{8,9},{9,10},{10,1... | collective-permute-start | bytes 319496 | tf_op jit(solution)/shard_map/ppermute | solution.py:102
  25.1 18.8 %collective-permute-start.17 = (bf16[112,960]{1,0:T(8,128)(2,1)S(1)}, bf16[112,960]{1,0:T(8,128)(2,1)S(1)}, u32[]{:S(2)}, u32[]{:S(2)}) collective-permute-start(bf16[112,960]{1,0:T(8,128)(2,1)S(1)} %fusion.62), channel_id=1, source_target_pairs={{0,2},{1,3},{2,0},{3,1},{4,6},{5,7},{6,4},{7,5},{8,10},{9,11},{10,... | collective-permute-start | bytes 645128 | tf_op jit(solution)/shard_map/ppermute | solution.py:102
  25.5 19.5 %collective-permute-start.18 = (bf16[112,960]{1,0:T(8,128)(2,1)S(1)}, bf16[112,960]{1,0:T(8,128)(2,1)S(1)}, u32[]{:S(2)}, u32[]{:S(2)}) collective-permute-start(bf16[112,960]{1,0:T(8,128)(2,1)S(1)} %fusion.62), channel_id=1, source_target_pairs={{0,3},{1,0},{2,1},{3,2},{4,7},{5,4},{6,5},{7,6},{8,11},{9,8},{10,9... | collective-permute-start | bytes 645128 | tf_op jit(solution)/shard_map/ppermute | solution.py:102
  29.5 20.1 %collective-permute-start.12 = (bf16[128,960]{0,1:T(8,128)(2,1)S(1)}, bf16[128,960]{0,1:T(8,128)(2,1)S(1)}, u32[]{:S(2)}, u32[]{:S(2)}) collective-permute-start(bf16[128,960]{0,1:T(8,128)(2,1)S(1)} %get-tuple-element.369), channel_id=1, source_target_pairs={{0,4},{4,12},{8,20},{12,28},{16,24},{20,16},{24,8},{28,0},{1,5},{5... | collective-permute-start | bytes 737288 | tf_op jit(solution)/shard_map/ppermute | solution.py:102
  29.6 20.0 %collective-permute-start.7 = (bf16[3,32,1664]{2,1,0:T(8,128)(2,1)S(1)}, bf16[3,32,1664]{2,1,0:T(8,128)(2,1)S(1)}, u32[]{:S(2)}, u32[]{:S(2)}) collective-permute-start(bf16[3,32,1664]{2,1,0:T(8,128)(2,1)S(1)} %pad_maximum_fusion.8.refs_1_), channel_id=1, source_target_pairs={{0,4},{4,0},{8,12},{12,8},{16,20},{20,16},{24,28},{28,24},{1,5},{5... | collective-permute-start | bytes 958472 | tf_op jit(solution)/shard_map/ppermute | solution.py:102
  49.5 19.1 %collective-permute-start.19 = (bf16[3,112,960]{2,1,0:T(8,128)(2,1)}, bf16[3,112,960]{2,1,0:T(8,128)(2,1)}, u32[]{:S(2)}, u32[]{:S(2)}) collective-permute-start(bf16[3,112,960]{2,1,0:T(8,128)(2,1)} %pad_maximum_fusion.6.refs_2_), channel_id=1, source_target_pairs={{0,8},{4,12},{8,0},{12,4},{16,24},{20,28},{24,16},{28,20},{1,9},{5... | collective-permute-start | bytes 1935368 | tf_op jit(solution)/shard_map/ppermute | solution.py:102
  49.6 24.6 %collective-permute-start.20 = (bf16[3,112,960]{2,1,0:T(8,128)(2,1)}, bf16[3,112,960]{2,1,0:T(8,128)(2,1)}, u32[]{:S(2)}, u32[]{:S(2)}) collective-permute-start(bf16[3,112,960]{2,1,0:T(8,128)(2,1)} %pad_maximum_fusion.6.refs_2_), channel_id=1, source_target_pairs={{0,16},{4,20},{8,24},{12,28},{16,0},{20,4},{24,8},{28,12},{1,17},{... | collective-permute-start | bytes 1935368 | tf_op jit(solution)/shard_map/ppermute | solution.py:102
  62.8 20.2 %collective-permute-start.31 = (bf16[3,32,1664]{2,1,0:T(8,128)(2,1)S(1)}, bf16[3,32,1664]{2,1,0:T(8,128)(2,1)S(1)}, u32[]{:S(2)}, u32[]{:S(2)}) collective-permute-start(bf16[3,32,1664]{2,1,0:T(8,128)(2,1)S(1)} %collective-permute-done.8.refs_3_), channel_id=1, source_target_pairs={{0,4},{4,0},{8,12},{12,8},{16,20},{20,16},{24,28},{28,24},{1,5},{5... | collective-permute-start | bytes 958472 | tf_op jit(solution)/shard_map/ppermute | solution.py:102
  62.9 20.2 %collective-permute-start.32 = (bf16[3,32,1664]{2,1,0:T(8,128)(2,1)S(1)}, bf16[3,32,1664]{2,1,0:T(8,128)(2,1)S(1)}, u32[]{:S(2)}, u32[]{:S(2)}) collective-permute-start(bf16[3,32,1664]{2,1,0:T(8,128)(2,1)S(1)} %collective-permute-done.9.refs_4_), channel_id=1, source_target_pairs={{0,4},{4,0},{8,12},{12,8},{16,20},{20,16},{24,28},{28,24},{1,5},{5... | collective-permute-start | bytes 958472 | tf_op jit(solution)/shard_map/ppermute | solution.py:102
  68.6 20.3 %collective-permute-start.27 = (bf16[32,5120]{1,0:T(8,128)(2,1)}, bf16[32,5120]{1,0:T(8,128)(2,1)S(1)}, u32[]{:S(2)}, u32[]{:S(2)}) collective-permute-start(bf16[32,5120]{1,0:T(8,128)(2,1)} %pad_dynamic-slice_fusion), channel_id=1, source_target_pairs={{0,2},{1,3},{2,0},{3,1},{4,6},{5,7},{6,4},{7,5},{8,10},{9,11},{10,... | collective-permute-start | bytes 983048 | tf_op jit(solution)/shard_map/ppermute | solution.py:102
  83.1 20.4 %collective-permute-start.23 = (bf16[3,112,960]{2,1,0:T(8,128)(2,1)}, bf16[3,112,960]{2,1,0:T(8,128)(2,1)}, u32[]{:S(2)}, u32[]{:S(2)}) collective-permute-start(bf16[3,112,960]{2,1,0:T(8,128)(2,1)} %pad_maximum_fusion.6.refs_2_), channel_id=1, source_target_pairs={{0,4},{4,0},{8,12},{12,8},{16,20},{20,16},{24,28},{28,24},{1,5},{5... | collective-permute-start | bytes 1935368 | tf_op jit(solution)/shard_map/ppermute | solution.py:102
  83.2 20.6 %collective-permute-start.24 = (bf16[3,112,960]{2,1,0:T(8,128)(2,1)}, bf16[3,112,960]{2,1,0:T(8,128)(2,1)}, u32[]{:S(2)}, u32[]{:S(2)}) collective-permute-start(bf16[3,112,960]{2,1,0:T(8,128)(2,1)} %collective-permute-done.19.refs_3_), channel_id=1, source_target_pairs={{0,4},{4,0},{8,12},{12,8},{16,20},{20,16},{24,28},{28,24},{1,5},{5... | collective-permute-start | bytes 1935368 | tf_op jit(solution)/shard_map/ppermute | solution.py:102
  83.6 21.3 %collective-permute-start.25 = (bf16[3,112,960]{2,1,0:T(8,128)(2,1)}, bf16[3,112,960]{2,1,0:T(8,128)(2,1)}, u32[]{:S(2)}, u32[]{:S(2)}) collective-permute-start(bf16[3,112,960]{2,1,0:T(8,128)(2,1)} %collective-permute-done.20.refs_4_), channel_id=1, source_target_pairs={{0,4},{4,0},{8,12},{12,8},{16,20},{20,16},{24,28},{28,24},{1,5},{5... | collective-permute-start | bytes 1935368 | tf_op jit(solution)/shard_map/ppermute | solution.py:102
  103.4 17.9 %collective-permute-start.36 = (bf16[256,640]{1,0:T(8,128)(2,1)}, bf16[256,640]{1,0:T(8,128)(2,1)S(1)}, u32[]{:S(2)}, u32[]{:S(2)}) collective-permute-start(bf16[256,640]{1,0:T(8,128)(2,1)} %get-tuple-element.419.refs_0_.refs_7_), channel_id=1, source_target_pairs={{0,16},{4,20},{8,24},{12,28},{16,0},{20,4},{24,8},{28,12},{1,17},{... | collective-permute-start | bytes 983048 | tf_op jit(solution)/shard_map/ppermute | solution.py:102
  105.1 58.0 %collective-permute-start.29 = (bf16[3,32,5120]{2,1,0:T(8,128)(2,1)S(1)}, bf16[3,32,5120]{2,1,0:T(8,128)(2,1)}, u32[]{:S(2)}, u32[]{:S(2)}) collective-permute-start(bf16[3,32,5120]{2,1,0:T(8,128)(2,1)S(1)} %pad_maximum_fusion.3.refs_1_), channel_id=1, source_target_pairs={{0,8},{4,12},{8,0},{12,4},{16,24},{20,28},{24,16},{28,20},{1,9},{5... | collective-permute-start | bytes 2949128 | tf_op jit(solution)/shard_map/ppermute | solution.py:102
  107.9 55.1 %collective-permute-start.30 = (bf16[3,32,5120]{2,1,0:T(8,128)(2,1)S(1)}, bf16[3,32,5120]{2,1,0:T(8,128)(2,1)}, u32[]{:S(2)}, u32[]{:S(2)}) collective-permute-start(bf16[3,32,5120]{2,1,0:T(8,128)(2,1)S(1)} %pad_maximum_fusion.3.refs_1_), channel_id=1, source_target_pairs={{0,16},{4,20},{8,24},{12,28},{16,0},{20,4},{24,8},{28,12},{1,17},{... | collective-permute-start | bytes 2949128 | tf_op jit(solution)/shard_map/ppermute | solution.py:102
  497.8 18.3 %collective-permute-start.76 = (bf16[4,2,640,128]{3,2,1,0:T(8,128)(2,1)}, bf16[4,2,640,128]{3,2,1,0:T(8,128)(2,1)}, u32[]{:S(2)}, u32[]{:S(2)}) collective-permute-start(bf16[4,2,640,128]{3,2,1,0:T(8,128)(2,1)} %get-tuple-element.566), channel_id=1, source_target_pairs={{0,4},{4,0},{8,12},{12,8},{16,20},{20,16},{24,28},{28,24},{1,5},{5... | collective-permute-start | bytes 3932168 | tf_op jit(solution)/shard_map/ppermute | solution.py:102
  516.1 20.5 %collective-permute-start.80 = (bf16[4,4,32,5120]{3,2,1,0:T(8,128)(2,1)}, bf16[4,4,32,5120]{3,2,1,0:T(8,128)(2,1)}, u32[]{:S(2)}, u32[]{:S(2)}) collective-permute-start(bf16[4,4,32,5120]{3,2,1,0:T(8,128)(2,1)} %get-tuple-element.573), channel_id=1, source_target_pairs={{0,4},{4,0},{8,12},{12,8},{16,20},{20,16},{24,28},{28,24},{1,5},{5... | collective-permute-start | bytes 15728648 | tf_op jit(solution)/shard_map/ppermute | solution.py:102
  542.7 32.3 %collective-permute-start.83 = (bf16[4,4,112,960]{3,2,1,0:T(8,128)(2,1)}, bf16[4,4,112,960]{3,2,1,0:T(8,128)(2,1)}, u32[]{:S(2)}, u32[]{:S(2)}) collective-permute-start(bf16[4,4,112,960]{3,2,1,0:T(8,128)(2,1)} %get-tuple-element.582), channel_id=1, source_target_pairs={{0,4},{4,0},{8,12},{12,8},{16,20},{20,16},{24,28},{28,24},{1,5},{5... | collective-permute-start | bytes 10321928 | tf_op jit(solution)/shard_map/ppermute | solution.py:102
  542.7 32.2 %collective-permute-start.81 = (bf16[2,2,32,5120]{3,2,1,0:T(8,128)(2,1)}, bf16[2,2,32,5120]{3,2,1,0:T(8,128)(2,1)}, u32[]{:S(2)}, u32[]{:S(2)}) collective-permute-start(bf16[2,2,32,5120]{3,2,1,0:T(8,128)(2,1)} %pad_maximum_fusion), channel_id=1, source_target_pairs={{0,8},{4,12},{8,0},{12,4},{16,24},{20,28},{24,16},{28,20},{1,9},{5... | collective-permute-start | bytes 3932168 | tf_op jit(solution)/shard_map/ppermute | solution.py:102
  543.7 31.2 %collective-permute-start.82 = (bf16[2,2,32,5120]{3,2,1,0:T(8,128)(2,1)}, bf16[2,2,32,5120]{3,2,1,0:T(8,128)(2,1)}, u32[]{:S(2)}, u32[]{:S(2)}) collective-permute-start(bf16[2,2,32,5120]{3,2,1,0:T(8,128)(2,1)} %pad_maximum_fusion.1), channel_id=1, source_target_pairs={{0,16},{4,20},{8,24},{12,28},{16,0},{20,4},{24,8},{28,12},{1,17},{... | collective-permute-start | bytes 3932168 | tf_op jit(solution)/shard_map/ppermute | solution.py:102
  575.0 22.2 %collective-permute-start.86 = (bf16[4,4,32,1664]{3,2,1,0:T(8,128)(2,1)}, bf16[4,4,32,1664]{3,2,1,0:T(8,128)(2,1)S(1)}, u32[]{:S(2)}, u32[]{:S(2)}) collective-permute-start(bf16[4,4,32,1664]{3,2,1,0:T(8,128)(2,1)} %get-tuple-element.608), channel_id=1, source_target_pairs={{0,4},{4,0},{8,12},{12,8},{16,20},{20,16},{24,28},{28,24},{1,5},{5... | collective-permute-start | bytes 5111816 | tf_op jit(solution)/shard_map/ppermute | solution.py:102
  597.2 39.3 %collective-permute-start.87 = (bf16[2,2,112,960]{3,2,1,0:T(8,128)(2,1)}, bf16[2,2,112,960]{3,2,1,0:T(8,128)(2,1)}, u32[]{:S(2)}, u32[]{:S(2)}) collective-permute-start(bf16[2,2,112,960]{3,2,1,0:T(8,128)(2,1)} %pad_maximum_fusion.4), channel_id=1, source_target_pairs={{0,8},{4,12},{8,0},{12,4},{16,24},{20,28},{24,16},{28,20},{1,9},{5... | collective-permute-start | bytes 2580488 | tf_op jit(solution)/shard_map/ppermute | solution.py:102
  597.9 38.6 %collective-permute-start.88 = (bf16[2,2,112,960]{3,2,1,0:T(8,128)(2,1)}, bf16[2,2,112,960]{3,2,1,0:T(8,128)(2,1)}, u32[]{:S(2)}, u32[]{:S(2)}) collective-permute-start(bf16[2,2,112,960]{3,2,1,0:T(8,128)(2,1)} %pad_maximum_fusion.5), channel_id=1, source_target_pairs={{0,16},{4,20},{8,24},{12,28},{16,0},{20,4},{24,8},{28,12},{1,17},{... | collective-permute-start | bytes 2580488 | tf_op jit(solution)/shard_map/ppermute | solution.py:102
  607.1 23.5 %collective-permute-start.107 = (bf16[32,5120]{1,0:T(8,128)(2,1)S(1)}, bf16[32,5120]{1,0:T(8,128)(2,1)S(1)}, u32[]{:S(2)}, u32[]{:S(2)}) collective-permute-start(bf16[32,5120]{1,0:T(8,128)(2,1)S(1)} %get-tuple-element.645), channel_id=1, source_target_pairs={{0,2},{1,3},{2,0},{3,1},{4,6},{5,7},{6,4},{7,5},{8,10},{9,11},{10,... | collective-permute-start | bytes 983048 | tf_op jit(solution)/shard_map/ppermute | solution.py:102
  610.8 21.7 %collective-permute-start.108 = (bf16[32,5120]{1,0:T(8,128)(2,1)S(1)}, bf16[32,5120]{1,0:T(8,128)(2,1)}, u32[]{:S(2)}, u32[]{:S(2)}) collective-permute-start(bf16[32,5120]{1,0:T(8,128)(2,1)S(1)} %get-tuple-element.646), channel_id=1, source_target_pairs={{0,3},{1,0},{2,1},{3,2},{4,7},{5,4},{6,5},{7,6},{8,11},{9,8},{10,9... | collective-permute-start | bytes 983048 | tf_op jit(solution)/shard_map/ppermute | solution.py:102
  646.2 17.9 %collective-permute-start.109 = (bf16[32,5120]{1,0:T(8,128)(2,1)S(1)}, bf16[32,5120]{1,0:T(8,128)(2,1)S(1)}, u32[]{:S(2)}, u32[]{:S(2)}) collective-permute-start(bf16[32,5120]{1,0:T(8,128)(2,1)S(1)} %fusion.10.refs_0_), channel_id=1, source_target_pairs={{0,4},{4,0},{8,12},{12,8},{16,20},{20,16},{24,28},{28,24},{1,5},{5... | collective-permute-start | bytes 983048 | tf_op jit(solution)/shard_map/ppermute | solution.py:102
  646.3 18.5 %collective-permute-start.110 = (bf16[32,5120]{1,0:T(8,128)(2,1)S(1)}, bf16[32,5120]{1,0:T(8,128)(2,1)S(1)}, u32[]{:S(2)}, u32[]{:S(2)}) collective-permute-start(bf16[32,5120]{1,0:T(8,128)(2,1)S(1)} %fusion.10.refs_0_), channel_id=1, source_target_pairs={{0,8},{4,12},{8,0},{12,4},{16,24},{20,28},{24,16},{28,20},{1,9},{5... | collective-permute-start | bytes 983048 | tf_op jit(solution)/shard_map/ppermute | solution.py:102
  646.3 18.5 %collective-permute-start.111 = (bf16[32,5120]{1,0:T(8,128)(2,1)S(1)}, bf16[32,5120]{1,0:T(8,128)(2,1)S(1)}, u32[]{:S(2)}, u32[]{:S(2)}) collective-permute-start(bf16[32,5120]{1,0:T(8,128)(2,1)S(1)} %fusion.10.refs_0_), channel_id=1, source_target_pairs={{0,16},{4,20},{8,24},{12,28},{16,0},{20,4},{24,8},{28,12},{1,17},{... | collective-permute-start | bytes 983048 | tf_op jit(solution)/shard_map/ppermute | solution.py:102
  664.1 22.4 %collective-permute-start.93 = (bf16[4,32,1664]{2,1,0:T(8,128)(2,1)S(1)}, bf16[4,32,1664]{2,1,0:T(8,128)(2,1)S(1)}, u32[]{:S(2)}, u32[]{:S(2)}) collective-permute-start(bf16[4,32,1664]{2,1,0:T(8,128)(2,1)S(1)} %get-tuple-element.623), channel_id=1, source_target_pairs={{0,8},{4,12},{8,0},{12,4},{16,24},{20,28},{24,16},{28,20},{1,9},{5... | collective-permute-start | bytes 1277960 | tf_op jit(solution)/shard_map/ppermute | solution.py:102
  664.8 22.2 %collective-permute-start.94 = (bf16[4,32,1664]{2,1,0:T(8,128)(2,1)S(1)}, bf16[4,32,1664]{2,1,0:T(8,128)(2,1)S(1)}, u32[]{:S(2)}, u32[]{:S(2)}) collective-permute-start(bf16[4,32,1664]{2,1,0:T(8,128)(2,1)S(1)} %get-tuple-element.624), channel_id=1, source_target_pairs={{0,16},{4,20},{8,24},{12,28},{16,0},{20,4},{24,8},{28,12},{1,17},{... | collective-permute-start | bytes 1277960 | tf_op jit(solution)/shard_map/ppermute | solution.py:102
  664.8 22.3 %collective-permute-start.95 = (bf16[4,32,1664]{2,1,0:T(8,128)(2,1)S(1)}, bf16[4,32,1664]{2,1,0:T(8,128)(2,1)S(1)}, u32[]{:S(2)}, u32[]{:S(2)}) collective-permute-start(bf16[4,32,1664]{2,1,0:T(8,128)(2,1)S(1)} %get-tuple-element.625), channel_id=1, source_target_pairs={{0,24},{4,28},{8,16},{12,20},{16,8},{20,12},{24,0},{28,4},{1,25},{... | collective-permute-start | bytes 1277960 | tf_op jit(solution)/shard_map/ppermute | solution.py:102
  (295 other events, 2940.0 us)

commit v6 on v5

--- a/solution.py
+++ b/solution.py
@@ -983,7 +983,7 @@
         + [pltpu.VMEM((tokens, l[0].shape[1]), BF) for l in lefts]
         + [pltpu.SemaphoreType.DMA((2 * k * STEPS,))],
         2 * tokens * sum(rows_z) * count * cols,
-        58,
+        42,
     )
 
 
@@ -1021,7 +1021,7 @@
         [VMEM] * len(segments),
         [],
         0,
-        32,
+        16,
     )
 
 

time: 741 us -> 752 us (1.015)
  local copies, waits for them, and re-layouts: 94.3 us -> 113 us
  Pallas kernels: 250 us -> 239 us
    unnamed x404 -> x458, local copies, waits for them, and re-layouts: 69.6 us -> 88.6 us
    pallas_call x27, Pallas kernels: 250 us -> 239 us  [call(): pl.pallas_call(kernel, out_shape=outs, in_specs=specs, out_specs=out_spec...]
  transfers between devices with their start and end apart: 126 -> 126, of which waited for: 42 -> 42; matrix products, arithmetic and copies ran while one was open for 9% -> 9% of each run, Pallas kernels for 11% -> 9%
where the time goes in v6:
time: 752 us; the launch traced here: 741 us
  Pallas kernels  239 us (32%)
  waiting for transfers between devices  180 us (24%)
  starting transfers between devices  151 us (20%)
  local copies, waits for them, and re-layouts  113 us (15%)
  other arithmetic  51.7 us (7%)
    pallas_call x27, Pallas kernels, call(): pl.pallas_call(kernel, out_shape=outs, in_specs=specs, out_specs=out_spec...  239 us
    ppermute x126, waiting for transfers between devices, start(): lax.ppermute(x, axis, perm)  180 us
    ppermute x126, starting transfers between devices, start(): lax.ppermute(x, axis, perm)  151 us
    unnamed x458, local copies, waits for them, and re-layouts  88.6 us
  transfers between devices with their start and end apart: 126, of which 42 were waited for; matrix products, arithmetic and copies ran while one was open for 9% of the time, Pallas kernels for 9%

profile of v6, /device:TPU:0, one launch (start us, length us, event | category | flops | bytes accessed | tf_op | source)
XLA Modules:
  0.0 741.4 jit_solution(12590955213144043431)
XLA Ops:
  37.2 6.9 collective-permute-done.17
  54.7 6.6 collective-permute-done.9.refs_4_
  112.3 9.1 %collective-permute-done.36.refs_3_.refs_10_ = bf16[256,640]{1,0:T(8,128)(2,1)S(1)} collective-permute-done((bf16[256,640]{1,0:T(8,128)(2,1)}, bf16[256,640]{1,0:T(8,128)(2,1)S(1)}, u32[]{:S(2)}, u32[]{:S(2)}) %collective-permute-start.36) | collective-permute-done | bytes 327712 | tf_op jit(solution)/shard_map/ppermute | solution.py:102
  141.4 20.8 %shard_map.180 = (bf16[256,1920]{1,0:T(8,128)(2,1)S(1)}, f32[2,384,128]{2,1,0:T(8,128)S(1)}) custom-call(s32[1,3]{1,0:T(1,128)S(1)} %fusion.99.flag_ref, bf16[256,1920]{1,0:T(8,128)(2,1)S(1)} %copy-done.105, s32[6,1024]{1,0:T(8,128)S(1)} %pad_add_fusion.keys_ref.refs_3_, s32[256,8]{1,0:T(8,128)S(1)} %copy.108.meta_ref.refs_4_, ...), custom_call_target="tpu_custom_call" | custom-call | flops 2013265920 | bytes 5013516 | tf_op jit(solution)/shard_map/pallas_call | solution.py:53
  168.4 12.0 %collective-permute-done.43.refs_4_ = bf16[3,16,5120]{2,1,0:T(8,128)(2,1)} collective-permute-done((bf16[3,16,5120]{2,1,0:T(8,128)(2,1)S(1)}, bf16[3,16,5120]{2,1,0:T(8,128)(2,1)}, u32[]{:S(2)}, u32[]{:S(2)}) %collective-permute-start.43) | collective-permute-done | bytes 491552 | tf_op jit(solution)/shard_map/ppermute | solution.py:102
  201.0 8.5 %shard_map.183 = (bf16[256,1024]{1,0:T(8,128)(2,1)S(1)}, f32[256,960]{1,0:T(8,128)S(1)}, bf16[256,960]{1,0:T(8,128)(2,1)S(1)}, bf16[256,5120]{1,0:T(8,128)(2,1)S...) custom-call(bf16[256,1920]{1,0:T(8,128)(2,1)S(1)} %copy-done.54, f32[256,960]{1,0:T(8,128)S(1)} %bitcast.178, ...), custom_call_target="tpu_custom_call" | custom-call | flops 4278190080 | bytes 25083392 | tf_op jit(solution)/shard_map/pallas_call | solution.py:53
  218.5 7.0 collective-permute-done.51.refs_2_.refs_9_
  238.8 7.1 collective-permute-done.58
  246.7 21.9 %shard_map.185 = (bf16[256,1920]{1,0:T(8,128)(2,1)S(1)}, f32[2,384,128]{2,1,0:T(8,128)S(1)}) custom-call(s32[1,3]{1,0:T(1,128)S(1)} %copy-done.182, bf16[256,1920]{1,0:T(8,128)(2,1)S(1)} %get-tuple-element.458.q_ref, s32[6,1024]{1,0:T(8,128)S(1)} %copy-done.92, s32[256,8]{1,0:T(8,128)S(1)} %copy.108.meta_ref.refs_4_, ...), custom_call_target="tpu_custom_call" | custom-call | flops 2013265920 | bytes 5013516 | tf_op jit(solution)/shard_map/pallas_call | solution.py:53
  272.9 8.5 %shard_map.186 = (bf16[256,1024]{1,0:T(8,128)(2,1)S(1)}, f32[256,960]{1,0:T(8,128)S(1)}, bf16[256,960]{1,0:T(8,128)(2,1)S(1)}, bf16[256,5120]{1,0:T(8,128)(2,1)S...) custom-call(bf16[256,1920]{1,0:T(8,128)(2,1)S(1)} %get-tuple-element.476.o_ref.refs_0_, f32[256,960]{1,0:T(8,128)S(1)} %copy-done.8, ...), custom_call_target="tpu_custom_call" | custom-call | flops 4278190080 | bytes 25083392 | tf_op jit(solution)/shard_map/pallas_call | solution.py:53
  293.2 6.0 collective-permute-done.60.refs_2_.refs_9_
  299.2 6.7 collective-permute-done.61.refs_3_.refs_10_
  308.7 9.7 %shard_map.188 = (bf16[256,1920]{1,0:T(8,128)(2,1)S(1)}, f32[2,384,128]{2,1,0:T(8,128)S(1)}) custom-call(s32[1,3]{1,0:T(1,128)S(1)} %copy-done.183, bf16[256,1920]{1,0:T(8,128)(2,1)S(1)} %copy-done.110, s32[6,1024]{1,0:T(8,128)S(1)} %copy-done.93, s32[256,8]{1,0:T(8,128)S(1)} %copy.108.meta_ref.refs_4_, bf16[256,640]{1,0:T(8,128)(2,1)} %get-tuple-element.483.refs_0_.refs_7_, ...), custom_call_target="tpu_custom_call" | custom-call | flops 2013265920 | bytes 5013516 | tf_op jit(solution)/shard_map/pallas_call | solution.py:53
  322.3 8.7 %shard_map.189 = (bf16[256,1024]{1,0:T(8,128)(2,1)S(1)}, f32[256,960]{1,0:T(8,128)S(1)}, bf16[256,960]{1,0:T(8,128)(2,1)S(1)}, bf16[256,5120]{1,0:T(8,128)(2,1)S...) custom-call(bf16[256,1920]{1,0:T(8,128)(2,1)S(1)} %get-tuple-element.494.o_ref.refs_0_, f32[256,960]{1,0:T(8,128)S(1)} %copy-done.11, ...), custom_call_target="tpu_custom_call" | custom-call | flops 4278190080 | bytes 25083392 | tf_op jit(solution)/shard_map/pallas_call | solution.py:53
  331.8 10.6 %shard_map.190 = (bf16[256,960]{1,0:T(8,128)(2,1)S(1)}, bf16[256,5120]{1,0:T(8,128)(2,1)S(1)}, bf16[256,2560]{1,0:T(8,128)(2,1)S(1)}, f32[256,960]{1,0:T(8,128)S...) custom-call(f32[256,960]{1,0:T(8,128)S(1)} %bitcast.181, ...), custom_call_target="tpu_custom_call" | custom-call | flops 4278190080 | bytes 31083776 | tf_op jit(solution)/shard_map/pallas_call | solution.py:53
  342.5 14.3 %shard_map.191 = (bf16[256,1024]{1,0:T(8,128)(2,1)S(1)}, bf16[4,2,640,128]{3,2,1,0:T(8,128)(2,1)S(1)}, bf16[4,2,640,128]{3,2,1,0:T(8,128)(2,1)S(1)}) custom-call(s32[1,3]{1,0:T(1,128)S(1)} %copy-done.183, bf16[256,1920]{1,0:T(8,128)(2,1)S(1)} %copy-done.111, bf16[256,1920]{1,0:T(8,128)(2,1)S(1)} %get-tuple-element.494.o_ref.refs_0_, ...), custom_call_target="tpu_custom_call" | custom-call | flops 5033164800 | bytes 9404428 | tf_op jit(solution)/shard_map/pallas_call | solution.py:53
  368.4 5.8 collective-permute-start.69
  380.9 10.6 %collective-permute-done.70.refs_2_ = bf16[2,640,128]{2,1,0:T(8,128)(2,1)S(1)} collective-permute-done((bf16[2,640,128]{2,1,0:T(8,128)(2,1)S(1)}, bf16[2,640,128]{2,1,0:T(8,128)(2,1)S(1)}, u32[]{:S(2)}, u32[]{:S(2)}) %collective-permute-start.70) | collective-permute-done | bytes 327712 | tf_op jit(solution)/shard_map/ppermute | solution.py:102
  395.0 10.6 %shard_map.193 = (bf16[256,960]{1,0:T(8,128)(2,1)S(1)}, bf16[256,5120]{1,0:T(8,128)(2,1)S(1)}, bf16[256,2560]{1,0:T(8,128)(2,1)S(1)}, f32[256,960]{1,0:T(8,128)S...) custom-call(f32[256,960]{1,0:T(8,128)S(1)} %get-tuple-element.523.dh, ...), custom_call_target="tpu_custom_call" | custom-call | flops 4278190080 | bytes 31083776 | tf_op jit(solution)/shard_map/pallas_call | solution.py:53
  412.1 26.7 %shard_map.194 = (bf16[256,1024]{1,0:T(8,128)(2,1)S(1)}, bf16[4,2,640,128]{3,2,1,0:T(8,128)(2,1)S(1)}, bf16[4,2,640,128]{3,2,1,0:T(8,128)(2,1)S(1)}) custom-call(s32[1,3]{1,0:T(1,128)S(1)} %copy-done.183, bf16[256,1920]{1,0:T(8,128)(2,1)S(1)} %copy-done.108, bf16[256,1920]{1,0:T(8,128)(2,1)S(1)} %copy-done.57, ...), custom_call_target="tpu_custom_call" | custom-call | flops 5033164800 | bytes 9404428 | tf_op jit(solution)/shard_map/pallas_call | solution.py:53
  446.0 7.0 collective-permute-done.73.refs_1_
  453.3 7.0 collective-permute-done.75.refs_3_
  463.8 10.8 %shard_map.196 = (bf16[256,960]{1,0:T(8,128)(2,1)S(1)}, bf16[256,5120]{1,0:T(8,128)(2,1)S(1)}, bf16[256,2560]{1,0:T(8,128)(2,1)S(1)}, f32[256,960]{1,0:T(8,128)S...) custom-call(f32[256,960]{1,0:T(8,128)S(1)} %get-tuple-element.541.dh, ...), custom_call_target="tpu_custom_call" | custom-call | flops 4278190080 | bytes 31083776 | tf_op jit(solution)/shard_map/pallas_call | solution.py:53
  479.2 26.1 %shard_map.199 = (bf16[256,1024]{1,0:T(8,128)(2,1)S(1)}, bf16[4,2,640,128]{3,2,1,0:T(8,128)(2,1)S(1)}, bf16[4,2,640,128]{3,2,1,0:T(8,128)(2,1)S(1)}) custom-call(s32[1,3]{1,0:T(1,128)S(1)} %copy-done.183, bf16[256,1920]{1,0:T(8,128)(2,1)S(1)} %copy-done.106, bf16[256,1920]{1,0:T(8,128)(2,1)S(1)} %copy-done.55, ...), custom_call_target="tpu_custom_call" | custom-call | flops 5033164800 | bytes 9404428 | tf_op jit(solution)/shard_map/pallas_call | solution.py:53
  506.2 15.6 %shard_map.198 = (bf16[4,4,32,5120]{3,2,1,0:T(8,128)(2,1)}, bf16[4,4,32,5120]{3,2,1,0:T(8,128)(2,1)}) custom-call(bf16[256,960]{1,0:T(8,128)(2,1)S(1)} %copy-done.127, bf16[256,960]{1,0:T(8,128)(2,1)S(1)} %copy-done.131, bf16[256,960]{1,0:T(8,128)(2,1)S(1)} %copy-done.137, bf16[256,5120]{1,0:T(8,128)(2,1)S(1)} %get-tuple-element.558.refs_3_, ...), custom_call_target="tpu_custom_call" | custom-call | flops 7549747200 | bytes 19824640 | tf_op jit(solution)/shard_map/pallas_call | solution.py:53
  531.0 10.9 %shard_map.197 = (bf16[4,4,112,960]{3,2,1,0:T(8,128)(2,1)S(1)}, bf16[4,4,112,960]{3,2,1,0:T(8,128)(2,1)}) custom-call(bf16[256,1024]{1,0:T(8,128)(2,1)S(1)} %copy-done.125, bf16[256,1024]{1,0:T(8,128)(2,1)S(1)} %copy-done.129, bf16[256,1024]{1,0:T(8,128)(2,1)S(1)} %get-tuple-element.511.refs_2_, bf16[256,2560]{1,0:T(8,128)(2,1)S(1)} %get-tuple-element.545.refs_3_, ...), custom_call_target="tpu_custom_call" | custom-call | flops 5190451200 | bytes 15335424 | tf_op jit(solution)/shard_map/pallas_call | solution.py:53
  594.9 10.7 %collective-permute-done.84 = bf16[2,32,5120]{2,1,0:T(8,128)(2,1)S(1)} collective-permute-done((bf16[2,32,5120]{2,1,0:T(8,128)(2,1)}, bf16[2,32,5120]{2,1,0:T(8,128)(2,1)S(1)}, u32[]{:S(2)}, u32[]{:S(2)}) %collective-permute-start.84) | collective-permute-done | bytes 655392 | tf_op jit(solution)/shard_map/ppermute | solution.py:102
  620.9 7.0 collective-permute-done.106
  631.4 8.5 %collective-permute-done.107 = bf16[32,5120]{1,0:T(8,128)(2,1)S(1)} collective-permute-done((bf16[32,5120]{1,0:T(8,128)(2,1)S(1)}, bf16[32,5120]{1,0:T(8,128)(2,1)S(1)}, u32[]{:S(2)}, u32[]{:S(2)}) %collective-permute-start.107) | collective-permute-done | bytes 327712 | tf_op jit(solution)/shard_map/ppermute | solution.py:102
  656.2 6.1 collective-permute-done.91
  685.3 8.0 %collective-permute-done.97 = bf16[112,960]{1,0:T(8,128)(2,1)S(1)} collective-permute-done((bf16[112,960]{1,0:T(8,128)(2,1)S(1)}, bf16[112,960]{1,0:T(8,128)(2,1)S(1)}, u32[]{:S(2)}, u32[]{:S(2)}) %collective-permute-start.97) | collective-permute-done | bytes 215072 | tf_op jit(solution)/shard_map/ppermute | solution.py:102
  708.1 6.4 collective-permute-done.100
  (822 shorter events, 395.4 us)
Async XLA Ops:
  3.0 20.6 %collective-permute-start = (bf16[32,1664]{1,0:T(8,128)(2,1)S(1)}, bf16[32,1664]{1,0:T(8,128)(2,1)S(1)}, u32[]{:S(2)}, u32[]{:S(2)}) collective-permute-start(bf16[32,1664]{1,0:T(8,128)(2,1)S(1)} %fusion.68), channel_id=1, source_target_pairs={{0,1},{1,2},{2,3},{3,0},{4,5},{5,6},{6,7},{7,4},{8,9},{9,10},{10,1... | collective-permute-start | bytes 319496 | tf_op jit(solution)/shard_map/ppermute | solution.py:102
  25.2 18.8 %collective-permute-start.17 = (bf16[112,960]{1,0:T(8,128)(2,1)S(1)}, bf16[112,960]{1,0:T(8,128)(2,1)S(1)}, u32[]{:S(2)}, u32[]{:S(2)}) collective-permute-start(bf16[112,960]{1,0:T(8,128)(2,1)S(1)} %fusion.62), channel_id=1, source_target_pairs={{0,2},{1,3},{2,0},{3,1},{4,6},{5,7},{6,4},{7,5},{8,10},{9,11},{10,... | collective-permute-start | bytes 645128 | tf_op jit(solution)/shard_map/ppermute | solution.py:102
  25.6 19.5 %collective-permute-start.18 = (bf16[112,960]{1,0:T(8,128)(2,1)S(1)}, bf16[112,960]{1,0:T(8,128)(2,1)S(1)}, u32[]{:S(2)}, u32[]{:S(2)}) collective-permute-start(bf16[112,960]{1,0:T(8,128)(2,1)S(1)} %fusion.62), channel_id=1, source_target_pairs={{0,3},{1,0},{2,1},{3,2},{4,7},{5,4},{6,5},{7,6},{8,11},{9,8},{10,9... | collective-permute-start | bytes 645128 | tf_op jit(solution)/shard_map/ppermute | solution.py:102
  29.6 20.1 %collective-permute-start.12 = (bf16[128,960]{0,1:T(8,128)(2,1)S(1)}, bf16[128,960]{0,1:T(8,128)(2,1)S(1)}, u32[]{:S(2)}, u32[]{:S(2)}) collective-permute-start(bf16[128,960]{0,1:T(8,128)(2,1)S(1)} %get-tuple-element.369), channel_id=1, source_target_pairs={{0,4},{4,12},{8,20},{12,28},{16,24},{20,16},{24,8},{28,0},{1,5},{5... | collective-permute-start | bytes 737288 | tf_op jit(solution)/shard_map/ppermute | solution.py:102
  29.6 20.0 %collective-permute-start.7 = (bf16[3,32,1664]{2,1,0:T(8,128)(2,1)S(1)}, bf16[3,32,1664]{2,1,0:T(8,128)(2,1)S(1)}, u32[]{:S(2)}, u32[]{:S(2)}) collective-permute-start(bf16[3,32,1664]{2,1,0:T(8,128)(2,1)S(1)} %pad_maximum_fusion.8.refs_1_), channel_id=1, source_target_pairs={{0,4},{4,0},{8,12},{12,8},{16,20},{20,16},{24,28},{28,24},{1,5},{5... | collective-permute-start | bytes 958472 | tf_op jit(solution)/shard_map/ppermute | solution.py:102
  49.6 19.0 %collective-permute-start.19 = (bf16[3,112,960]{2,1,0:T(8,128)(2,1)}, bf16[3,112,960]{2,1,0:T(8,128)(2,1)}, u32[]{:S(2)}, u32[]{:S(2)}) collective-permute-start(bf16[3,112,960]{2,1,0:T(8,128)(2,1)} %pad_maximum_fusion.6.refs_2_), channel_id=1, source_target_pairs={{0,8},{4,12},{8,0},{12,4},{16,24},{20,28},{24,16},{28,20},{1,9},{5... | collective-permute-start | bytes 1935368 | tf_op jit(solution)/shard_map/ppermute | solution.py:102
  49.7 24.6 %collective-permute-start.20 = (bf16[3,112,960]{2,1,0:T(8,128)(2,1)}, bf16[3,112,960]{2,1,0:T(8,128)(2,1)}, u32[]{:S(2)}, u32[]{:S(2)}) collective-permute-start(bf16[3,112,960]{2,1,0:T(8,128)(2,1)} %pad_maximum_fusion.6.refs_2_), channel_id=1, source_target_pairs={{0,16},{4,20},{8,24},{12,28},{16,0},{20,4},{24,8},{28,12},{1,17},{... | collective-permute-start | bytes 1935368 | tf_op jit(solution)/shard_map/ppermute | solution.py:102
  50.2 17.9 %collective-permute-start.26 = (bf16[32,5120]{1,0:T(8,128)(2,1)}, bf16[32,5120]{1,0:T(8,128)(2,1)S(1)}, u32[]{:S(2)}, u32[]{:S(2)}) collective-permute-start(bf16[32,5120]{1,0:T(8,128)(2,1)} %pad_dynamic-slice_fusion), channel_id=1, source_target_pairs={{0,1},{1,2},{2,3},{3,0},{4,5},{5,6},{6,7},{7,4},{8,9},{9,10},{10,1... | collective-permute-start | bytes 983048 | tf_op jit(solution)/shard_map/ppermute | solution.py:102
  62.9 20.2 %collective-permute-start.31 = (bf16[3,32,1664]{2,1,0:T(8,128)(2,1)S(1)}, bf16[3,32,1664]{2,1,0:T(8,128)(2,1)S(1)}, u32[]{:S(2)}, u32[]{:S(2)}) collective-permute-start(bf16[3,32,1664]{2,1,0:T(8,128)(2,1)S(1)} %collective-permute-done.8.refs_3_), channel_id=1, source_target_pairs={{0,4},{4,0},{8,12},{12,8},{16,20},{20,16},{24,28},{28,24},{1,5},{5... | collective-permute-start | bytes 958472 | tf_op jit(solution)/shard_map/ppermute | solution.py:102
  63.0 20.2 %collective-permute-start.32 = (bf16[3,32,1664]{2,1,0:T(8,128)(2,1)S(1)}, bf16[3,32,1664]{2,1,0:T(8,128)(2,1)S(1)}, u32[]{:S(2)}, u32[]{:S(2)}) collective-permute-start(bf16[3,32,1664]{2,1,0:T(8,128)(2,1)S(1)} %collective-permute-done.9.refs_4_), channel_id=1, source_target_pairs={{0,4},{4,0},{8,12},{12,8},{16,20},{20,16},{24,28},{28,24},{1,5},{5... | collective-permute-start | bytes 958472 | tf_op jit(solution)/shard_map/ppermute | solution.py:102
  68.7 20.2 %collective-permute-start.27 = (bf16[32,5120]{1,0:T(8,128)(2,1)}, bf16[32,5120]{1,0:T(8,128)(2,1)S(1)}, u32[]{:S(2)}, u32[]{:S(2)}) collective-permute-start(bf16[32,5120]{1,0:T(8,128)(2,1)} %pad_dynamic-slice_fusion), channel_id=1, source_target_pairs={{0,2},{1,3},{2,0},{3,1},{4,6},{5,7},{6,4},{7,5},{8,10},{9,11},{10,... | collective-permute-start | bytes 983048 | tf_op jit(solution)/shard_map/ppermute | solution.py:102
  83.1 20.4 %collective-permute-start.23 = (bf16[3,112,960]{2,1,0:T(8,128)(2,1)}, bf16[3,112,960]{2,1,0:T(8,128)(2,1)}, u32[]{:S(2)}, u32[]{:S(2)}) collective-permute-start(bf16[3,112,960]{2,1,0:T(8,128)(2,1)} %pad_maximum_fusion.6.refs_2_), channel_id=1, source_target_pairs={{0,4},{4,0},{8,12},{12,8},{16,20},{20,16},{24,28},{28,24},{1,5},{5... | collective-permute-start | bytes 1935368 | tf_op jit(solution)/shard_map/ppermute | solution.py:102
  83.2 20.6 %collective-permute-start.24 = (bf16[3,112,960]{2,1,0:T(8,128)(2,1)}, bf16[3,112,960]{2,1,0:T(8,128)(2,1)}, u32[]{:S(2)}, u32[]{:S(2)}) collective-permute-start(bf16[3,112,960]{2,1,0:T(8,128)(2,1)} %collective-permute-done.19.refs_3_), channel_id=1, source_target_pairs={{0,4},{4,0},{8,12},{12,8},{16,20},{20,16},{24,28},{28,24},{1,5},{5... | collective-permute-start | bytes 1935368 | tf_op jit(solution)/shard_map/ppermute | solution.py:102
  83.7 21.3 %collective-permute-start.25 = (bf16[3,112,960]{2,1,0:T(8,128)(2,1)}, bf16[3,112,960]{2,1,0:T(8,128)(2,1)}, u32[]{:S(2)}, u32[]{:S(2)}) collective-permute-start(bf16[3,112,960]{2,1,0:T(8,128)(2,1)} %collective-permute-done.20.refs_4_), channel_id=1, source_target_pairs={{0,4},{4,0},{8,12},{12,8},{16,20},{20,16},{24,28},{28,24},{1,5},{5... | collective-permute-start | bytes 1935368 | tf_op jit(solution)/shard_map/ppermute | solution.py:102
  103.5 17.9 %collective-permute-start.36 = (bf16[256,640]{1,0:T(8,128)(2,1)}, bf16[256,640]{1,0:T(8,128)(2,1)S(1)}, u32[]{:S(2)}, u32[]{:S(2)}) collective-permute-start(bf16[256,640]{1,0:T(8,128)(2,1)} %get-tuple-element.419.refs_0_.refs_7_), channel_id=1, source_target_pairs={{0,16},{4,20},{8,24},{12,28},{16,0},{20,4},{24,8},{28,12},{1,17},{... | collective-permute-start | bytes 983048 | tf_op jit(solution)/shard_map/ppermute | solution.py:102
  105.1 58.2 %collective-permute-start.29 = (bf16[3,32,5120]{2,1,0:T(8,128)(2,1)S(1)}, bf16[3,32,5120]{2,1,0:T(8,128)(2,1)}, u32[]{:S(2)}, u32[]{:S(2)}) collective-permute-start(bf16[3,32,5120]{2,1,0:T(8,128)(2,1)S(1)} %pad_maximum_fusion.3.refs_1_), channel_id=1, source_target_pairs={{0,8},{4,12},{8,0},{12,4},{16,24},{20,28},{24,16},{28,20},{1,9},{5... | collective-permute-start | bytes 2949128 | tf_op jit(solution)/shard_map/ppermute | solution.py:102
  107.9 55.4 %collective-permute-start.30 = (bf16[3,32,5120]{2,1,0:T(8,128)(2,1)S(1)}, bf16[3,32,5120]{2,1,0:T(8,128)(2,1)}, u32[]{:S(2)}, u32[]{:S(2)}) collective-permute-start(bf16[3,32,5120]{2,1,0:T(8,128)(2,1)S(1)} %pad_maximum_fusion.3.refs_1_), channel_id=1, source_target_pairs={{0,16},{4,20},{8,24},{12,28},{16,0},{20,4},{24,8},{28,12},{1,17},{... | collective-permute-start | bytes 2949128 | tf_op jit(solution)/shard_map/ppermute | solution.py:102
  521.8 21.4 %collective-permute-start.80 = (bf16[4,4,32,5120]{3,2,1,0:T(8,128)(2,1)}, bf16[4,4,32,5120]{3,2,1,0:T(8,128)(2,1)}, u32[]{:S(2)}, u32[]{:S(2)}) collective-permute-start(bf16[4,4,32,5120]{3,2,1,0:T(8,128)(2,1)} %get-tuple-element.573), channel_id=1, source_target_pairs={{0,4},{4,0},{8,12},{12,8},{16,20},{20,16},{24,28},{28,24},{1,5},{5... | collective-permute-start | bytes 15728648 | tf_op jit(solution)/shard_map/ppermute | solution.py:102
  549.3 35.1 %collective-permute-start.83 = (bf16[4,4,112,960]{3,2,1,0:T(8,128)(2,1)}, bf16[4,4,112,960]{3,2,1,0:T(8,128)(2,1)}, u32[]{:S(2)}, u32[]{:S(2)}) collective-permute-start(bf16[4,4,112,960]{3,2,1,0:T(8,128)(2,1)} %get-tuple-element.582), channel_id=1, source_target_pairs={{0,4},{4,0},{8,12},{12,8},{16,20},{20,16},{24,28},{28,24},{1,5},{5... | collective-permute-start | bytes 10321928 | tf_op jit(solution)/shard_map/ppermute | solution.py:102
  549.3 35.0 %collective-permute-start.81 = (bf16[2,2,32,5120]{3,2,1,0:T(8,128)(2,1)}, bf16[2,2,32,5120]{3,2,1,0:T(8,128)(2,1)}, u32[]{:S(2)}, u32[]{:S(2)}) collective-permute-start(bf16[2,2,32,5120]{3,2,1,0:T(8,128)(2,1)} %pad_maximum_fusion), channel_id=1, source_target_pairs={{0,8},{4,12},{8,0},{12,4},{16,24},{20,28},{24,16},{28,20},{1,9},{5... | collective-permute-start | bytes 3932168 | tf_op jit(solution)/shard_map/ppermute | solution.py:102
  550.3 34.1 %collective-permute-start.82 = (bf16[2,2,32,5120]{3,2,1,0:T(8,128)(2,1)}, bf16[2,2,32,5120]{3,2,1,0:T(8,128)(2,1)}, u32[]{:S(2)}, u32[]{:S(2)}) collective-permute-start(bf16[2,2,32,5120]{3,2,1,0:T(8,128)(2,1)} %pad_maximum_fusion.1), channel_id=1, source_target_pairs={{0,16},{4,20},{8,24},{12,28},{16,0},{20,4},{24,8},{28,12},{1,17},{... | collective-permute-start | bytes 3932168 | tf_op jit(solution)/shard_map/ppermute | solution.py:102
  584.4 21.6 %collective-permute-start.86 = (bf16[4,4,32,1664]{3,2,1,0:T(8,128)(2,1)}, bf16[4,4,32,1664]{3,2,1,0:T(8,128)(2,1)}, u32[]{:S(2)}, u32[]{:S(2)}) collective-permute-start(bf16[4,4,32,1664]{3,2,1,0:T(8,128)(2,1)} %get-tuple-element.608), channel_id=1, source_target_pairs={{0,4},{4,0},{8,12},{12,8},{16,20},{20,16},{24,28},{28,24},{1,5},{5... | collective-permute-start | bytes 5111816 | tf_op jit(solution)/shard_map/ppermute | solution.py:102
  606.0 40.2 %collective-permute-start.87 = (bf16[2,2,112,960]{3,2,1,0:T(8,128)(2,1)}, bf16[2,2,112,960]{3,2,1,0:T(8,128)(2,1)}, u32[]{:S(2)}, u32[]{:S(2)}) collective-permute-start(bf16[2,2,112,960]{3,2,1,0:T(8,128)(2,1)} %pad_maximum_fusion.4), channel_id=1, source_target_pairs={{0,8},{4,12},{8,0},{12,4},{16,24},{20,28},{24,16},{28,20},{1,9},{5... | collective-permute-start | bytes 2580488 | tf_op jit(solution)/shard_map/ppermute | solution.py:102
  607.1 39.1 %collective-permute-start.88 = (bf16[2,2,112,960]{3,2,1,0:T(8,128)(2,1)}, bf16[2,2,112,960]{3,2,1,0:T(8,128)(2,1)}, u32[]{:S(2)}, u32[]{:S(2)}) collective-permute-start(bf16[2,2,112,960]{3,2,1,0:T(8,128)(2,1)} %pad_maximum_fusion.5), channel_id=1, source_target_pairs={{0,16},{4,20},{8,24},{12,28},{16,0},{20,4},{24,8},{28,12},{1,17},{... | collective-permute-start | bytes 2580488 | tf_op jit(solution)/shard_map/ppermute | solution.py:102
  616.4 23.6 %collective-permute-start.107 = (bf16[32,5120]{1,0:T(8,128)(2,1)S(1)}, bf16[32,5120]{1,0:T(8,128)(2,1)S(1)}, u32[]{:S(2)}, u32[]{:S(2)}) collective-permute-start(bf16[32,5120]{1,0:T(8,128)(2,1)S(1)} %get-tuple-element.645), channel_id=1, source_target_pairs={{0,2},{1,3},{2,0},{3,1},{4,6},{5,7},{6,4},{7,5},{8,10},{9,11},{10,... | collective-permute-start | bytes 983048 | tf_op jit(solution)/shard_map/ppermute | solution.py:102
  620.0 22.2 %collective-permute-start.108 = (bf16[32,5120]{1,0:T(8,128)(2,1)S(1)}, bf16[32,5120]{1,0:T(8,128)(2,1)}, u32[]{:S(2)}, u32[]{:S(2)}) collective-permute-start(bf16[32,5120]{1,0:T(8,128)(2,1)S(1)} %get-tuple-element.646), channel_id=1, source_target_pairs={{0,3},{1,0},{2,1},{3,2},{4,7},{5,4},{6,5},{7,6},{8,11},{9,8},{10,9... | collective-permute-start | bytes 983048 | tf_op jit(solution)/shard_map/ppermute | solution.py:102
  655.9 18.8 %collective-permute-start.109 = (bf16[32,5120]{1,0:T(8,128)(2,1)S(1)}, bf16[32,5120]{1,0:T(8,128)(2,1)S(1)}, u32[]{:S(2)}, u32[]{:S(2)}) collective-permute-start(bf16[32,5120]{1,0:T(8,128)(2,1)S(1)} %fusion.10.refs_0_), channel_id=1, source_target_pairs={{0,4},{4,0},{8,12},{12,8},{16,20},{20,16},{24,28},{28,24},{1,5},{5... | collective-permute-start | bytes 983048 | tf_op jit(solution)/shard_map/ppermute | solution.py:102
  656.0 19.4 %collective-permute-start.110 = (bf16[32,5120]{1,0:T(8,128)(2,1)S(1)}, bf16[32,5120]{1,0:T(8,128)(2,1)S(1)}, u32[]{:S(2)}, u32[]{:S(2)}) collective-permute-start(bf16[32,5120]{1,0:T(8,128)(2,1)S(1)} %fusion.10.refs_0_), channel_id=1, source_target_pairs={{0,8},{4,12},{8,0},{12,4},{16,24},{20,28},{24,16},{28,20},{1,9},{5... | collective-permute-start | bytes 983048 | tf_op jit(solution)/shard_map/ppermute | solution.py:102
  656.0 19.3 %collective-permute-start.111 = (bf16[32,5120]{1,0:T(8,128)(2,1)S(1)}, bf16[32,5120]{1,0:T(8,128)(2,1)S(1)}, u32[]{:S(2)}, u32[]{:S(2)}) collective-permute-start(bf16[32,5120]{1,0:T(8,128)(2,1)S(1)} %fusion.10.refs_0_), channel_id=1, source_target_pairs={{0,16},{4,20},{8,24},{12,28},{16,0},{20,4},{24,8},{28,12},{1,17},{... | collective-permute-start | bytes 983048 | tf_op jit(solution)/shard_map/ppermute | solution.py:102
  674.7 21.3 %collective-permute-start.93 = (bf16[4,32,1664]{2,1,0:T(8,128)(2,1)S(1)}, bf16[4,32,1664]{2,1,0:T(8,128)(2,1)S(1)}, u32[]{:S(2)}, u32[]{:S(2)}) collective-permute-start(bf16[4,32,1664]{2,1,0:T(8,128)(2,1)S(1)} %get-tuple-element.623), channel_id=1, source_target_pairs={{0,8},{4,12},{8,0},{12,4},{16,24},{20,28},{24,16},{28,20},{1,9},{5... | collective-permute-start | bytes 1277960 | tf_op jit(solution)/shard_map/ppermute | solution.py:102
  675.4 21.1 %collective-permute-start.94 = (bf16[4,32,1664]{2,1,0:T(8,128)(2,1)S(1)}, bf16[4,32,1664]{2,1,0:T(8,128)(2,1)S(1)}, u32[]{:S(2)}, u32[]{:S(2)}) collective-permute-start(bf16[4,32,1664]{2,1,0:T(8,128)(2,1)S(1)} %get-tuple-element.624), channel_id=1, source_target_pairs={{0,16},{4,20},{8,24},{12,28},{16,0},{20,4},{24,8},{28,12},{1,17},{... | collective-permute-start | bytes 1277960 | tf_op jit(solution)/shard_map/ppermute | solution.py:102
  675.4 21.1 %collective-permute-start.95 = (bf16[4,32,1664]{2,1,0:T(8,128)(2,1)S(1)}, bf16[4,32,1664]{2,1,0:T(8,128)(2,1)S(1)}, u32[]{:S(2)}, u32[]{:S(2)}) collective-permute-start(bf16[4,32,1664]{2,1,0:T(8,128)(2,1)S(1)} %get-tuple-element.625), channel_id=1, source_target_pairs={{0,24},{4,28},{8,16},{12,20},{16,8},{20,12},{24,0},{28,4},{1,25},{... | collective-permute-start | bytes 1277960 | tf_op jit(solution)/shard_map/ppermute | solution.py:102
  (322 other events, 3045.0 us)
